TPU v7x, 32 devices: a whole 2x2x4 slice. The times are simulated.
32 devices in a mesh: dp: 4 (over z), seq: 2 (over core), head: 4 (over y, x).
Axes of the slice: x: 2, y: 2, z: 4, core: 2. Of those that a mesh axis runs over, the one named last changes fastest.
Arguments:
- tokens: bfloat16 [2, 8192, 768], P(None, ('dp', 'seq', 'head')), may hold values from -6 to 6
- lengths: int32 [2, 4, 4], P(None, 'dp'), may hold values from 64 to 1792, as said below
- ln_gain: float32 [768], replicated, may hold values from 0.5 to 1.5
- w_up: bfloat16 [768, 3072], replicated, may hold values from -0.21875 to 0.21875
- conv_w: float32 [4, 1536], replicated, may hold values from -3 to 3
- conv_b: float32 [1536], replicated, may hold values from -3 to 3
- w_q: bfloat16 [384, 4, 4], replicated, may hold values from -3 to 3
- w_k: bfloat16 [384, 4, 4], replicated, may hold values from -3 to 3
- w_v: bfloat16 [384, 4, 4], replicated, may hold values from -3 to 3
- gate_w: bfloat16 [4608, 8], replicated, may hold values from -0.09375 to 0.09375
- i_bias: float32 [4], replicated, may hold values from -9 to -6
- f_bias: float32 [4], replicated, may hold values from 2.5 to 9
- gn_gain: float32 [1536], replicated, may hold values from 0.5 to 1.5
- skip: float32 [1536], replicated, may hold values from 0.1 to 1.9
- w_down: bfloat16 [1536, 768], replicated, may hold values from -0.3125 to 0.3125
- cotangent: bfloat16 [2, 8192, 768], P(None, ('dp', 'seq', 'head')), may hold values from -6 to 6
Outputs:
- block_out: bfloat16 [2, 8192, 768], P(None, ('dp', 'seq', 'head'))
- d_tokens: bfloat16 [2, 8192, 768], P(None, ('dp', 'seq', 'head'))
- g_ln_gain: float32 [768], replicated
- g_w_up: float32 [768, 3072], P(None, ('dp', 'seq', 'head'))
- g_conv_w: float32 [4, 1536], replicated
- g_conv_b: float32 [1536], replicated
- g_w_q: float32 [384, 4, 4], replicated
- g_w_k: float32 [384, 4, 4], replicated
- g_w_v: float32 [384, 4, 4], replicated
- g_gate_w: float32 [4608, 8], replicated
- g_i_bias: float32 [4], replicated
- g_f_bias: float32 [4], replicated
- g_gn_gain: float32 [1536], replicated
- g_skip: float32 [1536], replicated
- g_w_down: float32 [1536, 768], P(('dp', 'seq', 'head'))
Inputs may be any that keep to these rules, and one draw needn't show every extreme that they name: lengths[m, g] are the lengths of the 4 sequences packed in this order from the start of stream g of micro-batch m; they sum to at most 2048, and the stream's remaining tokens are padding.
All inputs are finite; a program needn't handle non-finite values.
Results may differ from a plain program's by a relative error of at most 0.005.
The roundings to bfloat16 on the way count: a program that leaves them out, or rounds other values in their place, can miss the bound.
Values may be sent and summed in bfloat16 or wider, within the bound.
No kernel may reach another device: no remote copies, remote signals or barrier semaphores. Data moves between devices by JAX's collectives and lax.ppermute only.
A program may use at most 256 MiB of HBM per device.

v0:
```python
from functools import partial

import jax
import jax.numpy as jnp
from jax import lax
from jax.sharding import PartitionSpec as P

EPS = 1e-05
HIGH = lax.Precision.HIGHEST


def shifted(value, axis, steps):
    count = lax.axis_size(axis)
    leading, last = (max(0, -steps), min(count, count - steps))
    return lax.ppermute(value, axis, [(source, source + steps) for source in range(leading, last)])


def carried_in(value, axis, combine, identity, reverse):
    count, mine = (lax.axis_size(axis), lax.axis_index(axis))
    everything = jax.tree.map(lambda part: lax.all_gather(part, axis), value)
    start = jax.tree.map(
        lambda part, zero: jnp.broadcast_to(jnp.asarray(zero, part.dtype), part.shape),
        value,
        identity,
    )

    def step(k, before):
        at = count - 1 - k if reverse else k
        reached = at > mine if reverse else at < mine
        new = combine(before, jax.tree.map(lambda part: part[at], everything))
        return jax.tree.map(lambda a, b: jnp.where(reached, a, b), new, before)

    return lax.fori_loop(0, count, step, start)


def rounded(v):
    shorter = lax.optimization_barrier(v.astype(jnp.bfloat16)).astype(jnp.float32)
    return v + lax.stop_gradient(shorter - v)


def seg_ids(ends_at, start_at, how_many):
    positions = start_at + jnp.arange(how_many, dtype=jnp.int32)
    labels = jnp.sum((positions[:, None] >= ends_at[None, :]).astype(jnp.int32), axis=1)
    return jnp.where(positions >= 0, labels, -1)


def norm_rows(stream, ln_gain):
    average = jnp.mean(stream, axis=-1, keepdims=True)
    centred = stream - average
    variance = jnp.mean(centred * centred, axis=-1, keepdims=True)
    return rounded(centred * lax.rsqrt(variance + EPS) * ln_gain)


def block_mix(values_in, weight):
    blocks, size_in, size_out = weight.shape
    grouped = values_in.reshape(values_in.shape[0], blocks, size_in)
    mapped = jnp.einsum("tbi,bio->tbo", grouped, weight, precision=HIGH)
    return mapped.reshape(values_in.shape[0], blocks * size_out)


def conv_part(extended, conv_w, conv_b, seg_ext):
    kernel = conv_w.shape[0]
    lead_rows = kernel - 1
    own_rows = extended.shape[0] - lead_rows
    seg_own = seg_ext[lead_rows:]
    conv_sum = jnp.zeros((own_rows, extended.shape[1]), jnp.float32) + conv_b
    for lagged in range(kernel):
        offset = lead_rows - lagged
        same_seq = (seg_ext[offset : offset + own_rows] == seg_own).astype(jnp.float32)
        conv_sum = (
            conv_sum
            + conv_w[lead_rows - lagged] * extended[offset : offset + own_rows] * same_seq[:, None]
        )
    return rounded(jax.nn.silu(conv_sum))


def front(extended, conv_w, conv_b, w_q, w_k, w_v, gate_w, i_bias, f_bias, seg_ext):
    lead_rows = conv_w.shape[0] - 1
    conv_act = conv_part(extended, conv_w, conv_b, seg_ext)
    inner_rows = extended[lead_rows:]
    queries = rounded(block_mix(conv_act, w_q))
    key_rows = rounded(block_mix(conv_act, w_k))
    values = rounded(block_mix(inner_rows, w_v))
    joined = jnp.concatenate([queries, key_rows, values], axis=1)
    gate_lin = rounded(jnp.dot(joined, gate_w, precision=HIGH))
    return (conv_act, queries, key_rows, values, gate_lin)


def gate_terms(gate_pre, valid_rows):
    log_keep = valid_rows[:, None] * jax.nn.log_sigmoid(gate_pre[:, :, 1])
    weight = valid_rows[:, None] * jnp.exp(gate_pre[:, :, 0])
    return (jnp.cumsum(log_keep, axis=0), weight)


def mix_out(queries, key_rows, values, gate_pre, state_in, seg_span, valid_rows, prev_seg):
    length = seg_span.shape[0]
    factor = queries.shape[2] ** (-0.5)
    cumulative, weight = gate_terms(gate_pre, valid_rows)
    order_idx = jnp.arange(length)
    allowed = (seg_span[:, None] == seg_span[None, :]) & (order_idx[None, :] <= order_idx[:, None])
    differ = cumulative.T[:, :, None] - cumulative.T[:, None, :]
    decays = jnp.where(allowed[None], jnp.exp(jnp.minimum(differ, 0.0)) * weight.T[:, None, :], 0.0)
    scores = jnp.einsum("thd,shd->hts", queries, key_rows, precision=HIGH) * factor
    hidden = jnp.einsum("hts,shd->thd", scores * decays, values, precision=HIGH)
    carried = jnp.where((seg_span == prev_seg)[:, None], jnp.exp(cumulative), 0.0)
    hidden = hidden + carried[:, :, None] * jnp.einsum(
        "thd,hde->the", queries, state_in, precision=HIGH
    )
    average = jnp.mean(hidden, axis=-1, keepdims=True)
    centred = hidden - average
    variance = jnp.mean(centred * centred, axis=-1, keepdims=True)
    return rounded(centred * lax.rsqrt(variance + EPS))


def mix_summary(key_rows, values, gate_pre, seg_span, valid_rows, prev_seg):
    factor = key_rows.shape[2] ** (-0.5)
    cumulative, weight = gate_terms(gate_pre, valid_rows)
    last_cum = cumulative[-1]
    same_last = (seg_span == seg_span[-1])[:, None]
    tail_weight = (
        jnp.where(same_last, jnp.exp(jnp.minimum(last_cum[None, :] - cumulative, 0.0)), 0.0)
        * weight
        * factor
    )
    summary = jnp.einsum("shd,she->hde", key_rows * tail_weight[:, :, None], values, precision=HIGH)
    carry_on = jnp.where(seg_span[-1] == prev_seg, jnp.exp(last_cum), 0.0)
    return (carry_on, summary)


def chain_forward(earlier, later):
    return (earlier[0] * later[0], later[0][..., None, None] * earlier[1] + later[1])


def chain_backward(earlier, later):
    return (earlier[0] * later[0], later[1] + later[0][..., None, None] * earlier[1])


def branch_of(normed_h, conv_act, gate_z, gn_gain, skip):
    return rounded((normed_h * gn_gain + skip * conv_act) * jax.nn.silu(gate_z))


def per_device(
    tokens,
    lengths,
    ln_gain,
    w_up,
    conv_w,
    conv_b,
    w_q,
    w_k,
    w_v,
    gate_w,
    i_bias,
    f_bias,
    gn_gain,
    skip,
    w_down,
    cotangent,
):
    micro_count, tok_rows, model_width = tokens.shape
    inner_width = w_down.shape[0]
    head_count = i_bias.shape[0]
    head_width = inner_width // head_count
    lead_rows = conv_w.shape[0] - 1
    seq_count = lengths.shape[2]
    head_devices = lax.axis_size("head")
    stream_first = lax.axis_index(("seq", "head")) * tok_rows
    span_rows = tok_rows * head_devices
    span_first = lax.axis_index("seq") * span_rows
    head_place = lax.axis_index("head")
    bias_table = jnp.stack([i_bias, f_bias], axis=-1)
    bias_head = lax.dynamic_index_in_dim(bias_table, head_place, 0, keepdims=False)
    front_params = (
        conv_w,
        conv_b,
        w_q.astype(jnp.float32),
        w_k.astype(jnp.float32),
        w_v.astype(jnp.float32),
        gate_w.astype(jnp.float32),
        i_bias,
        f_bias,
    )
    by_rows = (((0,), (0,)), ((), ()))
    by_cols = (((1,), (1,)), ((), ()))
    small_total = (
        [jnp.zeros_like(ln_gain)]
        + [jnp.zeros_like(member) for member in front_params]
        + [jnp.zeros_like(gn_gain), jnp.zeros_like(skip)]
    )
    up_total = jnp.zeros((model_width, 2 * inner_width), jnp.float32)
    down_total = jnp.zeros((inner_width, model_width), jnp.float32)
    results = []
    grad_rows = []
    for micro_step in range(micro_count):
        stream = tokens[micro_step].astype(jnp.float32)
        ends_at = jnp.cumsum(lengths[micro_step, 0])
        seg_own = seg_ids(ends_at, stream_first, tok_rows)
        seg_ext = seg_ids(ends_at, stream_first - lead_rows, tok_rows + lead_rows)
        valid_rows = (seg_own < seq_count).astype(jnp.float32)
        normed, pull_norm = jax.vjp(norm_rows, stream, ln_gain)
        normed_b = normed.astype(jnp.bfloat16)
        up_proj = jnp.dot(normed_b, w_up, preferred_element_type=jnp.float32)
        inner_b = up_proj[:, :inner_width].astype(jnp.bfloat16)
        gate_z = up_proj[:, inner_width:]
        halo_rows = shifted(inner_b[tok_rows - lead_rows :], ("seq", "head"), 1)
        extended_b = jnp.concatenate([halo_rows, inner_b], axis=0)
        extended = extended_b.astype(jnp.float32)
        front_out, pull_front = jax.vjp(partial(front, seg_ext=seg_ext), extended, *front_params)
        conv_act, queries, key_rows, values, gate_lin = front_out
        gate_b = gate_lin.astype(jnp.bfloat16).reshape(tok_rows, head_count, 2)
        query_b = queries.astype(jnp.bfloat16).reshape(tok_rows, head_count, head_width)
        key_b = key_rows.astype(jnp.bfloat16).reshape(tok_rows, head_count, head_width)
        value_b = values.astype(jnp.bfloat16).reshape(tok_rows, head_count, head_width)
        moved = (
            lax.all_to_all(query_b, "head", split_axis=1, concat_axis=0, tiled=True),
            lax.all_to_all(key_b, "head", split_axis=1, concat_axis=0, tiled=True),
            lax.all_to_all(value_b, "head", split_axis=1, concat_axis=0, tiled=True),
            lax.all_to_all(gate_b, "head", split_axis=1, concat_axis=0, tiled=True),
        )
        span_query, span_key, span_value, span_gate = [
            member.astype(jnp.float32) for member in moved
        ]
        span_gate = span_gate + bias_head[None, None, :]
        seg_span = seg_ids(ends_at, span_first, span_rows)
        prev_seg = seg_ids(ends_at, span_first - 1, 1)[0]
        valid_span = (seg_span < seq_count).astype(jnp.float32)
        summary_fn = partial(
            mix_summary, seg_span=seg_span, valid_rows=valid_span, prev_seg=prev_seg
        )
        (carry_on, summary), pull_summary = jax.vjp(summary_fn, span_key, span_value, span_gate)
        incoming = carried_in(
            (carry_on, summary),
            "seq",
            chain_forward,
            (jnp.ones_like(carry_on), jnp.zeros_like(summary)),
            False,
        )
        state_in = incoming[1]
        mix_fn = partial(mix_out, seg_span=seg_span, valid_rows=valid_span, prev_seg=prev_seg)
        normed_span, pull_mix = jax.vjp(
            mix_fn, span_query, span_key, span_value, span_gate, state_in
        )
        normed_sent = normed_span.astype(jnp.bfloat16)
        normed_back = lax.all_to_all(normed_sent, "head", split_axis=0, concat_axis=1, tiled=True)
        normed_h = normed_back.reshape(tok_rows, inner_width).astype(jnp.float32)
        branch, pull_branch = jax.vjp(branch_of, normed_h, conv_act, gate_z, gn_gain, skip)
        branch_b = branch.astype(jnp.bfloat16)
        mixed = jnp.dot(branch_b, w_down, preferred_element_type=jnp.float32)
        results.append((stream + valid_rows[:, None] * mixed).astype(jnp.bfloat16))
        cot_rows = cotangent[micro_step]
        cot_mix = cot_rows * valid_rows.astype(jnp.bfloat16)[:, None]
        down_step = lax.dot_general(branch_b, cot_mix, by_rows, preferred_element_type=jnp.float32)
        d_branch = lax.dot_general(cot_mix, w_down, by_cols, preferred_element_type=jnp.float32)
        d_normed, d_conv_act, d_gate_z, d_gn_gain, d_skip = pull_branch(d_branch)
        d_sent = d_normed.astype(jnp.bfloat16).reshape(tok_rows, head_count, head_width)
        d_span = lax.all_to_all(d_sent, "head", split_axis=1, concat_axis=0, tiled=True)
        d_query, d_key_mix, d_value_mix, d_gate_mix, d_state_in = pull_mix(
            d_span.astype(jnp.float32)
        )
        after = carried_in(
            (carry_on, d_state_in),
            "seq",
            chain_backward,
            (jnp.ones_like(carry_on), jnp.zeros_like(d_state_in)),
            True,
        )
        d_state_out = after[1]
        d_carry = jnp.sum(d_state_out * state_in, axis=(1, 2))
        d_key_sum, d_value_sum, d_gate_sum = pull_summary((d_carry, d_state_out))
        d_key_span = d_key_mix + d_key_sum
        d_value_span = d_value_mix + d_value_sum
        d_gate_span = d_gate_mix + d_gate_sum
        bias_grad = jnp.sum(d_gate_span, axis=(0, 1))
        grads_back = (
            lax.all_to_all(d_query, "head", split_axis=0, concat_axis=1, tiled=True),
            lax.all_to_all(d_key_span, "head", split_axis=0, concat_axis=1, tiled=True),
            lax.all_to_all(d_value_span, "head", split_axis=0, concat_axis=1, tiled=True),
            lax.all_to_all(d_gate_span, "head", split_axis=0, concat_axis=1, tiled=True),
        )
        front_grads = pull_front(
            (
                d_conv_act,
                grads_back[0].reshape(tok_rows, inner_width),
                grads_back[1].reshape(tok_rows, inner_width),
                grads_back[2].reshape(tok_rows, inner_width),
                grads_back[3].reshape(tok_rows, 2 * head_count),
            )
        )
        d_extended = front_grads[0]
        front_list = list(front_grads[1:])
        front_list[6] = front_list[6] + lax.dynamic_update_slice_in_dim(
            jnp.zeros_like(i_bias), bias_grad[0:1], head_place, 0
        )
        front_list[7] = front_list[7] + lax.dynamic_update_slice_in_dim(
            jnp.zeros_like(f_bias), bias_grad[1:2], head_place, 0
        )
        d_halo = shifted(d_extended[:lead_rows], ("seq", "head"), -1)
        d_inner = d_extended[lead_rows:] + jnp.pad(d_halo, ((tok_rows - lead_rows, 0), (0, 0)))
        d_up_b = jnp.concatenate([d_inner, d_gate_z], axis=1).astype(jnp.bfloat16)
        up_step = lax.dot_general(normed_b, d_up_b, by_rows, preferred_element_type=jnp.float32)
        d_normed_in = lax.dot_general(d_up_b, w_up, by_cols, preferred_element_type=jnp.float32)
        d_stream, d_ln_gain = pull_norm(d_normed_in)
        grad_rows.append((cot_rows.astype(jnp.float32) + d_stream).astype(jnp.bfloat16))
        step_small = [d_ln_gain] + front_list + [d_gn_gain, d_skip]
        small_total = [held + fresh for held, fresh in zip(small_total, step_small)]
        up_total = up_total + up_step
        down_total = down_total + down_step
    up_share, down_share = (
        lax.psum_scatter(up_total, ("dp", "seq", "head"), scatter_dimension=1, tiled=True),
        lax.psum_scatter(down_total, ("dp", "seq", "head"), scatter_dimension=0, tiled=True),
    )
    summed = lax.psum(
        (
            small_total[0],
            small_total[1],
            small_total[2],
            small_total[3],
            small_total[4],
            small_total[5],
            small_total[6],
            small_total[7],
            small_total[8],
            small_total[9],
            small_total[10],
        ),
        ("dp", "seq", "head"),
    )
    return (
        jnp.stack(results),
        jnp.stack(grad_rows),
        summed[0],
        up_share,
        summed[1],
        summed[2],
        summed[3],
        summed[4],
        summed[5],
        summed[6],
        summed[7],
        summed[8],
        summed[9],
        summed[10],
        down_share,
    )


def solution(mesh):
    placed = (
        P(None, ("dp", "seq", "head"), None),
        P(None, "dp", None),
        P(),
        P(),
        P(),
        P(),
        P(),
        P(),
        P(),
        P(),
        P(),
        P(),
        P(),
        P(),
        P(),
        P(None, ("dp", "seq", "head"), None),
    )
    return jax.shard_map(
        per_device,
        mesh=mesh,
        in_specs=placed,
        out_specs=(
            P(None, ("dp", "seq", "head"), None),
            P(None, ("dp", "seq", "head"), None),
            P(),
            P(None, ("dp", "seq", "head")),
            P(),
            P(),
            P(),
            P(),
            P(),
            P(),
            P(),
            P(),
            P(),
            P(),
            P(("dp", "seq", "head"), None),
        ),
        check_vma=False,
    )
```

profile of v0, /device:TPU:0, one launch (start us, length us, event | category | flops | bytes accessed | tf_op | source)
XLA Modules:
  0.0 1402.9 jit_solution(12322774250816711972)
XLA Ops:
  150.3 10.0 all-to-all-done.15
  183.1 6.5 all-to-all-done.10
  196.4 7.7 all-to-all-done
  303.6 7.9 while.61
  315.1 8.0 fusion.316
  334.8 10.8 fusion.231
  345.6 8.1 while.60
  357.4 8.0 fusion.317
  369.8 10.9 fusion.233
  401.7 7.2 add_bitcast_fusion
  447.4 7.1 while.63
  463.3 7.0 while.62
  534.0 6.7 fusion.91
  552.8 10.4 add_bitcast_fusion.1
  588.8 7.4 fusion.58
  601.2 6.7 fusion.95
  612.5 10.4 add_bitcast_fusion.3
  627.8 8.1 fusion.81
  783.2 10.6 multiply_reduce_fusion
  860.9 7.0 convolution_add_fusion.1
  891.9 113.9 %all-reduce.39.cloned.1.call-done = (f32[768]{0:T(1024)}, f32[4,1536]{1,0:T(4,128)}, f32[1536]{0:T(1024)}, f32[384,4,4]{2,1,0:T(4,128)}, f32[384,4,4]{2,1,0:T(4,...) async-done(((f32[768]{0:T(1024)}, f32[4,1536]{1,0:T(4,128)}, f32[1536]{0:T(1024)}, f32[384,4,4]{2,1,0:T(4,128)}, ...) | async-done | bytes 119856 | tf_op jit(solution)/shard_map/psum | solution.py:312
  1011.9 121.3 %all-reduce.37.cloned.1.call-done = f32[4608,8]{0,1:T(8,128)} async-done(((f32[4608,8]{0,1:T(8,128)}), f32[4608,8]{0,1:T(8,128)}) %all-reduce.37.cloned.1.call-update) | async-done | bytes 147472 | tf_op jit(solution)/shard_map/psum | solution.py:312
  1133.2 115.9 %reduce-scatter.5.cloned.1.call-done = f32[48,768]{1,0:T(8,128)} async-done(((f32[1536,768]{1,0:T(8,128)}), f32[48,768]{1,0:T(8,128)}) %reduce-scatter.5.cloned.1.call-update) | async-done | bytes 147472 | tf_op jit(solution)/shard_map/reduce_scatter | solution.py:310
  1249.1 141.0 %reduce-scatter.3.cloned.1.call-done = f32[768,96]{0,1:T(8,128)} async-done(((f32[768,3072]{0,1:T(8,128)}), f32[768,96]{0,1:T(8,128)}) %reduce-scatter.3.cloned.1.call-update) | async-done | bytes 294928 | tf_op jit(solution)/shard_map/reduce_scatter | solution.py:309
  (853 shorter events, 750.5 us)
Async XLA Ops:
  17.0 46.6 %collective-permute-start = (bf16[3,1536]{1,0:T(4,128)(2,1)S(1)}, bf16[3,1536]{1,0:T(4,128)(2,1)S(1)}, u32[]{:S(2)}, u32[]{:S(2)}) collective-permute-start(bf16[3,1536]{1,0:T(4,128)(2,1)S(1)} %slice.259), channel_id=1, source_target_pairs={{0,1},{1,2},{2,3},{3,4},{4,5},{5,6},{6,7},{8,9},{9,10},{10,11},{11... | collective-permute-start | bytes 27656 | tf_op jit(solution)/shard_map/ppermute | solution.py:15
  25.2 40.0 %collective-permute-start.1 = (bf16[3,1536]{1,0:T(4,128)(2,1)S(1)}, bf16[3,1536]{1,0:T(4,128)(2,1)S(1)}, u32[]{:S(2)}, u32[]{:S(2)}) collective-permute-start(bf16[3,1536]{1,0:T(4,128)(2,1)S(1)} %slice.269), channel_id=1, source_target_pairs={{0,1},{1,2},{2,3},{3,4},{4,5},{5,6},{6,7},{8,9},{9,10},{10,11},{11... | collective-permute-start | bytes 27656 | tf_op jit(solution)/shard_map/ppermute | solution.py:15
  218.7 17.6 %all-to-all-start.7 = ((bf16[256,4,384]{0,2,1:T(8,128)(2,1)}), bf16[256,4,384]{0,2,1:T(8,128)(2,1)}, u32[]{:S(2)}, u32[]{:S(2)}) async-start(bf16[256,4,384]{0,2,1:T(8,128)(2,1)} %bitcast.831), calls=%async_computation.7 | async-start | bytes 1572864 | tf_op jit(solution)/shard_map/all_to_all | solution.py:216
  236.3 21.3 %all-to-all-start.1 = ((bf16[256,4,384]{0,2,1:T(8,128)(2,1)}), bf16[256,4,384]{0,2,1:T(8,128)(2,1)}, u32[]{:S(2)}, u32[]{:S(2)}) async-start(bf16[256,4,384]{0,2,1:T(8,128)(2,1)} %bitcast.828), calls=%async_computation.1 | async-start | bytes 1572864 | tf_op jit(solution)/shard_map/all_to_all | solution.py:215
  257.5 24.8 %all-to-all-start.2 = ((bf16[256,4,384]{0,2,1:T(8,128)(2,1)}), bf16[256,4,384]{0,2,1:T(8,128)(2,1)}, u32[]{:S(2)}, u32[]{:S(2)}) async-start(bf16[256,4,384]{0,2,1:T(8,128)(2,1)} %bitcast.827), calls=%async_computation.2 | async-start | bytes 1572864 | tf_op jit(solution)/shard_map/all_to_all | solution.py:216
  261.7 41.8 %all-gather.13.cloned.1.call-start = ((), (), s32[]{:S(2)}) async-start(), calls=%async_computation.26 | async-start | bytes 1769472 | tf_op jit(solution)/shard_map/all_gather | solution.py:20
  266.8 78.8 %all-gather.11.cloned.1.call-start = ((), (), s32[]{:S(2)}) async-start(), calls=%async_computation.25 | async-start | bytes 1769472 | tf_op jit(solution)/shard_map/all_gather | solution.py:20
  394.8 75.5 %all-to-all-start.9 = ((bf16[4,2,49152]{2,1,0:T(2,128)(2,1)}), bf16[4,2,49152]{2,1,0:T(2,128)(2,1)}, u32[]{:S(2)}, u32[]{:S(2)}) async-start(bf16[4,2,49152]{2,1,0:T(2,128)(2,1)} %reshape.2516), calls=%async_computation.9 | async-start | bytes 1572864 | tf_op jit(solution)/shard_map/all_to_all | solution.py:244
  399.0 48.4 %all-gather.17.cloned.1.call-start = ((), (), s32[]{:S(2)}) async-start(), calls=%async_computation.28 | async-start | bytes 1769472 | tf_op jit(solution)/shard_map/all_gather | solution.py:20
  401.2 62.2 %all-gather.15.cloned.1.call-start = ((), (), s32[]{:S(2)}) async-start(), calls=%async_computation.27 | async-start | bytes 1769472 | tf_op jit(solution)/shard_map/all_gather | solution.py:20
  470.3 15.9 %all-to-all-start.4 = ((bf16[4,2,49152]{2,1,0:T(2,128)(2,1)}), bf16[4,2,49152]{2,1,0:T(2,128)(2,1)}, u32[]{:S(2)}, u32[]{:S(2)}) async-start(bf16[4,2,49152]{2,1,0:T(2,128)(2,1)} %reshape.2518), calls=%async_computation.4 | async-start | bytes 1572864 | tf_op jit(solution)/shard_map/all_to_all | solution.py:244
  486.3 24.5 %all-to-all-start.19 = ((f32[1024,1,384]{2,1,0:T(1,128)}), f32[1024,1,384]{2,1,0:T(1,128)}, u32[]{:S(2)}, u32[]{:S(2)}) async-start(f32[1024,1,384]{2,1,0:T(1,128)} %copy.395), calls=%async_computation.19 | async-start | bytes 3145728 | tf_op jit(solution)/shard_map/all_to_all | solution.py:275
  510.8 29.9 %all-to-all-start.14 = ((f32[1024,1,384]{2,1,0:T(1,128)}), f32[1024,1,384]{2,1,0:T(1,128)}, u32[]{:S(2)}, u32[]{:S(2)}) async-start(f32[1024,1,384]{2,1,0:T(1,128)} %copy.372), calls=%async_computation.14 | async-start | bytes 3145728 | tf_op jit(solution)/shard_map/all_to_all | solution.py:275
  549.5 18.6 %all-to-all-start.12 = ((f32[4,1,512]{2,1,0:T(1,128)}), f32[4,1,512]{2,1,0:T(1,128)S(1)}, u32[]{:S(2)}, u32[]{:S(2)}) async-start(f32[4,1,512]{2,1,0:T(1,128)} %reshape.2522), calls=%async_computation.12 | async-start | bytes 16384 | tf_op jit(solution)/shard_map/all_to_all | solution.py:278
  568.1 39.8 %all-to-all-start.16 = ((f32[1024,1,384]{2,1,0:T(1,128)}), f32[1024,1,384]{2,1,0:T(1,128)}, u32[]{:S(2)}, u32[]{:S(2)}) async-start(f32[1024,1,384]{2,1,0:T(1,128)} %copy.381), calls=%async_computation.16 | async-start | bytes 3145728 | tf_op jit(solution)/shard_map/all_to_all | solution.py:277
  607.9 28.0 %all-to-all-start.18 = ((f32[1024,1,384]{2,1,0:T(1,128)}), f32[1024,1,384]{2,1,0:T(1,128)}, u32[]{:S(2)}, u32[]{:S(2)}) async-start(f32[1024,1,384]{2,1,0:T(1,128)} %copy.390), calls=%async_computation.18 | async-start | bytes 3145728 | tf_op jit(solution)/shard_map/all_to_all | solution.py:276
  635.9 43.4 %all-to-all-start.11 = ((f32[1024,1,384]{2,1,0:T(1,128)}), f32[1024,1,384]{2,1,0:T(1,128)}, u32[]{:S(2)}, u32[]{:S(2)}) async-start(f32[1024,1,384]{2,1,0:T(1,128)} %copy.358), calls=%async_computation.11 | async-start | bytes 3145728 | tf_op jit(solution)/shard_map/all_to_all | solution.py:277
  679.2 46.6 %all-to-all-start.13 = ((f32[1024,1,384]{2,1,0:T(1,128)}), f32[1024,1,384]{2,1,0:T(1,128)}, u32[]{:S(2)}, u32[]{:S(2)}) async-start(f32[1024,1,384]{2,1,0:T(1,128)} %copy.367), calls=%async_computation.13 | async-start | bytes 3145728 | tf_op jit(solution)/shard_map/all_to_all | solution.py:276
  683.6 322.2 %all-reduce.39.cloned.1.call-start = ((), (), s32[]{:S(2)}) async-start(), calls=%async_computation.29 | async-start | bytes 4827136 | tf_op jit(solution)/shard_map/psum | solution.py:312
  837.4 16.4 %collective-permute-start.3 = (f32[3,1536]{1,0:T(4,128)S(1)}, f32[3,1536]{1,0:T(4,128)S(1)}, u32[]{:S(2)}, u32[]{:S(2)}) collective-permute-start(f32[3,1536]{1,0:T(4,128)S(1)} %pad_add_fusion.2), channel_id=1, source_target_pairs={{1,0},{2,1},{3,2},{4,3},{5,4},{6,5},{7,6},{9,8},{10,9},{11,10},{12... | collective-permute-start | bytes 55304 | tf_op jit(solution)/shard_map/ppermute | solution.py:15
  838.7 16.9 %collective-permute-start.2 = (f32[3,1536]{1,0:T(4,128)S(1)}, f32[3,1536]{1,0:T(4,128)S(1)}, u32[]{:S(2)}, u32[]{:S(2)}) collective-permute-start(f32[3,1536]{1,0:T(4,128)S(1)} %pad_add_fusion.3), channel_id=1, source_target_pairs={{1,0},{2,1},{3,2},{4,3},{5,4},{6,5},{7,6},{9,8},{10,9},{11,10},{12... | collective-permute-start | bytes 55304 | tf_op jit(solution)/shard_map/ppermute | solution.py:15
  860.5 272.6 %all-reduce.37.cloned.1.call-start = ((), (), s32[]{:S(2)}) async-start(), calls=%async_computation.23 | async-start | bytes 294912 | tf_op jit(solution)/shard_map/psum | solution.py:312
  867.9 381.1 %reduce-scatter.5.cloned.1.call-start = ((), (), s32[]{:S(2)}) async-start(), calls=%async_computation.24 | async-start | bytes 4866048 | tf_op jit(solution)/shard_map/reduce_scatter | solution.py:310
  874.0 516.1 %reduce-scatter.3.cloned.1.call-start = ((), (), s32[]{:S(2)}) async-start(), calls=%async_computation.22 | async-start | bytes 9732096 | tf_op jit(solution)/shard_map/reduce_scatter | solution.py:309
  (225 other events, 4279.4 us)
Sparse Core Ops, SparseCore 0:
  266.9 10.8 all-gather.12
  299.0 10.8 all-gather.10
  401.4 10.9 all-gather.16
  447.5 10.9 all-gather.14
  860.7 145.0 all-reduce.38
  1012.7 120.4 all-reduce.36
  1140.1 108.8 reduce-scatter.4
  1255.5 134.4 reduce-scatter.2
where the time goes:
time: 1410 us; the launch traced here: 1400 us
  waiting for transfers between devices  529 us (38%)
  local copies, waits for them, and re-layouts  288 us (20%)
  matrix products  278 us (20%)
  other arithmetic  185 us (13%)
  starting transfers between devices  96.1 us (7%)
  between operations  23.6 us (2%)
    psum x2, waiting for transfers between devices, per_device(): lax.psum((small_total[0], small_total[1], small_total[2], small_total[3],...  235 us
    reduce_scatter x1, waiting for transfers between devices, per_device(): lax.psum_scatter(up_total, ('dp', 'seq', 'head'), scatter_dimension=1, ti...  141 us
    reduce_scatter x1, waiting for transfers between devices, per_device(): lax.psum_scatter(down_total, ('dp', 'seq', 'head'), scatter_dimension=0,...  116 us
    unnamed x471, local copies, waits for them, and re-layouts  67.4 us
    dot_general x18, matrix products, block_mix(): mapped = jnp.einsum('tbi,bio->tbo', grouped, weight, precision=HIGH)  65.1 us
    dot_general x6, matrix products, mix_out(): hidden = jnp.einsum('hts,shd->thd', scores * decays, values, precision=HIGH)  58.5 us
    reshape x16, local copies, waits for them, and re-layouts, block_mix(): grouped = values_in.reshape(values_in.shape[0], blocks, size_in)  45.4 us
    dot_general x6, matrix products, mix_out(): jnp.einsum('thd,shd->hts', queries, key_rows, precision=HIGH) * factor  37.3 us
  transfers between devices with their start and end apart: 32, of which 11 were waited for; matrix products, arithmetic and copies ran while one was open for 36% of the time, Pallas kernels for 0%

commit v1 on v0

v1 whole, which is shorter than its diff:
```python
from functools import partial

import jax
import jax.numpy as jnp
from jax import lax
from jax.experimental import pallas as pl
from jax.experimental.pallas import tpu as pltpu
from jax.sharding import PartitionSpec as P

EPS = 1e-05
HIGH = lax.Precision.HIGHEST
BF = jnp.bfloat16
F32 = jnp.float32
EDGE = 16
SMALL = 48
NEVER = -1e30
VMEM_BYTES = 60 * 1024 * 1024


def mm(a, b):
    return lax.dot_general(a, b, (((1,), (0,)), ((), ())), preferred_element_type=F32)


def nt(a, b):
    return lax.dot_general(a, b, (((1,), (1,)), ((), ())), preferred_element_type=F32)


def tn(a, b):
    return lax.dot_general(a, b, (((0,), (0,)), ((), ())), preferred_element_type=F32)


def split(v):
    high = v.astype(BF)
    return high, (v - high.astype(F32)).astype(BF)


def iota(shape, dim):
    return lax.broadcasted_iota(jnp.int32, shape, dim)


def seg_of(pos, sc, seqs, m):
    total = (pos >= sc[2 + m * seqs]).astype(jnp.int32)
    for e in range(1, seqs):
        total = total + (pos >= sc[2 + m * seqs + e]).astype(jnp.int32)
    return total


def pick(refs, which, dest, rows):
    for at, ref in enumerate(refs):

        @pl.when(which == at)
        def _(ref=ref):
            dest[...] = ref[rows, :]


def put(refs, which, value):
    for at, ref in enumerate(refs):

        @pl.when(which == at)
        def _(ref=ref):
            ref[...] = value


def lane_sums(v):
    ones = jnp.ones((8, v.shape[1]), BF)
    high, low = split(v)
    return nt(ones, high) + nt(ones, low)


def running_sum(v):
    width = v.shape[1] // 8
    tri = (iota((width, width), 0) <= iota((width, width), 1)).astype(BF)
    chunks = jnp.concatenate([v[:, c * width : (c + 1) * width] for c in range(8)], axis=0)
    high, rest = split(chunks)
    rest = chunks - high.astype(F32)
    mid, low = split(rest)
    within = mm(high, tri) + (mm(mid, tri) + mm(low, tri))
    carry, parts = jnp.zeros((1, 1), F32), []
    for c in range(8):
        parts.append(within[c : c + 1, :] + carry)
        carry = carry + within[c : c + 1, width - 1 : width]
    return jnp.concatenate(parts, axis=1)


LANES = 128


def to_tiles(ext, start, value):
    rows, width = value.shape
    for t in range(width // LANES):
        ext[t, start : start + rows, :] = value[:, t * LANES : (t + 1) * LANES]


def conv_blocks(ext, rows, ages, cw, cb, step):
    for r in range(0, rows, step):
        age = jnp.broadcast_to(ages[r : r + step], (step, LANES))
        for t in range(ext.shape[0]):
            lanes = slice(t * LANES, (t + 1) * LANES)
            lags = [ext[t, EDGE + r : EDGE + r + step, :]]
            for lag in range(1, 4):
                earlier = ext[t, EDGE + r - lag : EDGE + r - lag + step, :]
                lags.append(jnp.where(age >= lag, earlier, 0.0))
            total = cb[:, lanes] + cw[3:4, lanes] * lags[0]
            for lag in range(1, 4):
                total = total + cw[3 - lag : 4 - lag, lanes] * lags[lag]
            yield slice(r, r + step), lanes, total, lags


def folded(v):
    return sum(v[e : e + 8] for e in range(8, v.shape[0], 8)) + v[0:8]


def front_kernel(
    sc, x0, x1, x2, x3, xh, marks, gain, w_in, w_gt, cw, cb, wq, wk, wv, gq, gk, gv, *rest
):
    normed_o, gz_o, five_o, halo_o, gt_o, xs, ext = rest[-7:]
    i = pl.program_id(0)
    chunk = xs.shape[0]
    pick((x0, x1, x2, x3), i ^ sc[0], xs, slice(0, chunk))

    def norm(rows):
        stream = rows.astype(F32)
        centred = stream - jnp.mean(stream, axis=-1, keepdims=True)
        variance = jnp.mean(centred * centred, axis=-1, keepdims=True)
        return (centred * lax.rsqrt(variance + EPS) * gain[...]).astype(BF)

    @pl.when(i == 0)
    def _():
        edge = mm(norm(xh[...]), w_in[...]).astype(BF)
        to_tiles(ext, 0, edge.astype(F32))
        halo_o[...] = edge

    @pl.when(i > 0)
    def _():
        ext[:, 0:EDGE, :] = ext[:, chunk : chunk + EDGE, :]

    for r in range(0, chunk, 32):
        normed_o[r : r + 32, :] = norm(xs[r : r + 32, :])
    inner = mm(normed_o[...], w_in[...]).astype(BF)
    five_o[4] = inner
    to_tiles(ext, EDGE, inner.astype(F32))
    gz_o[...] = mm(normed_o[...], w_gt[...])
    ages = jnp.transpose(marks[...])[:, 0:1]
    for rows, lanes, total, _ in conv_blocks(ext, chunk, ages, cw, cb, 64):
        five_o[3, rows, lanes] = (total / (1.0 + jnp.exp(-total))).astype(BF)
    q = mm(five_o[3], wq[...]).astype(BF)
    k = mm(five_o[3], wk[...]).astype(BF)
    v = mm(five_o[4], wv[...]).astype(BF)
    five_o[0] = q
    five_o[1] = k
    five_o[2] = v
    gt_o[...] = nt(gq[...], q) + nt(gk[...], k) + nt(gv[...], v)


def gates_kernel(seqs, sc, ib, fb, g0, g1, g2, g3, k, v, rows_o, s_o):
    m = pl.program_id(0)
    h, s = sc[0], sc[1]
    span, width = k.shape
    factor = width ** (-0.5)
    lin = (g0[...] + g1[...] + g2[...] + g3[...]).astype(BF).astype(F32)
    r = iota(lin.shape, 0)
    ig = jnp.sum(jnp.where(r == 2 * h, lin, 0.0), axis=0, keepdims=True) + ib[h]
    fg = jnp.sum(jnp.where(r == 2 * h + 1, lin, 0.0), axis=0, keepdims=True) + fb[h]
    pos = s * span + iota((1, span), 1)
    seg = seg_of(pos, sc, seqs, m)
    valid = (seg < seqs).astype(F32)
    log_keep = valid * (jnp.minimum(fg, 0.0) - jnp.log1p(jnp.exp(-jnp.abs(fg))))
    cum = running_sum(log_keep)
    prev = jnp.where(s == 0, -1, seg_of(s * span - 1, sc, seqs, m))
    last = seg_of(s * span + span - 1, sc, seqs, m)
    carried = jnp.where(seg == prev, jnp.exp(cum), 0.0)
    offset = jnp.where(seg < seqs, ig - cum, NEVER)
    tail = jnp.exp(jnp.where(seg == last, cum[:, span - 1 : span] + offset, NEVER)) * factor
    slope = valid / (1.0 + jnp.exp(fg))
    rows = jnp.zeros((8, span), F32)
    for at, row in enumerate((cum, offset, seg.astype(F32), slope, carried, tail, valid)):
        rows = jnp.where(r == at, row, rows)
    rows_o[...] = rows
    cols = jnp.transpose(rows)
    high, low = split(k[...].astype(F32) * cols[:, 5:6])
    s_o[...] = tn(high, v[...]) + tn(low, v[...])


def mix_kernel(
    sc, rows, s_in, gn, sk, five, gz, normed, c0, c1, c2, c3a, c3b, w_dn, *rest
):
    p0, p1, p2, p3, gd_o, gg_o, four_o, ds_o, small_o, sums_o = rest[:10]
    fb, zb, nb, cb, wb, pb, four, gd, gg, go, acc, a_high, decays = rest[10:23]
    q2, v2, dh2, dbr, brs, dgs, in_sems, out_sems = rest[23:]
    h = sc[0]
    micros, _, span, width = fb.shape
    chunk = acc.shape[0]
    two = 2 * chunk
    factor = width ** (-0.5)

    def rows_of(i, size=chunk):
        return pl.ds(pl.multiple_of(i * size, size), size)

    def qkv_in(m, j):
        at, three = rows_of(j, two), pl.ds(0, 3)
        to = fb.at[m, three, at]
        return pltpu.make_async_copy(five.at[m, three, at], to, in_sems.at[m, 0, j])

    def chunk_in(m, i):
        at = rows_of(i)
        return [
            pltpu.make_async_copy(five.at[m, 3, at], fb.at[m, 3, at], in_sems.at[m, 1, i]),
            pltpu.make_async_copy(gz.at[m, at], zb.at[m, at], in_sems.at[m, 2, i]),
            pltpu.make_async_copy(normed.at[m, at], nb.at[m, at], in_sems.at[m, 3, i]),
        ]

    def cot_in(m, rel, i, last=False):
        ref = (c0.at[m], c1.at[m], c2.at[m], c3b if last else c3a)[rel]
        return pltpu.make_async_copy(ref, cb.at[m, i], in_sems.at[m, 4, i])

    weight_in = pltpu.make_async_copy(w_dn.at[rows_of(h, width)], wb, in_sems.at[0, 5, 0])

    def others_in(m, last):
        for rel in range(4):
            cot_in(m, rel, rel ^ h, last).start()
        for copy in (*chunk_in(m, 1), qkv_in(m, 1), *chunk_in(m, 2), *chunk_in(m, 3)):
            copy.start()

    for copy in (qkv_in(0, 0), weight_in, *chunk_in(0, 0)):
        copy.start()
    others_in(0, False)
    small_o[...] = jnp.zeros_like(small_o)
    gd[...] = jnp.zeros_like(gd)
    gg[...] = jnp.zeros_like(gg)

    def pair_out(m, rel, i):
        at = pl.ds(2 * m, 2)
        to = (p0, p1, p2, p3)[rel].at[at]
        return pltpu.make_async_copy(pb.at[i, at], to, out_sems.at[m, 0, rel])

    def rows_out(m, i):
        at = rows_of(i)
        return [
            pltpu.make_async_copy(four.at[m, 0, at], four_o.at[m, 0, at], out_sems.at[m, 1, i]),
            pltpu.make_async_copy(four.at[m, 3, at], four_o.at[m, 3, at], out_sems.at[m, 2, i]),
        ]

    def key_out(m, j):
        at, pair = rows_of(j, two), pl.ds(1, 2)
        to = four_o.at[m, pair, at]
        return pltpu.make_async_copy(four.at[m, pair, at], to, out_sems.at[m, 3, j])

    grads_out = [
        pltpu.make_async_copy(go.at[0], gd_o, out_sems.at[0, 4, 0]),
        pltpu.make_async_copy(go.at[1], gg_o, out_sems.at[0, 4, 1]),
    ]

    def one(at_step, none):
        m, i = at_step // 4, at_step % 4

        @pl.when(i == 0)
        def _():
            four[m, 1] = jnp.zeros((span, width), F32)
            four[m, 2] = jnp.zeros((span, width), F32)
            ds_o[m] = jnp.zeros((width, width), F32)

        @pl.when(at_step == 1)
        def _():
            for copy in (qkv_in(1, 0), *chunk_in(1, 0)):
                copy.start()
            others_in(1, True)

        start = pl.multiple_of(i * chunk, chunk)
        own = pl.ds(start, chunk)

        @pl.when(i % 2 == 0)
        def _():
            at = rows_of(i // 2, two)
            qkv_in(m, i // 2).wait()
            v2[at, 0:width] = fb[m, 2, at, :]
            v2[at, width:] = fb[m, 2, at, :]

        acc[...] = jnp.zeros_like(acc)
        here = start + iota((chunk, 1), 0)
        cols = jnp.transpose(rows[m, :, own])
        cum, seg, carried, valid = cols[:, 0:1], cols[:, 2:3], cols[:, 4:5], cols[:, 6:7]

        def attend(j, none):
            at = rows_of(j, two)
            scores = nt(fb[m, 0, own, :], fb[m, 1, at, :]) * factor
            allowed = (seg == rows[m, 2:3, at]) & (j * two + iota((1, two), 1) <= here)
            decay = jnp.exp(jnp.where(allowed, cum + rows[m, 1:2, at], NEVER))
            decays[j] = decay
            high, low = split(scores * decay)
            a_high[j] = high
            acc[...] += mm(high, fb[m, 2, at, :]) + mm(low, fb[m, 2, at, :])
            return none

        lax.fori_loop(0, i // 2 + 1, attend, 0)
        q2[:, 0:width] = fb[m, 0, own, :]
        q2[:, width:] = fb[m, 0, own, :]
        acc[...] += carried * mm(q2[...], jnp.concatenate(split(s_in[m]), axis=0))

        @pl.when(at_step == 0)
        def _():
            weight_in.wait()

        for copy in chunk_in(m, i):
            copy.wait()
        cot_in(m, 0, i).wait()
        cb[m, i] = (cb[m, i].astype(F32) * valid).astype(BF)
        dbr[...] = nt(cb[m, i], wb[...])
        step = 32
        sum_gn, sum_sk = jnp.zeros((8, width), F32), jnp.zeros((8, width), F32)
        for r in range(0, chunk, step):
            part, at = slice(r, r + step), pl.ds(start + r, step)
            hidden = acc[part, :]
            centred = hidden - jnp.mean(hidden, axis=-1, keepdims=True)
            rstd = lax.rsqrt(jnp.mean(centred * centred, axis=-1, keepdims=True) + EPS)
            exact = centred * rstd
            normed_h = exact.astype(BF).astype(F32)
            gate = zb[m, at, :]
            sig = 1.0 / (1.0 + jnp.exp(-gate))
            gate_act = gate * sig
            act_f = fb[m, 3, at, :].astype(F32)
            mid = normed_h * gn[...] + sk[...] * act_f
            brs[part, :] = (mid * gate_act).astype(BF)
            d_branch = dbr[part, :]
            d_mid = d_branch * gate_act
            dgs[part, :] = (d_branch * mid * (sig + gate_act * (1.0 - sig))).astype(BF)
            sum_gn, sum_sk = sum_gn + folded(d_mid * normed_h), sum_sk + folded(d_mid * act_f)
            four[m, 3, at, :] = d_mid * sk[...]
            d_norm = (d_mid * gn[...]).astype(BF).astype(F32)
            along = jnp.mean(d_norm * exact, axis=-1, keepdims=True)
            d_hid = rstd * (d_norm - jnp.mean(d_norm, axis=-1, keepdims=True) - exact * along)
            dh_high, dh_low = split(d_hid)
            dh2[part, 0:width] = dh_high
            dh2[part, width:] = dh_low
            q2[part, width:] = (d_hid * carried[part]).astype(BF)
        small_o[0:1, :] += jnp.sum(sum_gn, axis=0, keepdims=True)
        small_o[1:2, :] += jnp.sum(sum_sk, axis=0, keepdims=True)
        pb[i, 2 * m] = brs[...]
        pb[i, 2 * m + 1] = dgs[...]
        gd[...] += tn(brs[...], cb[m, i])
        gg[...] += tn(dgs[...], nb[m, own, :])
        ds_o[m] += tn(fb[m, 0, own, :], q2[:, width:])
        acc[...] = carried * nt(dh2[:, 0:width], s_in[m].astype(BF))
        for rel in range(4):

            @pl.when((i ^ h) == rel)
            def _(rel=rel):
                pair_out(m, rel, i).start()

        @pl.when(at_step == 4 * micros - 1)
        def _():
            go[0] = gd[...].astype(BF)
            go[1] = gg[...].astype(BF)
            for copy in grads_out:
                copy.start()

        def attend_back(j, none):
            at = rows_of(j, two)
            d_att = nt(dh2[...], v2[at, :])
            four[m, 2, at, :] += tn(a_high[j], dh2[:, 0:width])
            w_high, w_low = split(decays[j] * d_att * factor)
            acc[...] += mm(w_high, fb[m, 1, at, :]) + mm(w_low, fb[m, 1, at, :])
            four[m, 1, at, :] += tn(w_high, fb[m, 0, own, :]) + tn(w_low, fb[m, 0, own, :])

            @pl.when(i == 3)
            def _():
                key_out(m, j).start()

            return none

        lax.fori_loop(0, i // 2 + 1, attend_back, 0)
        four[m, 0, own, :] = acc[...]
        for copy in rows_out(m, i):
            copy.start()
        sums_o[m, :, own] = lane_sums(acc[...] * fb[m, 0, own, :].astype(F32))
        return none

    lax.fori_loop(0, 4 * micros, one, 0)

    def finish(at_step, none):
        m, at = at_step // 4, rows_of(at_step % 4)
        col_sum = lane_sums(four[m, 1, at, :] * fb[m, 1, at, :].astype(F32))
        held = sums_o[m, :, at]
        sums_o[m, :, at] = jnp.where(iota((8, chunk), 0) == 0, col_sum, held - col_sum)
        return none

    lax.fori_loop(0, 4 * micros, finish, 0)
    for m in range(micros):
        for rel in range(4):
            pair_out(m, rel, rel ^ h).wait()
        for i in range(4):
            for copy in rows_out(m, i):
                copy.wait()
        for copy in (key_out(m, 0), key_out(m, 1)):
            copy.wait()
    for copy in grads_out:
        copy.wait()


def gates_back_kernel(sc, k, v, rows, sums, ds_out, dg_o):
    h, s = sc[0], sc[1]
    span = k.shape[0]
    turned = nt(twice(v[...], 1), jnp.concatenate(split(ds_out[...]), axis=1))
    cross = rows[5:6, :] * lane_sums(turned * k[...].astype(F32))
    r = iota((8, span), 0)
    d_ig = sums[0:1, :] + cross[0:1, :]
    d_cum = sums[1:2, :] - cross[0:1, :]
    running = running_sum(d_cum)
    total = jnp.where(s == 0, 0.0, running[:, span - 1 : span])
    d_fg = rows[3:4, :] * (total - running + d_cum)
    dg_o[...] = jnp.where(r == 2 * h, d_ig, jnp.where(r == 2 * h + 1, d_fg, 0.0))


def twice(v, axis=0):
    return jnp.concatenate([v, v], axis=axis)


def silu_slope(v):
    sig = 1.0 / (1.0 + jnp.exp(-v))
    return sig * (1.0 + v * (1.0 - sig))


def edge_kernel(
    sc, dq, dk, d0, d1, d2, d3, inner, halo, marks, skip_d, gq, gk, wq, wk, cw, cb, dcs_o, ext
):
    to_tiles(ext, 0, halo[...].astype(F32))
    to_tiles(ext, EDGE, inner[...].astype(F32))
    g_all = jnp.concatenate(split(d0[...] + d1[...] + d2[...] + d3[...]), axis=0)
    dq_h, dq_l = split(dq[...] + tn(g_all, twice(gq[...]))[0:EDGE, :])
    dk_h, dk_l = split(dk[...] + tn(g_all, twice(gk[...]))[0:EDGE, :])
    d_act = skip_d[...] + nt(dq_h, wq[...]) + nt(dq_l, wq[...]) + nt(dk_h, wk[...]) + nt(dk_l, wk[...])
    for _, lanes, total, _ in conv_blocks(ext, EDGE, jnp.transpose(marks[...])[0:EDGE, 0:1], cw, cb, EDGE):
        dcs_o[:, lanes] = d_act[:, lanes] * silu_slope(total)


def front_back_kernel(
    sc, d0, d1, d2, d3, rows_t, marks, ds_out, halo, small_i, edge, gq, gk, gv, wq, wk, wv,
    cw, cb, gain, on_map_i, to_lanes_i, four, five, normed, gg_i, w_up, *rest,
):
    i0, i1, i2, i3, late_o = rest[:5]
    fb, qb, nb, bb, wb, ib, ext, nxt, wide, fq, fk, fv, d_act, gi = rest[5:19]
    on_map, to_lanes, gg, small_o, in_sems, out_sems = rest[19:]
    h = sc[0]
    micros, _, span, width = fb.shape
    chunk = d_act.shape[0]

    def inward(m, i):
        at = pl.ds(pl.multiple_of(i * chunk, chunk), chunk)
        return [
            pltpu.make_async_copy(four.at[m, :, at], fb.at[m, :, at], in_sems.at[m, 0, i]),
            pltpu.make_async_copy(five.at[m, :, at], qb.at[m, :, at], in_sems.at[m, 1, i]),
            pltpu.make_async_copy(normed.at[m, at], nb.at[m, at], in_sems.at[m, 2, i]),
        ]

    def before(m, i):
        at = pl.ds(i * chunk - EDGE, EDGE)
        return pltpu.make_async_copy(five.at[m, 4, at], bb.at[m, i], in_sems.at[m, 3, i])

    befores = [before(m, i) for m in range(micros) for i in range(1, 4)]
    consts = [
        pltpu.make_async_copy(on_map_i, on_map, in_sems.at[0, 4, 0]),
        pltpu.make_async_copy(to_lanes_i, to_lanes, in_sems.at[0, 4, 1]),
        pltpu.make_async_copy(gg_i, gg, in_sems.at[0, 4, 2]),
    ]
    for at in range(2):
        columns = pl.ds(pl.multiple_of(at * (w_up.shape[1] // 2) + h * width, width), width)
        to = wb.at[:, pl.ds(at * width, width)]
        consts.append(pltpu.make_async_copy(w_up.at[:, columns], to, in_sems.at[1, 4, at]))
    for copy in (*inward(0, 3), *befores, *inward(0, 2), *inward(0, 1), *inward(0, 0)):
        copy.start()
    small_o[...] = jnp.zeros_like(small_o)
    small_o[41:43, :] += small_i[0:2, :]
    fq[...] = jnp.zeros_like(fq)
    fk[...] = jnp.zeros_like(fk)
    fv[...] = jnp.zeros_like(fv)
    gi[...] = jnp.zeros_like(gi)
    for m in range(micros):
        bb[m, 0] = halo[m]
    for copy in befores:
        copy.wait()

    def inner_out(m, rel, i):
        to = (i0, i1, i2, i3)[rel].at[m]
        return pltpu.make_async_copy(ib.at[m, i], to, out_sems.at[m, rel])

    def one(step, none):
        m, i = step // 4, 3 - step % 4

        @pl.when(i == 3)
        def _():
            to_tiles(nxt, chunk, edge[m])

        @pl.when(step == 1)
        def _():
            for at in (3, 2, 1, 0):
                for copy in inward(1, at):
                    copy.start()
            for copy in consts:
                copy.start()

        start = pl.multiple_of(i * chunk, chunk)
        own = pl.ds(start, chunk)
        for copy in inward(m, i):
            copy.wait()
        to_tiles(ext, 0, bb[m, i].astype(F32))
        to_tiles(ext, EDGE, qb[m, 4, own, :].astype(F32))
        dg = (d0[m, :, own] + d1[m, :, own]) + (d2[m, :, own] + d3[m, :, own])
        g_all = jnp.concatenate(split(dg), axis=0)
        for at in range(3):
            part = mm(g_all, qb[m, at, own, :])
            small_o[8 * at : 8 * at + 8, :] += part[0:8, :] + part[8:16, :]
        order = [dg[r : r + 1, :] for r in (0, 2, 4, 6, 1, 3, 5, 7)]
        small_o[45:46, 0:8] += lane_sums(jnp.concatenate(order, axis=0))[0:1, :]
        state = ds_out[m].astype(BF)
        tail = jnp.transpose(rows_t[m, :, own])[:, 5:6]
        both = jnp.transpose(marks[m, :, own])
        for at, gate in enumerate((gq, gk, gv)):
            total = fb[m, at, own, :] + tn(g_all, twice(gate[...]))
            if at == 1:
                total = total + tail * nt(qb[m, 2, own, :], state)
            if at == 2:
                total = total + tail * mm(qb[m, 1, own, :], state)
            high, low = split(total)
            wide[:, 2 * at * width : (2 * at + 1) * width] = high
            wide[:, (2 * at + 1) * width : (2 * at + 2) * width] = low
        maps = jnp.concatenate([wq[...], wq[...], wk[...], wk[...]], axis=1)
        d_act[...] = fb[m, 3, own, :] + nt(wide[:, 0 : 4 * width], maps)
        sums = [[0.0] * 5 for _ in range(width // LANES)]
        for at, lanes, total, lags in conv_blocks(ext, chunk, both[:, 0:1], cw, cb, 64):
            d_cs = d_act[at, lanes] * silu_slope(total)
            t = lanes.start // LANES
            nxt[t, at, :] = d_cs
            for lag in range(4):
                sums[t][3 - lag] = sums[t][3 - lag] + folded(d_cs * lags[lag])
            sums[t][4] = sums[t][4] + folded(d_cs)
        for t, group in enumerate(sums):
            for at, total in enumerate(group):
                lanes = slice(t * LANES, (t + 1) * LANES)
                small_o[36 + at : 37 + at, lanes] += jnp.sum(total, axis=0, keepdims=True)
        maps = jnp.concatenate([wv[...], wv[...]], axis=1)
        d_act[...] = nt(wide[:, 4 * width :], maps)
        fq[...] += tn(qb[m, 3, own, :], wide[:, 0:width])
        fk[...] += tn(qb[m, 3, own, :], wide[:, 2 * width : 3 * width])
        fv[...] += tn(qb[m, 4, own, :], wide[:, 4 * width : 5 * width])
        for r in range(0, chunk, 64):
            left = jnp.broadcast_to(both[r : r + 64, 1:2], (64, LANES))
            for t in range(width // LANES):
                lanes = slice(t * LANES, (t + 1) * LANES)
                total = d_act[r : r + 64, lanes] + cw[3:4, lanes] * nxt[t, r : r + 64, :]
                for lag in range(1, 4):
                    later = jnp.where(left >= lag, nxt[t, r + lag : r + lag + 64, :], 0.0)
                    total = total + cw[3 - lag : 4 - lag, lanes] * later
                ib[m, i, r : r + 64, lanes] = total.astype(BF)
        for rel in range(4):

            @pl.when((i ^ h) == rel)
            def _(rel=rel):
                inner_out(m, rel, i).start()

        gi[...] += tn(ib[m, i], nb[m, own, :])
        nxt[:, chunk : chunk + EDGE, :] = nxt[:, 0:EDGE, :]
        return none

    lax.fori_loop(0, 4 * micros, one, 0)
    late_o[0:width, :] = gi[...]
    for copy in consts:
        copy.wait()
    ones = (iota((16, width), 1) % 4 == iota((16, width), 0) % 4).astype(BF)
    for at, full in enumerate((fq, fk, fv)):
        high, low = split(full[...] * on_map[...])
        high, low = split(nt(ones, high) + nt(ones, low))
        compact = mm(high, to_lanes[...]) + mm(low, to_lanes[...])
        small_o[24 + 4 * at : 28 + 4 * at, :] += compact[0:4, :]
    both = gi[...] * jnp.transpose(wb[:, 0:width].astype(F32))
    both = both + gg[...].astype(F32) * jnp.transpose(wb[:, width:].astype(F32))
    total = jnp.sum(both, axis=0, keepdims=True) / gain[...]
    small_o[43:44, :] = total[:, 0:width]
    small_o[44:45, :] = total[:, width:]
    late_o[width:, 0:width] = small_o[0 : SMALL // 2, :]
    late_o[width:, width:] = small_o[SMALL // 2 :, :]
    for m in range(micros):
        for rel in range(4):
            inner_out(m, rel, rel ^ h).wait()


def tokens_kernel(seqs, sc, gain, *rest):
    (x_i, c_i), pairs, inners, (w_up, w_dn, out_o, back_o) = rest[:2], rest[2:6], rest[6:10], rest[10:14]
    x, c, ups, downs, acc, mix, dup, brs, sems = rest[14:]
    h = sc[0]
    micros, rows, dim = x.shape
    width = downs.shape[0] // 4
    inner = w_up.shape[1] // 2

    def place(rel, half=0, count=1):
        return pl.ds(pl.multiple_of((count * rel + half) * width, width), width)

    def columns_in(rel, half):
        at = pl.ds(pl.multiple_of(half * inner + (h ^ rel) * width, width), width)
        return pltpu.make_async_copy(w_up.at[:, at], ups.at[:, place(rel, half, 2)], sems.at[half, rel])

    def rows_in(rel):
        return pltpu.make_async_copy(w_dn.at[place(h ^ rel)], downs.at[place(rel)], sems.at[2, rel])

    def inner_in(m, rel, ref):
        to = dup.at[pl.ds(m * rows, rows), place(rel, 0, 2)]
        return pltpu.make_async_copy(ref.at[m], to, sems.at[3 + m, rel])

    def gate_in(m, rel, ref):
        to = dup.at[pl.ds(m * rows, rows), place(rel, 1, 2)]
        return pltpu.make_async_copy(ref.at[2 * m + 1], to, sems.at[5 + m, rel])

    def branch_in(m, rel, ref):
        to = brs.at[pl.ds(m * rows, rows), place(rel)]
        return pltpu.make_async_copy(ref.at[2 * m], to, sems.at[7 + m, rel])

    def first_in(rel, pair):
        return [rows_in(rel)] + [branch_in(m, rel, pair) for m in range(micros)]

    def second_in(rel, pair, ref):
        group = [columns_in(rel, 0), columns_in(rel, 1)]
        for m in range(micros):
            group = group + [inner_in(m, rel, ref), gate_in(m, rel, pair)]
        return group

    tokens_in = [
        pltpu.make_async_copy(x_i, x, sems.at[9, 0]),
        pltpu.make_async_copy(c_i, c, sems.at[9, 1]),
    ]
    for rel in range(4):
        for copy in first_in(rel, pairs[rel]):
            copy.start()
    for rel in range(4):
        for copy in second_in(rel, pairs[rel], inners[rel]):
            copy.start()
    for copy in tokens_in:
        copy.start()
    acc[...] = jnp.zeros_like(acc)
    for rel in range(4):
        for copy in first_in(rel, pairs[0]):
            copy.wait()
    mix[...] = mm(brs[...], downs[...])

    def one(rel, none):
        at = pl.ds(pl.multiple_of(2 * rel * width, 2 * width), 2 * width)
        for copy in second_in(rel, pairs[0], inners[0]):
            copy.wait()
        acc[...] += nt(dup[:, at], ups[:, at])
        return none

    lax.fori_loop(0, 4, one, 0)
    for copy in tokens_in:
        copy.wait()
    step = 128

    def finish(at, none):
        m, r = at // (rows // step), pl.multiple_of(at % (rows // step) * step, step)
        here, both = pl.ds(r, step), pl.ds(pl.multiple_of(at * step, step), step)
        stream = x[m, here, :].astype(F32)
        pos = (sc[1] * 4 + h) * rows + r + iota((step, 1), 0)
        valid = (seg_of(pos, sc, seqs, m) < seqs).astype(F32)
        out_o[m, here, :] = (stream + valid * mix[both, :]).astype(BF)
        centred = stream - jnp.mean(stream, axis=-1, keepdims=True)
        rstd = lax.rsqrt(jnp.mean(centred * centred, axis=-1, keepdims=True) + EPS)
        exact = centred * rstd
        d_n = acc[both, :] * gain[...]
        along = jnp.mean(d_n * exact, axis=-1, keepdims=True)
        d_x = rstd * (d_n - jnp.mean(d_n, axis=-1, keepdims=True) - exact * along)
        back_o[m, here, :] = (c[m, here, :].astype(F32) + d_x).astype(BF)
        return none

    lax.fori_loop(0, micros * rows // step, finish, 0)


def table_kernel(
    sc, t0, t1, t2, t3, gate_o, wq_o, wk_o, wv_o, cw_o, cb_o, gn_o, sk_o, ln_o, ib_o, fb_o, small
):
    heads, _, width = small.shape
    blocks = width // 4
    for rel, ref in enumerate((t0, t1, t2, t3)):
        small[sc[0] ^ rel, 0 : SMALL // 2, :] = ref[:, 0:width]
        small[sc[0] ^ rel, SMALL // 2 :, :] = ref[:, width:]
    for h in range(heads):
        at = slice(h * width, (h + 1) * width)
        for part in range(3):
            start = (part * heads + h) * width
            gate_o[:, start : start + width] = small[h, 8 * part : 8 * part + 8, :]
        cw_o[:, at] = small[h, 36:40, :]
        for row, ref in ((40, cb_o), (41, gn_o), (42, sk_o)):
            ref[at] = small[h, row, :]
    for at, ref in enumerate((wq_o, wk_o, wv_o)):
        rows = slice(24 + 4 * at, 28 + 4 * at)
        for i in range(4):
            lanes = slice(i * blocks, (i + 1) * blocks)
            ref[i] = jnp.concatenate([small[h, rows, lanes] for h in range(heads)], axis=1)
    for half in range(2):
        ln_o[half * width : (half + 1) * width] = sum(small[h, 43 + half, :] for h in range(heads))
    ib_o[...] = small[0, 45, 0:4]
    fb_o[...] = small[0, 45, 4:8]


def whole(shape):
    return pl.BlockSpec(shape, lambda i, sc: (0,) * len(shape))


def by_chunk(rows, width):
    return pl.BlockSpec((rows, width), lambda i, sc: (i, 0))


def head_cols(rows, width, skip=0):
    return pl.BlockSpec((rows, width), lambda i, sc: (0, sc[0] + skip))


def head_rows(rows, width, skip=0):
    return pl.BlockSpec((rows, width), lambda i, sc: (sc[0] + skip, 0))


def of_micro(m, *shape):
    rest = (0,) * len(shape)
    return pl.BlockSpec((None,) + shape, lambda i, sc: (i if m is None else m,) + rest)


def micro_chunk(m, rows, width):
    return pl.BlockSpec((None, rows, width), lambda i, sc: (m, i, 0))


def micro_lanes(m, rows):
    return pl.BlockSpec((None, 8, rows), lambda i, sc: (m, 0, i))


def call(body, grid, in_specs, out_specs, out_shape, scratch, micros_us, args, aliases=None):
    return pl.pallas_call(
        body,
        grid_spec=pltpu.PrefetchScalarGridSpec(
            num_scalar_prefetch=1,
            grid=grid,
            in_specs=in_specs,
            out_specs=out_specs,
            scratch_shapes=scratch,
        ),
        out_shape=[jax.ShapeDtypeStruct(shape, dtype) for shape, dtype in out_shape],
        compiler_params=pltpu.CompilerParams(vmem_limit_bytes=VMEM_BYTES),
        cost_estimate=pl.CostEstimate(
            flops=int(micros_us * 0.05 * 1.15e9), bytes_accessed=1_000_000, transcendentals=0
        ),
        input_output_aliases=aliases or {},
    )(*args)


def together(*groups):
    flat = iter(lax.optimization_barrier([part for group in groups for part in group]))
    return [[next(flat) for _ in group] for group in groups]


def after(value, *others):
    return lax.optimization_barrier((value, *others))[0]


def per_device(
    tokens, lengths, ln_gain, w_up, conv_w, conv_b, w_q, w_k, w_v, gate_w, i_bias, f_bias,
    gn_gain, skip, w_down, cotangent,
):
    micros, rows, dim = tokens.shape
    inner = w_down.shape[0]
    heads = i_bias.shape[0]
    width = inner // heads
    seqs = lengths.shape[2]
    dp, sq, hd = lax.axis_size("dp"), lax.axis_size("seq"), lax.axis_size("head")
    assert hd == heads == 4 and sq == 2 and micros == 2 and conv_w.shape[0] == 4
    ranks = dp * sq
    every = ranks * hd
    span = rows * hd
    h, s = lax.axis_index("head"), lax.axis_index("seq")
    ends = jnp.cumsum(lengths[:, 0], axis=1).astype(jnp.int32)
    sc = jnp.concatenate([jnp.stack([h, s]).astype(jnp.int32), ends.reshape(-1)])

    def across(value, rel):
        return lax.ppermute(value, "head", [(at, at ^ rel) for at in range(hd)])

    def exchange(parts):
        return [parts[0]] + [across(parts[rel], rel) for rel in range(1, hd)]

    def gather(value):
        return exchange([value] * hd)

    def halo_of(parts):
        ends_of = [part[rows - EDGE :] for part in parts]
        last_rows = ends_of[0]
        for rel in range(1, hd):
            last_rows = jnp.where(h == (hd - 1) ^ rel, ends_of[rel], last_rows)
        return lax.ppermute(last_rows, "seq", [(0, 1)])

    xs = [gather(tokens[0])]

    place = s * span + jnp.arange(span, dtype=jnp.int32)[None, :, None]
    past = place >= ends[:, None, :]
    age = place[..., 0] - jnp.max(jnp.where(past, ends[:, None, :], 0), axis=2)
    left = jnp.min(jnp.where(past, 1 << 20, ends[:, None, :]), axis=2) - 1 - place[..., 0]
    marks = jnp.stack([age, left] + [jnp.zeros_like(age)] * 6, axis=1).astype(F32)
    gain = ln_gain.reshape(1, dim)
    cb, gn, sk = conv_b.reshape(1, inner), gn_gain.reshape(1, inner), skip.reshape(1, inner)
    gate_t = gate_w.T

    r, c = jnp.arange(width)[:, None], jnp.arange(width)[None, :]
    on = r // 4 == c // 4
    on_map = on.astype(F32)
    to_lanes = (c == r % 4 * (width // 4) + r // 4).astype(BF)

    def spread(weight):
        mine = lax.dynamic_slice_in_dim(weight, h * (width // 4), width // 4, 0).reshape(width, 4)
        return jnp.where(on, jnp.tile(mine, (1, width // 4)), 0).astype(BF)

    wq, wk, wv = spread(w_q), spread(w_k), spread(w_v)
    consts = [sc, marks, gain, cb, gn, sk, gate_t, wq, wk, wv, on_map, to_lanes]
    xs[0], consts = together(xs[0], consts)
    sc, marks, gain, cb, gn, sk, gate_t, wq, wk, wv, on_map, to_lanes = consts
    x_halo = [halo_of(xs[0])]
    xs.append(gather(after(tokens[1], *xs[0])))
    sq_spec = whole((width, width))
    tiles = pltpu.VMEM((width // LANES, rows + EDGE, LANES), F32)
    dma = pltpu.SemaphoreType.DMA
    gate_specs = [head_cols(8, width, part * heads) for part in range(3)]
    conv_specs = [head_cols(4, width), head_cols(1, width)]
    anywhere = pl.BlockSpec(memory_space=pl.ANY)

    bf_span, f_span = ((micros, span, width), BF), ((micros, span, width), F32)
    block = whole((rows, width))
    big = whole((width, dim))
    lanes = (micros, 8, span)
    front = None
    for m in range(micros):
        args = [sc, *xs[m], x_halo[m], marks, gain, w_up, w_up, conv_w, cb, wq, wk, wv]
        args = args + [gate_t] * 3 + (list(front) if m else [])
        front = call(
            front_kernel,
            (hd,),
            [whole((rows, dim))] * 4
            + [
                whole((EDGE, dim)), micro_lanes(m, rows), whole((1, dim)),
                head_cols(dim, width), head_cols(dim, width, heads), *conv_specs,
            ]
            + [sq_spec] * 3
            + gate_specs
            + [anywhere] * (5 if m else 0),
            [
                micro_chunk(m, rows, dim), micro_chunk(m, rows, width),
                pl.BlockSpec((None, 5, rows, width), partial(lambda m, i, sc: (m, 0, i, 0), m)),
                of_micro(m, EDGE, width),
                micro_lanes(m, rows),
            ],
            [
                ((micros, span, dim), BF), f_span, ((micros, 5, span, width), BF),
                ((micros, EDGE, width), BF), (lanes, F32),
            ],
            [pltpu.VMEM((rows, dim), BF), tiles],
            11,
            args,
            {len(args) - 5 + at: at for at in range(5)} if m else None,
        )
        if m == 0:
            front, xs[1] = together(front, xs[1])
            x_halo.append(halo_of(xs[1]))
            cot = after(cotangent, *xs[1])
            c_parts = [cot, across(cot, 1), across(cot, 2)]
        else:
            front, c_parts = together(front, c_parts)
    normed, gz, five, halo, gate_terms = front
    gates = exchange([gate_terms] * hd)
    def of_five(at, count):
        return pl.BlockSpec((None, None, count, width), lambda i, sc: (i, at, 0, 0))

    lane_spec = of_micro(None, 8, span)
    state_spec = of_micro(None, width, width)
    gates, (c_x, c_y) = together(gates, c_parts[1:])
    c_parts = c_parts + [across(c_x[0], 2), across(c_y[1], 1)]
    state = call(
        partial(gates_kernel, seqs),
        (micros,),
        [pl.BlockSpec(memory_space=pltpu.SMEM)] * 2 + [lane_spec] * 4 + [of_five(1, span), of_five(2, span)],
        [lane_spec, state_spec],
        [(lanes, F32), ((micros, width, width), F32)],
        [],
        7,
        [sc, i_bias, f_bias, *gates, five, five],
    )
    state, c_parts = together(state, c_parts)
    rows_t, states = state
    states_in = lax.ppermute(states, "seq", [(0, 1)])

    *pairs, gd, gg, four, d_states, small_mix, sums = call(
        mix_kernel,
        (1,),
        [whole(lanes), whole((micros, width, width)), head_cols(1, width), head_cols(1, width)]
        + [anywhere] * 9,
        [anywhere] * 7 + [whole((micros, width, width)), whole((8, width)), whole(lanes)],
        [((2 * micros, rows, width), BF)] * 4
        + [((width, dim), BF)] * 2
        + [
            ((micros, 4, span, width), F32), ((micros, width, width), F32), ((8, width), F32),
            (lanes, F32),
        ],
        [
            pltpu.VMEM((micros, 4, span, width), BF),
            pltpu.VMEM((micros, span, width), F32),
            pltpu.VMEM((micros, span, dim), BF),
            pltpu.VMEM((micros, hd, rows, dim), BF),
            pltpu.VMEM((width, dim), BF),
            pltpu.VMEM((hd, 2 * micros, rows, width), BF),
            pltpu.VMEM((micros, 4, span, width), F32),
            pltpu.VMEM((width, dim), F32),
            pltpu.VMEM((width, dim), F32),
            pltpu.VMEM((2, width, dim), BF),
            pltpu.VMEM((rows, width), F32),
            pltpu.VMEM((hd // 2, rows, 2 * rows), BF),
            pltpu.VMEM((hd // 2, rows, 2 * rows), F32),
            pltpu.VMEM((rows, 2 * width), BF),
            pltpu.VMEM((span, 2 * width), BF),
            pltpu.VMEM((rows, 2 * width), BF),
            pltpu.VMEM((rows, width), F32),
            pltpu.VMEM((rows, width), BF),
            pltpu.VMEM((rows, width), BF),
            dma((micros, 6, 4)),
            dma((micros, 5, 4)),
        ],
        45,
        [sc, rows_t, states_in, gn, sk, five, gz, normed, *c_parts, w_down],
    )
    d_states = lax.ppermute(d_states, "seq", [(1, 0)])
    d_gates = call(
        gates_back_kernel,
        (micros,),
        [of_five(1, span), of_five(2, span), lane_spec, lane_spec, state_spec],
        [lane_spec],
        [(lanes, F32)],
        [],
        8,
        [sc, five, five, rows_t, sums, d_states],
    )[0]
    d_gates = exchange([d_gates] * hd)

    half_w, down_w = inner // every, inner // every
    early = [gg.reshape(ranks, half_w, dim), gd.reshape(ranks, down_w, dim)]
    early = lax.all_to_all(
        jnp.concatenate(early, axis=1), ("dp", "seq"), split_axis=0, concat_axis=0, tiled=True
    )
    pairs = exchange([after(part, *d_gates) for part in pairs])

    top = of_micro(None, EDGE, width)

    def of_four(at):
        return pl.BlockSpec((None, None, EDGE, width), lambda i, sc: (i, at, 0, 0))

    edges = call(
        edge_kernel,
        (micros,),
        [of_four(0), of_four(1)]
        + [of_micro(None, 8, 128)] * 4
        + [of_five(4, EDGE), top, of_micro(None, 8, 128), of_four(3)]
        + gate_specs[:2]
        + [sq_spec, sq_spec, *conv_specs],
        [top],
        [((micros, EDGE, width), F32)],
        [pltpu.VMEM((width // LANES, 2 * EDGE, LANES), F32)],
        4,
        [sc, four, four, *d_gates, five, halo, marks, four, gate_t, gate_t, wq, wk, conv_w, cb],
    )[0]
    edges = lax.ppermute(edges, "seq", [(1, 0)])
    axes = ("dp", "seq", "head")
    *d_inners, late = call(
        front_back_kernel,
        (1,),
        [whole(lanes)] * 6
        + [
            whole((micros, width, width)), whole((micros, EDGE, width)), whole((8, width)),
            whole((micros, EDGE, width)),
        ]
        + gate_specs
        + [sq_spec] * 3
        + conv_specs
        + [whole((1, dim))]
        + [anywhere] * 7,
        [anywhere] * 4 + [whole((width + SMALL // 2, dim))],
        [((micros, rows, width), BF)] * 4 + [((width + SMALL // 2, dim), F32)],
        [
            pltpu.VMEM((micros, 4, span, width), F32),
            pltpu.VMEM((micros, 5, span, width), BF),
            pltpu.VMEM((micros, span, dim), BF),
            pltpu.VMEM((micros, hd, EDGE, width), BF),
            pltpu.VMEM((dim, 2 * width), BF),
            pltpu.VMEM((micros, hd, rows, width), BF),
            tiles,
            tiles,
            pltpu.VMEM((rows, 6 * width), BF),
            *[pltpu.VMEM((width, width), F32)] * 3,
            pltpu.VMEM((rows, width), F32),
            pltpu.VMEM((width, dim), F32),
            pltpu.VMEM((width, width), F32),
            pltpu.VMEM((width, width), BF),
            pltpu.VMEM((width, dim), BF),
            pltpu.VMEM((SMALL, width), F32),
            dma((micros, 5, 4)),
            dma((micros, 4)),
        ],
        28,
        [
            sc, *d_gates, rows_t, marks, d_states, halo, small_mix, edges, gate_t, gate_t, gate_t,
            wq, wk, wv, conv_w, cb, gain, on_map, to_lanes, four, five, normed, gg, w_up,
        ],
    )
    (late, *d_inners), pairs = together([late, *d_inners], pairs)
    d_inners = exchange(d_inners)

    late = late + lax.ppermute(late, "seq", [(0, 1), (1, 0)])
    small = late[width:]
    blocks = late[:width].reshape(dp, 2 * half_w, dim)
    d = lax.axis_index("dp")
    if dp == 4:
        high = lax.reduce_precision(small, 8, 7)
        table = jnp.concatenate([high.astype(BF), (small - high).astype(BF)], axis=0)

        def to_plane(rel):
            block = lax.dynamic_index_in_dim(blocks, d ^ rel, 0, keepdims=False).astype(BF)
            block = jnp.concatenate([block, table], axis=0)
            if rel == 0:
                return block
            pairs_of = [(a * sq + 1, (a ^ rel) * sq + 1) for a in range(dp)]
            return lax.ppermute(block, ("dp", "seq"), pairs_of)

        terms = [to_plane(rel).astype(F32) for rel in range(dp)]
        terms = (terms[0] + terms[1]) + (terms[2] + terms[3])
        g_inner, small = terms[: 2 * half_w], terms[2 * half_w :]
        small = small[: SMALL // 2] + small[SMALL // 2 :]
        small = jnp.where(s == 1, small, lax.ppermute(small, "seq", [(1, 0)]))
    else:
        small = lax.psum(small, "dp")
        terms = lax.all_to_all(blocks.astype(BF), "dp", split_axis=0, concat_axis=0, tiled=True)
        g_inner = jnp.sum(terms.astype(F32), axis=0)
    early = jnp.sum(early.astype(F32), axis=0)
    g_gate, g_down = early[:half_w], early[half_w:]
    g_gate = jnp.concatenate([g_gate, lax.ppermute(g_gate, "seq", [(1, 0)])], axis=0)
    up_pairs, down_pairs = [], []
    for rank in range(ranks):
        for at in range(hd):
            block_at = at * dp + rank // 2 + (0 if rank % 2 else every // 2)
            up_pairs.append((rank * hd + at, block_at))
            down_pairs.append((rank * hd + at, at * ranks + rank))
    g_down = lax.ppermute(g_down, axes, down_pairs)
    g_up = jnp.where(s == 0, g_gate, g_inner)
    d_inners, (small, g_up) = together(d_inners, [small, g_up])
    g_up = lax.ppermute(g_up, axes, up_pairs).T

    token_spec = whole(tokens.shape)
    block_out, d_tokens = call(
        partial(tokens_kernel, seqs),
        (1,),
        [whole((1, dim))] + [anywhere] * 12,
        [token_spec] * 2,
        [(tokens.shape, BF)] * 2,
        [
            pltpu.VMEM(tokens.shape, BF),
            pltpu.VMEM(tokens.shape, BF),
            pltpu.VMEM((dim, 2 * inner), BF),
            pltpu.VMEM((inner, dim), BF),
            pltpu.VMEM((micros * rows, dim), F32),
            pltpu.VMEM((micros * rows, dim), F32),
            pltpu.VMEM((micros * rows, 2 * inner), BF),
            pltpu.VMEM((micros * rows, inner), BF),
            dma((10, hd)),
        ],
        10,
        [sc, gain, tokens, cotangent, *pairs, *d_inners, w_up, w_down],
    )

    (block_out, d_tokens), (small,) = together([block_out, d_tokens], [small])
    table = gather(small)
    flat = [((8, 3 * inner), F32), *[((4, 4, inner // 4), F32)] * 3, ((4, inner), F32)]
    flat = flat + [((inner,), F32)] * 3 + [((dim,), F32)] + [((heads,), F32)] * 2
    g_gate, g_wq, g_wk, g_wv, g_cw, g_cb, g_gn, g_sk, g_ln, g_ib, g_fb = call(
        table_kernel,
        (1,),
        [whole(small.shape)] * 4,
        [whole(shape) for shape, _ in flat],
        flat,
        [pltpu.VMEM((hd, SMALL, width), F32)],
        3,
        [sc, *table],
    )
    maps = [part.transpose(2, 0, 1) for part in (g_wq, g_wk, g_wv)]
    return (
        block_out, d_tokens, g_ln, g_up, g_cw, g_cb, *maps, g_gate.T, g_ib, g_fb, g_gn, g_sk, g_down,
    )


def solution(mesh):
    rows = P(None, ("dp", "seq", "head"), None)
    placed = (rows, P(None, "dp", None), *[P()] * 13, rows)
    outs = (rows, rows, P(), P(None, ("dp", "seq", "head")), *[P()] * 10, P(("dp", "seq", "head"), None))
    return jax.shard_map(per_device, mesh=mesh, in_specs=placed, out_specs=outs, check_vma=False)
```

time: 1410 us -> 249 us (0.18)
  waiting for transfers between devices: 529 us -> 45.4 us
  matrix products: 278 us -> 0 us
  local copies, waits for them, and re-layouts: 288 us -> 13.1 us
  other arithmetic: 185 us -> 9.46 us
  Pallas kernels: 0 us -> 125 us
  starting transfers between devices: 96.1 us -> 53.7 us
  between operations: 23.6 us -> 1.31 us
    dot_general x60 -> x0, matrix products: 278 us -> none  [the longest x18 65.1 us: block_mix(): mapped = jnp.einsum('tbi,bio->tbo', grouped, weight, precision=HIGH)]
    reduce_scatter x2 -> x0, waiting for transfers between devices: 257 us -> none  [the longest x1 141 us: per_device(): lax.psum_scatter(up_total, ('dp', 'seq', 'head'), scatter_dimension=1, ti...]
    psum x2 -> x0, waiting for transfers between devices: 235 us -> none  [per_device(): lax.psum((small_total[0], small_total[1], small_total[2], small_total[3],...]
    pallas_call x0 -> x9, Pallas kernels: none -> 125 us  [call(): pl.pallas_call(body, grid_spec=pltpu.PrefetchScalarGridSpec(num_scalar_pr...]
    reshape x42 -> x5, local copies, waits for them, and re-layouts: 83 us -> 2.46 us  [the longest x1 0.6 us: per_device(): conv_b.reshape(1, inner)]
    all_to_all x20 -> x1, starting transfers between devices: 84 us -> 5.68 us  [per_device(): lax.all_to_all(jnp.concatenate(early, axis=1), ('dp', 'seq'), split_axis=...]
    unnamed x471 -> x86, local copies, waits for them, and re-layouts: 67.4 us -> 6.11 us
    ppermute x4 -> x38, waiting for transfers between devices: 0.01 us -> 45.4 us  [the longest x25 26 us: across(): return lax.ppermute(value, 'head', [(at, at ^ rel) for at in range(hd)])]
  transfers between devices with their start and end apart: 32 -> 39, of which waited for: 11 -> 21; matrix products, arithmetic and copies ran while one was open for 36% -> 6% of each run, Pallas kernels for 0% -> 31%
where the time goes in v1:
time: 249 us; the launch traced here: 248 us
  Pallas kernels  125 us (50%)
  starting transfers between devices  53.7 us (22%)
  waiting for transfers between devices  45.4 us (18%)
  local copies, waits for them, and re-layouts  13.1 us (5%)
  other arithmetic  9.46 us (4%)
    pallas_call x9, Pallas kernels, call(): pl.pallas_call(body, grid_spec=pltpu.PrefetchScalarGridSpec(num_scalar_pr...  125 us
    ppermute x25, starting transfers between devices, across(): return lax.ppermute(value, 'head', [(at, at ^ rel) for at in range(hd)])  32.1 us
    ppermute x25, waiting for transfers between devices, across(): return lax.ppermute(value, 'head', [(at, at ^ rel) for at in range(hd)])  26 us
    ppermute x1, waiting for transfers between devices, per_device(): lax.ppermute(g_gate, 'seq', [(1, 0)])  9.27 us
    unnamed x86, local copies, waits for them, and re-layouts  6.11 us
    all_to_all x1, starting transfers between devices, per_device(): lax.all_to_all(jnp.concatenate(early, axis=1), ('dp', 'seq'), split_axis=...  5.68 us
  transfers between devices with their start and end apart: 39, of which 21 were waited for; matrix products, arithmetic and copies ran while one was open for 6% of the time, Pallas kernels for 31%

profile of v1, /device:TPU:0, one launch (start us, length us, event | category | flops | bytes accessed | tf_op | source)
XLA Modules:
  0.0 248.2 jit_solution(1437828037634341889)
XLA Ops:
  1.9 3.0 %collective-permute-start = (bf16[256,768]{1,0:T(8,128)(2,1)S(1)}, bf16[256,768]{1,0:T(8,128)(2,1)S(1)}, u32[]{:S(2)}, u32[]{:S(2)}) collective-permute-start(bf16[256,768]{1,0:T(8,128)(2,1)S(1)} %get-tuple-element.127.x0), channel_id=1, source_target_pairs={{0,1},{1,0},{2,3},{3,2},{4,5},{5,4},{6,7},{7,6},{8,9},{9,8},{10,11... | collective-permute-start | bytes 1179656 | tf_op jit(solution)/shard_map/ppermute | solution.py:776
  16.8 7.1 %collective-permute-done.1.x2 = bf16[256,768]{1,0:T(8,128)(2,1)S(1)} collective-permute-done((bf16[256,768]{1,0:T(8,128)(2,1)S(1)}, bf16[256,768]{1,0:T(8,128)(2,1)S(1)}, u32[]{:S(2)}, u32[]{:S(2)}) %collective-permute-start.1) | collective-permute-done | bytes 393248 | tf_op jit(solution)/shard_map/ppermute | solution.py:776
  30.3 10.6 %shard_map.271 = (bf16[2,1024,768]{2,1,0:T(8,128)(2,1)}, f32[2,1024,384]{2,1,0:T(8,128)}, bf16[2,5,1024,384]{3,2,1,0:T(8,128)(2,1)}, bf16[2,16,384]{2,1,0:T(8,128)(2,1)}, f32[2,8,1024]{2,1,0:T(8,128)}) custom-call(s32[10]{0:T(128)} %pad_add_fusion.sc, bf16[256,768]{1,0:T(8,128)(2,1)} %copy-done.6, bf16[256,768]{1,0:T(8,128)(2,1)} %copy-done.12, ...), custom_call_target="tpu_custom_call" | custom-call | flops 632499968 | bytes 1000000 | tf_op jit(solution)/shard_map/pallas_call | solution.py:730
  41.0 2.2 collective-permute-done.5.x2
  48.6 10.6 %shard_map.272 = (bf16[2,1024,768]{2,1,0:T(8,128)(2,1)}, f32[2,1024,384]{2,1,0:T(8,128)}, bf16[2,5,1024,384]{3,2,1,0:T(8,128)(2,1)}, bf16[2,16,384]{2,1,0:T(8,128)(2,1)}, f32[2,8,1024]{2,1,0:T(8,128)}) custom-call(s32[10]{0:T(128)} %pad_add_fusion.sc, ...), custom_call_target="tpu_custom_call", output_to_operand_aliasing={{0}: (18, {}), {1}: (19, {}), {2}: (20, {}), {3}: (21, {}),... | custom-call | flops 632499968 | bytes 1000000 | tf_op jit(solution)/shard_map/pallas_call | solution.py:730
  67.1 2.5 %collective-permute-done.12.g3 = f32[2,8,1024]{2,1,0:T(8,128)S(1)} collective-permute-done((f32[2,8,1024]{2,1,0:T(8,128)}, f32[2,8,1024]{2,1,0:T(8,128)S(1)}, u32[]{:S(2)}, u32[]{:S(2)}) %collective-permute-start.12) | collective-permute-done | bytes 65568 | tf_op jit(solution)/shard_map/ppermute | solution.py:776
  71.5 7.0 %shard_map.273 = (f32[2,8,1024]{2,1,0:T(8,128)}, f32[2,384,384]{2,1,0:T(8,128)}) custom-call(s32[10]{0:T(128)} %pad_add_fusion.sc, f32[4]{0:T(128)} %ib.1, f32[4]{0:T(128)} %fb.1, f32[2,8,1024]{2,1,0:T(8,128)} %get-tuple-element.162.g0, f32[2,8,1024]{2,1,0:T(8,128)} %copy-done.26, f32[2,8,1024]{2,1,0:T(8,128)} %copy-done.27, f32[2,8,1024]{2,1,0:T(8,128)} %copy-done.28, ...), custom_call_target="tpu_custom_call" | custom-call | flops 402500000 | bytes 1000000 | tf_op jit(solution)/shard_map/pallas_call | solution.py:730
  80.1 2.4 collective-permute-done.15.s_in
  83.6 48.9 %shard_map.274 = (bf16[4,256,384]{2,1,0:T(8,128)(2,1)}, bf16[4,256,384]{2,1,0:T(8,128)(2,1)}, bf16[4,256,384]{2,1,0:T(8,128)(2,1)}, bf16[4,256,384]{2,1,0:T(8,12...) custom-call(s32[10]{0:T(128)} %pad_add_fusion.sc, ...), custom_call_target="tpu_custom_call" | custom-call | flops 2587500032 | bytes 1000000 | tf_op jit(solution)/shard_map/pallas_call | solution.py:730
  133.8 2.3 pad_maximum_fusion
  136.2 5.7 %all-to-all-start = ((bf16[8,96,768]{2,1,0:T(8,128)(2,1)}), bf16[8,96,768]{2,1,0:T(8,128)(2,1)S(1)}, u32[]{:S(2)}, u32[]{:S(2)}) async-start(bf16[8,96,768]{2,1,0:T(8,128)(2,1)} %pad_maximum_fusion), calls=%async_computation | async-start | bytes 2359296 | tf_op jit(solution)/shard_map/all_to_all | solution.py:941
  142.9 6.4 %shard_map.275.d0 = f32[2,8,1024]{2,1,0:T(8,128)} custom-call(s32[10]{0:T(128)} %pad_add_fusion.sc, bf16[2,5,1024,384]{3,2,1,0:T(8,128)(2,1)} %get-tuple-element.158.k.v.five.inner, bf16[2,5,1024,384]{3,2,1,0:T(8,128)(2,1)} %get-tuple-element.158.k.v.five.inner, f32[2,8,1024]{2,1,0:T(8,128)} %get-tuple-element.171.rows.rows_t, ...), custom_call_target="tpu_custom_call" | custom-call | flops 460000000 | bytes 1000000 | tf_op jit(solution)/shard_map/pallas_call | solution.py:730
  154.7 2.4 collective-permute-done.19.d3
  160.6 3.8 %shard_map.276 = f32[2,16,384]{2,1,0:T(8,128)} custom-call(s32[10]{0:T(128)} %pad_add_fusion.sc, f32[2,4,1024,384]{3,2,1,0:T(8,128)} %get-tuple-element.186.dq.dk.skip_d.four, f32[2,4,1024,384]{3,2,1,0:T(8,128)} %get-tuple-element.186.dq.dk.skip_d.four, f32[2,8,1024]{2,1,0:T(8,128)} %shard_map.275.d0, f32[2,8,1024]{2,1,0:T(8,128)} %copy-done.22, ...), custom_call_target="tpu_custom_call" | custom-call | flops 230000000 | bytes 1000000 | tf_op jit(solution)/shard_map/pallas_call | solution.py:730
  165.7 2.0 collective-permute-done.20.edge
  168.4 24.6 %shard_map.277 = (bf16[2,256,384]{2,1,0:T(8,128)(2,1)}, bf16[2,256,384]{2,1,0:T(8,128)(2,1)}, bf16[2,256,384]{2,1,0:T(8,128)(2,1)}, bf16[2,256,384]{2,1,0:T(8,128)(2,1)}, f32[408,768]{1,0:T(8,128)}) custom-call(s32[10]{0:T(128)} %pad_add_fusion.sc, f32[2,8,1024]{2,1,0:T(8,128)} %shard_map.275.d0, f32[2,8,1024]{2,1,0:T(8,128)} %copy-done.22, ...), custom_call_target="tpu_custom_call" | custom-call | flops 1610000000 | bytes 1000000 | tf_op jit(solution)/shard_map/pallas_call | solution.py:730
  204.7 9.3 %collective-permute-done.32 = f32[48,768]{1,0:T(8,128)S(1)} collective-permute-done((f32[48,768]{1,0:T(8,128)S(1)}, f32[48,768]{1,0:T(8,128)S(1)}, u32[]{:S(2)}, u32[]{:S(2)}) %collective-permute-start.32) | collective-permute-done | bytes 147488 | tf_op jit(solution)/shard_map/ppermute | solution.py:1038
  214.0 2.7 %collective-permute-done.31 = f32[24,768]{1,0:T(8,128)S(1)} collective-permute-done((f32[24,768]{1,0:T(8,128)S(1)}, f32[24,768]{1,0:T(8,128)S(1)}, u32[]{:S(2)}, u32[]{:S(2)}) %collective-permute-start.31) | collective-permute-done | bytes 73760 | tf_op jit(solution)/shard_map/ppermute | solution.py:1031
  216.7 3.8 %collective-permute-start.36 = (f32[96,768]{1,0:T(8,128)S(1)}, f32[96,768]{1,0:T(8,128)S(1)}, u32[]{:S(2)}, u32[]{:S(2)}) collective-permute-start(f32[96,768]{1,0:T(8,128)S(1)} %slice_select_fusion), channel_id=1, source_target_pairs={{0,16},{1,20},{2,24},{3,28},{4,0},{5,4},{6,8},{7,12},{8,17},{9,21}... | collective-permute-start | bytes 884744 | tf_op jit(solution)/shard_map/ppermute | solution.py:1048
  221.2 10.8 %shard_map.278 = (bf16[2,256,768]{2,1,0:T(8,128)(2,1)}, bf16[2,256,768]{2,1,0:T(8,128)(2,1)}) custom-call(s32[10]{0:T(128)} %pad_add_fusion.sc, f32[1,768]{1,0:T(1,128)} %reshape.229.gain, bf16[2,256,768]{2,1,0:T(8,128)(2,1)} %rest_0_.1, bf16[2,256,768]{2,1,0:T(8,128)(2,1)} %rest_1_.1, bf16[4,256,384]{2,1,0:T(8,128)(2,1)} %get-tuple-element.203.rest_2_, ...), custom_call_target="tpu_custom_call" | custom-call | flops 575000000 | bytes 1000000 | tf_op jit(solution)/shard_map/pallas_call | solution.py:730
  232.1 3.5 %collective-permute-start.33 = (f32[24,768]{1,0:T(8,128)S(1)}, f32[24,768]{1,0:T(8,128)S(1)}, u32[]{:S(2)}, u32[]{:S(2)}) collective-permute-start(f32[24,768]{1,0:T(8,128)S(1)} %broadcast_select_fusion.t0), channel_id=1, source_target_pairs={{0,1},{1,0},{2,3},{3,2},{4,5},{5,4},{6,7},{7,6},{8,9},{9,8},{10,11... | collective-permute-start | bytes 221192 | tf_op jit(solution)/shard_map/ppermute | solution.py:776
  235.6 2.9 %collective-permute-start.34 = (f32[24,768]{1,0:T(8,128)S(1)}, f32[24,768]{1,0:T(8,128)S(1)}, u32[]{:S(2)}, u32[]{:S(2)}) collective-permute-start(f32[24,768]{1,0:T(8,128)S(1)} %broadcast_select_fusion.t0), channel_id=1, source_target_pairs={{0,2},{1,3},{2,0},{3,1},{4,6},{5,7},{6,4},{7,5},{8,10},{9,11},{10,... | collective-permute-start | bytes 221192 | tf_op jit(solution)/shard_map/ppermute | solution.py:776
  241.6 2.1 collective-permute-done.35.t3
  244.4 2.4 shard_map.279
  (203 shorter events, 67.6 us)
Async XLA Ops:
  1.9 14.9 %collective-permute-start = (bf16[256,768]{1,0:T(8,128)(2,1)S(1)}, bf16[256,768]{1,0:T(8,128)(2,1)S(1)}, u32[]{:S(2)}, u32[]{:S(2)}) collective-permute-start(bf16[256,768]{1,0:T(8,128)(2,1)S(1)} %get-tuple-element.127.x0), channel_id=1, source_target_pairs={{0,1},{1,0},{2,3},{3,2},{4,5},{5,4},{6,7},{7,6},{8,9},{9,8},{10,11... | collective-permute-start | bytes 1179656 | tf_op jit(solution)/shard_map/ppermute | solution.py:776
  4.9 19.0 %collective-permute-start.1 = (bf16[256,768]{1,0:T(8,128)(2,1)S(1)}, bf16[256,768]{1,0:T(8,128)(2,1)S(1)}, u32[]{:S(2)}, u32[]{:S(2)}) collective-permute-start(bf16[256,768]{1,0:T(8,128)(2,1)S(1)} %get-tuple-element.127.x0), channel_id=1, source_target_pairs={{0,2},{1,3},{2,0},{3,1},{4,6},{5,7},{6,4},{7,5},{8,10},{9,11},{10,... | collective-permute-start | bytes 1179656 | tf_op jit(solution)/shard_map/ppermute | solution.py:776
  6.4 17.5 %collective-permute-start.2 = (bf16[256,768]{1,0:T(8,128)(2,1)S(1)}, bf16[256,768]{1,0:T(8,128)(2,1)S(1)}, u32[]{:S(2)}, u32[]{:S(2)}) collective-permute-start(bf16[256,768]{1,0:T(8,128)(2,1)S(1)} %get-tuple-element.127.x0), channel_id=1, source_target_pairs={{0,3},{1,2},{2,1},{3,0},{4,7},{5,6},{6,5},{7,4},{8,11},{9,10},{10,... | collective-permute-start | bytes 1179656 | tf_op jit(solution)/shard_map/ppermute | solution.py:776
  23.9 17.1 %collective-permute-start.4 = (bf16[256,768]{1,0:T(8,128)(2,1)S(1)}, bf16[256,768]{1,0:T(8,128)(2,1)S(1)}, u32[]{:S(2)}, u32[]{:S(2)}) collective-permute-start(bf16[256,768]{1,0:T(8,128)(2,1)S(1)} %get-tuple-element.143.x0), channel_id=1, source_target_pairs={{0,1},{1,0},{2,3},{3,2},{4,5},{5,4},{6,7},{7,6},{8,9},{9,8},{10,11... | collective-permute-start | bytes 1179656 | tf_op jit(solution)/shard_map/ppermute | solution.py:776
  25.1 18.1 %collective-permute-start.5 = (bf16[256,768]{1,0:T(8,128)(2,1)S(1)}, bf16[256,768]{1,0:T(8,128)(2,1)S(1)}, u32[]{:S(2)}, u32[]{:S(2)}) collective-permute-start(bf16[256,768]{1,0:T(8,128)(2,1)S(1)} %get-tuple-element.143.x0), channel_id=1, source_target_pairs={{0,2},{1,3},{2,0},{3,1},{4,6},{5,7},{6,4},{7,5},{8,10},{9,11},{10,... | collective-permute-start | bytes 1179656 | tf_op jit(solution)/shard_map/ppermute | solution.py:776
  26.0 17.2 %collective-permute-start.6 = (bf16[256,768]{1,0:T(8,128)(2,1)S(1)}, bf16[256,768]{1,0:T(8,128)(2,1)}, u32[]{:S(2)}, u32[]{:S(2)}) collective-permute-start(bf16[256,768]{1,0:T(8,128)(2,1)S(1)} %get-tuple-element.143.x0), channel_id=1, source_target_pairs={{0,3},{1,2},{2,1},{3,0},{4,7},{5,6},{6,5},{7,4},{8,11},{9,10},{10,... | collective-permute-start | bytes 1179656 | tf_op jit(solution)/shard_map/ppermute | solution.py:776
  43.3 17.7 %collective-permute-start.8 = (bf16[2,256,768]{2,1,0:T(8,128)(2,1)S(1)}, bf16[2,256,768]{2,1,0:T(8,128)(2,1)S(1)}, u32[]{:S(2)}, u32[]{:S(2)}) collective-permute-start(bf16[2,256,768]{2,1,0:T(8,128)(2,1)S(1)} %copy-done.3), channel_id=1, source_target_pairs={{0,1},{1,0},{2,3},{3,2},{4,5},{5,4},{6,7},{7,6},{8,9},{9,8},{10,11... | collective-permute-start | bytes 2359304 | tf_op jit(solution)/shard_map/ppermute | solution.py:776
  43.9 17.9 %collective-permute-start.9 = (bf16[2,256,768]{2,1,0:T(8,128)(2,1)S(1)}, bf16[2,256,768]{2,1,0:T(8,128)(2,1)S(1)}, u32[]{:S(2)}, u32[]{:S(2)}) collective-permute-start(bf16[2,256,768]{2,1,0:T(8,128)(2,1)S(1)} %copy-done.3), channel_id=1, source_target_pairs={{0,2},{1,3},{2,0},{3,1},{4,6},{5,7},{6,4},{7,5},{8,10},{9,11},{10,... | collective-permute-start | bytes 2359304 | tf_op jit(solution)/shard_map/ppermute | solution.py:776
  69.7 8.8 %collective-permute-start.13 = (bf16[256,768]{1,0:T(8,128)(2,1)S(1)}, bf16[256,768]{1,0:T(8,128)(2,1)S(1)}, u32[]{:S(2)}, u32[]{:S(2)}) collective-permute-start(bf16[256,768]{1,0:T(8,128)(2,1)S(1)} %slice_bitcast_fusion.1), channel_id=1, source_target_pairs={{0,2},{1,3},{2,0},{3,1},{4,6},{5,7},{6,4},{7,5},{8,10},{9,11},{10,... | collective-permute-start | bytes 1179656 | tf_op jit(solution)/shard_map/ppermute | solution.py:776
  70.3 8.2 %collective-permute-start.14 = (bf16[256,768]{1,0:T(8,128)(2,1)S(1)}, bf16[256,768]{1,0:T(8,128)(2,1)S(1)}, u32[]{:S(2)}, u32[]{:S(2)}) collective-permute-start(bf16[256,768]{1,0:T(8,128)(2,1)S(1)} %slice_bitcast_fusion), channel_id=1, source_target_pairs={{0,1},{1,0},{2,3},{3,2},{4,5},{5,4},{6,7},{7,6},{8,9},{9,8},{10,11... | collective-permute-start | bytes 1179656 | tf_op jit(solution)/shard_map/ppermute | solution.py:776
  132.5 9.3 %collective-permute-start.16 = (f32[2,384,384]{2,1,0:T(8,128)}, f32[2,384,384]{2,1,0:T(8,128)S(1)}, u32[]{:S(2)}, u32[]{:S(2)}) collective-permute-start(f32[2,384,384]{2,1,0:T(8,128)} %get-tuple-element.183), channel_id=1, source_target_pairs={{4,0},{5,1},{6,2},{7,3},{12,8},{13,9},{14,10},{15,11},{20,16},{21,... | collective-permute-start | bytes 3538952 | tf_op jit(solution)/shard_map/ppermute | solution.py:926
  136.2 58.9 %all-to-all-start = ((bf16[8,96,768]{2,1,0:T(8,128)(2,1)}), bf16[8,96,768]{2,1,0:T(8,128)(2,1)S(1)}, u32[]{:S(2)}, u32[]{:S(2)}) async-start(bf16[8,96,768]{2,1,0:T(8,128)(2,1)} %pad_maximum_fusion), calls=%async_computation | async-start | bytes 2359296 | tf_op jit(solution)/shard_map/all_to_all | solution.py:941
  157.1 35.9 %collective-permute-start.23 = (bf16[4,256,384]{2,1,0:T(8,128)(2,1)}, bf16[4,256,384]{2,1,0:T(8,128)(2,1)S(1)}, u32[]{:S(2)}, u32[]{:S(2)}) collective-permute-start(bf16[4,256,384]{2,1,0:T(8,128)(2,1)} %get-tuple-element.202), channel_id=1, source_target_pairs={{0,3},{1,2},{2,1},{3,0},{4,7},{5,6},{6,5},{7,4},{8,11},{9,10},{10,... | collective-permute-start | bytes 2359304 | tf_op jit(solution)/shard_map/ppermute | solution.py:776
  158.2 35.0 %collective-permute-start.22 = (bf16[4,256,384]{2,1,0:T(8,128)(2,1)}, bf16[4,256,384]{2,1,0:T(8,128)(2,1)S(1)}, u32[]{:S(2)}, u32[]{:S(2)}) collective-permute-start(bf16[4,256,384]{2,1,0:T(8,128)(2,1)} %get-tuple-element.200), channel_id=1, source_target_pairs={{0,2},{1,3},{2,0},{3,1},{4,6},{5,7},{6,4},{7,5},{8,10},{9,11},{10,... | collective-permute-start | bytes 2359304 | tf_op jit(solution)/shard_map/ppermute | solution.py:776
  159.3 33.9 %collective-permute-start.21 = (bf16[4,256,384]{2,1,0:T(8,128)(2,1)S(1)}, bf16[4,256,384]{2,1,0:T(8,128)(2,1)}, u32[]{:S(2)}, u32[]{:S(2)}) collective-permute-start(bf16[4,256,384]{2,1,0:T(8,128)(2,1)S(1)} %copy-done.37), channel_id=1, source_target_pairs={{0,1},{1,0},{2,3},{3,2},{4,5},{5,4},{6,7},{7,6},{8,9},{9,8},{10,11... | collective-permute-start | bytes 2359304 | tf_op jit(solution)/shard_map/ppermute | solution.py:776
  193.2 23.4 %collective-permute-start.24 = (bf16[2,256,384]{2,1,0:T(8,128)(2,1)}, bf16[2,256,384]{2,1,0:T(8,128)(2,1)S(1)}, u32[]{:S(2)}, u32[]{:S(2)}) collective-permute-start(bf16[2,256,384]{2,1,0:T(8,128)(2,1)} %get-tuple-element.208), channel_id=1, source_target_pairs={{0,1},{1,0},{2,3},{3,2},{4,5},{5,4},{6,7},{7,6},{8,9},{9,8},{10,11... | collective-permute-start | bytes 1179656 | tf_op jit(solution)/shard_map/ppermute | solution.py:776
  194.1 22.6 %collective-permute-start.25 = (bf16[2,256,384]{2,1,0:T(8,128)(2,1)}, bf16[2,256,384]{2,1,0:T(8,128)(2,1)S(1)}, u32[]{:S(2)}, u32[]{:S(2)}) collective-permute-start(bf16[2,256,384]{2,1,0:T(8,128)(2,1)} %get-tuple-element.209), channel_id=1, source_target_pairs={{0,2},{1,3},{2,0},{3,1},{4,6},{5,7},{6,4},{7,5},{8,10},{9,11},{10,... | collective-permute-start | bytes 1179656 | tf_op jit(solution)/shard_map/ppermute | solution.py:776
  200.3 16.4 %collective-permute-start.26 = (bf16[2,256,384]{2,1,0:T(8,128)(2,1)S(1)}, bf16[2,256,384]{2,1,0:T(8,128)(2,1)S(1)}, u32[]{:S(2)}, u32[]{:S(2)}) collective-permute-start(bf16[2,256,384]{2,1,0:T(8,128)(2,1)S(1)} %copy-done.38), channel_id=1, source_target_pairs={{0,3},{1,2},{2,1},{3,0},{4,7},{5,6},{6,5},{7,4},{8,11},{9,10},{10,... | collective-permute-start | bytes 1179656 | tf_op jit(solution)/shard_map/ppermute | solution.py:776
  201.9 12.0 %collective-permute-start.32 = (f32[48,768]{1,0:T(8,128)S(1)}, f32[48,768]{1,0:T(8,128)S(1)}, u32[]{:S(2)}, u32[]{:S(2)}) collective-permute-start(f32[48,768]{1,0:T(8,128)S(1)} %get-tuple-element.246), channel_id=1, source_target_pairs={{4,0},{5,1},{6,2},{7,3},{12,8},{13,9},{14,10},{15,11},{20,16},{21,... | collective-permute-start | bytes 442376 | tf_op jit(solution)/shard_map/ppermute | solution.py:1038
  203.4 13.3 %collective-permute-start.31 = (f32[24,768]{1,0:T(8,128)S(1)}, f32[24,768]{1,0:T(8,128)S(1)}, u32[]{:S(2)}, u32[]{:S(2)}) collective-permute-start(f32[24,768]{1,0:T(8,128)S(1)} %slice_add_fusion), channel_id=1, source_target_pairs={{4,0},{5,1},{6,2},{7,3},{12,8},{13,9},{14,10},{15,11},{20,16},{21,... | collective-permute-start | bytes 221192 | tf_op jit(solution)/shard_map/ppermute | solution.py:1031
  216.7 30.1 %collective-permute-start.36 = (f32[96,768]{1,0:T(8,128)S(1)}, f32[96,768]{1,0:T(8,128)S(1)}, u32[]{:S(2)}, u32[]{:S(2)}) collective-permute-start(f32[96,768]{1,0:T(8,128)S(1)} %slice_select_fusion), channel_id=1, source_target_pairs={{0,16},{1,20},{2,24},{3,28},{4,0},{5,4},{6,8},{7,12},{8,17},{9,21}... | collective-permute-start | bytes 884744 | tf_op jit(solution)/shard_map/ppermute | solution.py:1048
  220.5 18.0 %collective-permute-start.37 = (f32[48,768]{1,0:T(8,128)S(1)}, f32[48,768]{1,0:T(8,128)S(1)}, u32[]{:S(2)}, u32[]{:S(2)}) collective-permute-start(f32[48,768]{1,0:T(8,128)S(1)} %get-tuple-element.245), channel_id=1, source_target_pairs={{0,0},{1,8},{2,16},{3,24},{4,1},{5,9},{6,17},{7,25},{8,2},{9,10},{... | collective-permute-start | bytes 442376 | tf_op jit(solution)/shard_map/ppermute | solution.py:1045
  232.1 8.3 %collective-permute-start.33 = (f32[24,768]{1,0:T(8,128)S(1)}, f32[24,768]{1,0:T(8,128)S(1)}, u32[]{:S(2)}, u32[]{:S(2)}) collective-permute-start(f32[24,768]{1,0:T(8,128)S(1)} %broadcast_select_fusion.t0), channel_id=1, source_target_pairs={{0,1},{1,0},{2,3},{3,2},{4,5},{5,4},{6,7},{7,6},{8,9},{9,8},{10,11... | collective-permute-start | bytes 221192 | tf_op jit(solution)/shard_map/ppermute | solution.py:776
  235.6 6.0 %collective-permute-start.34 = (f32[24,768]{1,0:T(8,128)S(1)}, f32[24,768]{1,0:T(8,128)S(1)}, u32[]{:S(2)}, u32[]{:S(2)}) collective-permute-start(f32[24,768]{1,0:T(8,128)S(1)} %broadcast_select_fusion.t0), channel_id=1, source_target_pairs={{0,2},{1,3},{2,0},{3,1},{4,6},{5,7},{6,4},{7,5},{8,10},{9,11},{10,... | collective-permute-start | bytes 221192 | tf_op jit(solution)/shard_map/ppermute | solution.py:776
  (57 other events, 371.6 us)

commit v2 on v1

--- a/solution.py
+++ b/solution.py
@@ -14,7 +14,7 @@
 EDGE = 16
 SMALL = 48
 NEVER = -1e30
-VMEM_BYTES = 60 * 1024 * 1024
+VMEM_BYTES = 52 * 1024 * 1024
 
 
 def mm(a, b):
@@ -111,12 +111,13 @@
 
 
 def front_kernel(
-    sc, x0, x1, x2, x3, xh, marks, gain, w_in, w_gt, cw, cb, wq, wk, wv, gq, gk, gv, *rest
+    sc, x0, x1, x2, x3a, x3b, xh, marks, gain, w_in, w_gt, cw, cb, wq, wk, wv, gq, gk, gv, *rest
 ):
     normed_o, gz_o, five_o, halo_o, gt_o, xs, ext = rest[-7:]
-    i = pl.program_id(0)
+    m, i = pl.program_id(0) // 4, pl.program_id(0) % 4
     chunk = xs.shape[0]
-    pick((x0, x1, x2, x3), i ^ sc[0], xs, slice(0, chunk))
+    rel = i ^ sc[0]
+    pick((x0, x1, x2, x3a, x3b), jnp.where((rel == 3) & (m == 1), 4, rel), xs, slice(0, chunk))
 
     def norm(rows):
         stream = rows.astype(F32)
@@ -157,7 +158,7 @@
     h, s = sc[0], sc[1]
     span, width = k.shape
     factor = width ** (-0.5)
-    lin = (g0[...] + g1[...] + g2[...] + g3[...]).astype(BF).astype(F32)
+    lin = ((g0[...] + g1[m]) + (g2[m] + g3[m])).astype(BF).astype(F32)
     r = iota(lin.shape, 0)
     ig = jnp.sum(jnp.where(r == 2 * h, lin, 0.0), axis=0, keepdims=True) + ib[h]
     fg = jnp.sum(jnp.where(r == 2 * h + 1, lin, 0.0), axis=0, keepdims=True) + fb[h]
@@ -184,9 +185,9 @@
 def mix_kernel(
     sc, rows, s_in, gn, sk, five, gz, normed, c0, c1, c2, c3a, c3b, w_dn, *rest
 ):
-    p0, p1, p2, p3, gd_o, gg_o, four_o, ds_o, small_o, sums_o = rest[:10]
-    fb, zb, nb, cb, wb, pb, four, gd, gg, go, acc, a_high, decays = rest[10:23]
-    q2, v2, dh2, dbr, brs, dgs, in_sems, out_sems = rest[23:]
+    p0, p1, p2, p3, gd_o, gg_o, both_o, four_o, ds_o, small_o, sums_o = rest[:11]
+    fb, zb, nb, cb, wb, pb, four, gd, gg, go, acc, a_high, decays = rest[11:24]
+    q2, v2, dh2, dbr, brs, dgs, in_sems, out_sems, pack_sems = rest[24:]
     h = sc[0]
     micros, _, span, width = fb.shape
     chunk = acc.shape[0]
@@ -249,6 +250,14 @@
         pltpu.make_async_copy(go.at[0], gd_o, out_sems.at[0, 4, 0]),
         pltpu.make_async_copy(go.at[1], gg_o, out_sems.at[0, 4, 1]),
     ]
+    ranks, piece = both_o.shape[0], both_o.shape[1] // 2
+    if piece % EDGE == 0:
+        grads_out = grads_out[1:]
+        for r in range(ranks):
+            for at, which in enumerate((1, 0)):
+                to = both_o.at[r, pl.ds(at * piece, piece)]
+                rows_r = go.at[which, pl.ds(r * piece, piece)]
+                grads_out.append(pltpu.make_async_copy(rows_r, to, pack_sems.at[at, r]))
 
     def one(at_step, none):
         m, i = at_step // 4, at_step % 4
@@ -275,36 +284,39 @@
             v2[at, 0:width] = fb[m, 2, at, :]
             v2[at, width:] = fb[m, 2, at, :]
 
-        acc[...] = jnp.zeros_like(acc)
+        @pl.when(at_step == 0)
+        def _():
+            weight_in.wait()
+
+        for copy in chunk_in(m, i):
+            copy.wait()
+        cot_in(m, 0, i).wait()
         here = start + iota((chunk, 1), 0)
         cols = jnp.transpose(rows[m, :, own])
         cum, seg, carried, valid = cols[:, 0:1], cols[:, 2:3], cols[:, 4:5], cols[:, 6:7]
 
-        def attend(j, none):
-            at = rows_of(j, two)
+        def attend(j):
+            at = slice(j * two, (j + 1) * two)
             scores = nt(fb[m, 0, own, :], fb[m, 1, at, :]) * factor
             allowed = (seg == rows[m, 2:3, at]) & (j * two + iota((1, two), 1) <= here)
             decay = jnp.exp(jnp.where(allowed, cum + rows[m, 1:2, at], NEVER))
             decays[j] = decay
             high, low = split(scores * decay)
             a_high[j] = high
-            acc[...] += mm(high, fb[m, 2, at, :]) + mm(low, fb[m, 2, at, :])
-            return none
-
-        lax.fori_loop(0, i // 2 + 1, attend, 0)
+            return mm(high, fb[m, 2, at, :]) + mm(low, fb[m, 2, at, :])
+
         q2[:, 0:width] = fb[m, 0, own, :]
         q2[:, width:] = fb[m, 0, own, :]
-        acc[...] += carried * mm(q2[...], jnp.concatenate(split(s_in[m]), axis=0))
-
-        @pl.when(at_step == 0)
-        def _():
-            weight_in.wait()
-
-        for copy in chunk_in(m, i):
-            copy.wait()
-        cot_in(m, 0, i).wait()
+        state = jnp.concatenate(split(s_in[m]), axis=0)
+        acc[...] = attend(0) + carried * mm(q2[...], state)
+
         cb[m, i] = (cb[m, i].astype(F32) * valid).astype(BF)
         dbr[...] = nt(cb[m, i], wb[...])
+
+        @pl.when(i >= 2)
+        def _():
+            acc[...] += attend(1)
+
         step = 32
         sum_gn, sum_sk = jnp.zeros((8, width), F32), jnp.zeros((8, width), F32)
         for r in range(0, chunk, step):
@@ -340,6 +352,15 @@
         gg[...] += tn(dgs[...], nb[m, own, :])
         ds_o[m] += tn(fb[m, 0, own, :], q2[:, width:])
         acc[...] = carried * nt(dh2[:, 0:width], s_in[m].astype(BF))
+        def attend_back(j):
+            at = slice(j * two, (j + 1) * two)
+            d_att = nt(dh2[...], v2[at, :])
+            four[m, 2, at, :] += tn(a_high[j], dh2[:, 0:width])
+            w_high, w_low = split(decays[j] * d_att * factor)
+            four[m, 1, at, :] += tn(w_high, fb[m, 0, own, :]) + tn(w_low, fb[m, 0, own, :])
+            return mm(w_high, fb[m, 1, at, :]) + mm(w_low, fb[m, 1, at, :])
+
+        acc[...] += attend_back(0)
         for rel in range(4):
 
             @pl.when((i ^ h) == rel)
@@ -353,21 +374,18 @@
             for copy in grads_out:
                 copy.start()
 
-        def attend_back(j, none):
-            at = rows_of(j, two)
-            d_att = nt(dh2[...], v2[at, :])
-            four[m, 2, at, :] += tn(a_high[j], dh2[:, 0:width])
-            w_high, w_low = split(decays[j] * d_att * factor)
-            acc[...] += mm(w_high, fb[m, 1, at, :]) + mm(w_low, fb[m, 1, at, :])
-            four[m, 1, at, :] += tn(w_high, fb[m, 0, own, :]) + tn(w_low, fb[m, 0, own, :])
-
-            @pl.when(i == 3)
-            def _():
-                key_out(m, j).start()
-
-            return none
-
-        lax.fori_loop(0, i // 2 + 1, attend_back, 0)
+        @pl.when(i == 3)
+        def _():
+            key_out(m, 0).start()
+
+        @pl.when(i >= 2)
+        def _():
+            acc[...] += attend_back(1)
+
+        @pl.when(i == 3)
+        def _():
+            key_out(m, 1).start()
+
         four[m, 0, own, :] = acc[...]
         for copy in rows_out(m, i):
             copy.start()
@@ -399,7 +417,7 @@
 def gates_back_kernel(sc, k, v, rows, sums, ds_out, dg_o):
     h, s = sc[0], sc[1]
     span = k.shape[0]
-    turned = nt(twice(v[...], 1), jnp.concatenate(split(ds_out[...]), axis=1))
+    turned = nt(twice(v[...], 1), jnp.concatenate(split(ds_out[pl.program_id(0)]), axis=1))
     cross = rows[5:6, :] * lane_sums(turned * k[...].astype(F32))
     r = iota((8, span), 0)
     d_ig = sums[0:1, :] + cross[0:1, :]
@@ -424,7 +442,9 @@
 ):
     to_tiles(ext, 0, halo[...].astype(F32))
     to_tiles(ext, EDGE, inner[...].astype(F32))
-    g_all = jnp.concatenate(split(d0[...] + d1[...] + d2[...] + d3[...]), axis=0)
+    m, at = pl.program_id(0), slice(0, 128)
+    total = (d0[m, :, at] + d1[m, :, at]) + (d2[m, :, at] + d3[m, :, at])
+    g_all = jnp.concatenate(split(total), axis=0)
     dq_h, dq_l = split(dq[...] + tn(g_all, twice(gq[...]))[0:EDGE, :])
     dk_h, dk_l = split(dk[...] + tn(g_all, twice(gk[...]))[0:EDGE, :])
     d_act = skip_d[...] + nt(dq_h, wq[...]) + nt(dq_l, wq[...]) + nt(dk_h, wk[...]) + nt(dk_l, wk[...])
@@ -550,14 +570,14 @@
                     later = jnp.where(left >= lag, nxt[t, r + lag : r + lag + 64, :], 0.0)
                     total = total + cw[3 - lag : 4 - lag, lanes] * later
                 ib[m, i, r : r + 64, lanes] = total.astype(BF)
+        gi[...] += tn(ib[m, i], nb[m, own, :])
+        nxt[:, chunk : chunk + EDGE, :] = nxt[:, 0:EDGE, :]
         for rel in range(4):
 
             @pl.when((i ^ h) == rel)
             def _(rel=rel):
                 inner_out(m, rel, i).start()
 
-        gi[...] += tn(ib[m, i], nb[m, own, :])
-        nxt[:, chunk : chunk + EDGE, :] = nxt[:, 0:EDGE, :]
         return none
 
     lax.fori_loop(0, 4 * micros, one, 0)
@@ -781,14 +801,7 @@
     def gather(value):
         return exchange([value] * hd)
 
-    def halo_of(parts):
-        ends_of = [part[rows - EDGE :] for part in parts]
-        last_rows = ends_of[0]
-        for rel in range(1, hd):
-            last_rows = jnp.where(h == (hd - 1) ^ rel, ends_of[rel], last_rows)
-        return lax.ppermute(last_rows, "seq", [(0, 1)])
-
-    xs = [gather(tokens[0])]
+    x_near = [across(tokens, 1), across(tokens, 2)]
 
     place = s * span + jnp.arange(span, dtype=jnp.int32)[None, :, None]
     past = place >= ends[:, None, :]
@@ -810,58 +823,67 @@
 
     wq, wk, wv = spread(w_q), spread(w_k), spread(w_v)
     consts = [sc, marks, gain, cb, gn, sk, gate_t, wq, wk, wv, on_map, to_lanes]
-    xs[0], consts = together(xs[0], consts)
+    x_near, consts = together(x_near, consts)
     sc, marks, gain, cb, gn, sk, gate_t, wq, wk, wv, on_map, to_lanes = consts
-    x_halo = [halo_of(xs[0])]
-    xs.append(gather(after(tokens[1], *xs[0])))
+    x_far = [across(x_near[0][0], 2), across(x_near[1][1], 1)]
+    x_parts, x_far = together([tokens, *x_near], x_far)
+    tails = [part[:, rows - EDGE :] for part in x_parts]
+    tails.append(jnp.stack([part[rows - EDGE :] for part in x_far]))
+    tail = tails[0]
+    for rel in range(1, hd):
+        tail = jnp.where(h == (hd - 1) ^ rel, tails[rel], tail)
+    x_halo = lax.ppermute(tail, "seq", [(0, 1)])
+    cot = after(cotangent, *x_far)
+    c_parts = [cot, across(cot, 1), across(cot, 2)]
+
     sq_spec = whole((width, width))
     tiles = pltpu.VMEM((width // LANES, rows + EDGE, LANES), F32)
     dma = pltpu.SemaphoreType.DMA
     gate_specs = [head_cols(8, width, part * heads) for part in range(3)]
     conv_specs = [head_cols(4, width), head_cols(1, width)]
     anywhere = pl.BlockSpec(memory_space=pl.ANY)
+    held = pl.BlockSpec(memory_space=pltpu.VMEM)
 
     bf_span, f_span = ((micros, span, width), BF), ((micros, span, width), F32)
     block = whole((rows, width))
     big = whole((width, dim))
     lanes = (micros, 8, span)
-    front = None
-    for m in range(micros):
-        args = [sc, *xs[m], x_halo[m], marks, gain, w_up, w_up, conv_w, cb, wq, wk, wv]
-        args = args + [gate_t] * 3 + (list(front) if m else [])
-        front = call(
-            front_kernel,
-            (hd,),
-            [whole((rows, dim))] * 4
-            + [
-                whole((EDGE, dim)), micro_lanes(m, rows), whole((1, dim)),
-                head_cols(dim, width), head_cols(dim, width, heads), *conv_specs,
-            ]
-            + [sq_spec] * 3
-            + gate_specs
-            + [anywhere] * (5 if m else 0),
-            [
-                micro_chunk(m, rows, dim), micro_chunk(m, rows, width),
-                pl.BlockSpec((None, 5, rows, width), partial(lambda m, i, sc: (m, 0, i, 0), m)),
-                of_micro(m, EDGE, width),
-                micro_lanes(m, rows),
-            ],
-            [
-                ((micros, span, dim), BF), f_span, ((micros, 5, span, width), BF),
-                ((micros, EDGE, width), BF), (lanes, F32),
-            ],
-            [pltpu.VMEM((rows, dim), BF), tiles],
-            11,
-            args,
-            {len(args) - 5 + at: at for at in range(5)} if m else None,
-        )
-        if m == 0:
-            front, xs[1] = together(front, xs[1])
-            x_halo.append(halo_of(xs[1]))
-            cot = after(cotangent, *xs[1])
-            c_parts = [cot, across(cot, 1), across(cot, 2)]
-        else:
-            front, c_parts = together(front, c_parts)
+    def chunked(rows, width):
+        return pl.BlockSpec((None, rows, width), lambda i, sc: (i // hd, i % hd, 0))
+
+    def of_step(*shape):
+        rest = (0,) * len(shape)
+        return pl.BlockSpec((None,) + shape, lambda i, sc: (i // hd,) + rest)
+
+    chunk_lanes = pl.BlockSpec((None, 8, rows), lambda i, sc: (i // hd, 0, i % hd))
+    front = call(
+        front_kernel,
+        (micros * hd,),
+        [of_step(rows, dim)] * 3
+        + [whole((rows, dim))] * 2
+        + [
+            of_step(EDGE, dim), chunk_lanes, whole((1, dim)), head_cols(dim, width),
+            head_cols(dim, width, heads), *conv_specs,
+        ]
+        + [sq_spec] * 3
+        + gate_specs,
+        [
+            chunked(rows, dim), chunked(rows, width),
+            pl.BlockSpec((None, 5, rows, width), lambda i, sc: (i // hd, 0, i % hd, 0)),
+            of_step(EDGE, width), chunk_lanes,
+        ],
+        [
+            ((micros, span, dim), BF), f_span, ((micros, 5, span, width), BF),
+            ((micros, EDGE, width), BF), (lanes, F32),
+        ],
+        [pltpu.VMEM((rows, dim), BF), tiles],
+        20,
+        [
+            sc, *x_parts, *x_far, x_halo, marks, gain, w_up, w_up, conv_w, cb, wq, wk, wv, gate_t,
+            gate_t, gate_t,
+        ],
+    )
+    front, c_parts = together(front, c_parts)
     normed, gz, five, halo, gate_terms = front
     gates = exchange([gate_terms] * hd)
     def of_five(at, count):
@@ -869,12 +891,12 @@
 
     lane_spec = of_micro(None, 8, span)
     state_spec = of_micro(None, width, width)
-    gates, (c_x, c_y) = together(gates, c_parts[1:])
-    c_parts = c_parts + [across(c_x[0], 2), across(c_y[1], 1)]
+    gates, onward = together(gates, [c_parts[1][0], c_parts[2][1]])
+    c_parts = c_parts + [across(onward[0], 2), across(onward[1], 1)]
     state = call(
         partial(gates_kernel, seqs),
         (micros,),
-        [pl.BlockSpec(memory_space=pltpu.SMEM)] * 2 + [lane_spec] * 4 + [of_five(1, span), of_five(2, span)],
+        [pl.BlockSpec(memory_space=pltpu.SMEM)] * 2 + [lane_spec] + [held] * 3 + [of_five(1, span), of_five(2, span)],
         [lane_spec, state_spec],
         [(lanes, F32), ((micros, width, width), F32)],
         [],
@@ -885,16 +907,17 @@
     rows_t, states = state
     states_in = lax.ppermute(states, "seq", [(0, 1)])
 
-    *pairs, gd, gg, four, d_states, small_mix, sums = call(
+    half_w = inner // every
+    *pairs, gd, gg, both, four, d_states, small_mix, sums = call(
         mix_kernel,
         (1,),
-        [whole(lanes), whole((micros, width, width)), head_cols(1, width), head_cols(1, width)]
+        [whole(lanes), held, head_cols(1, width), head_cols(1, width)]
         + [anywhere] * 9,
-        [anywhere] * 7 + [whole((micros, width, width)), whole((8, width)), whole(lanes)],
+        [anywhere] * 8 + [whole((micros, width, width)), whole((8, width)), whole(lanes)],
         [((2 * micros, rows, width), BF)] * 4
         + [((width, dim), BF)] * 2
         + [
-            ((micros, 4, span, width), F32), ((micros, width, width), F32), ((8, width), F32),
+            ((ranks, 2 * half_w, dim), BF), ((micros, 4, span, width), F32), ((micros, width, width), F32), ((8, width), F32),
             (lanes, F32),
         ],
         [
@@ -919,6 +942,7 @@
             pltpu.VMEM((rows, width), BF),
             dma((micros, 6, 4)),
             dma((micros, 5, 4)),
+            dma((2, ranks)),
         ],
         45,
         [sc, rows_t, states_in, gn, sk, five, gz, normed, *c_parts, w_down],
@@ -927,7 +951,7 @@
     d_gates = call(
         gates_back_kernel,
         (micros,),
-        [of_five(1, span), of_five(2, span), lane_spec, lane_spec, state_spec],
+        [of_five(1, span), of_five(2, span), lane_spec, lane_spec, held],
         [lane_spec],
         [(lanes, F32)],
         [],
@@ -936,11 +960,10 @@
     )[0]
     d_gates = exchange([d_gates] * hd)
 
-    half_w, down_w = inner // every, inner // every
-    early = [gg.reshape(ranks, half_w, dim), gd.reshape(ranks, down_w, dim)]
-    early = lax.all_to_all(
-        jnp.concatenate(early, axis=1), ("dp", "seq"), split_axis=0, concat_axis=0, tiled=True
-    )
+    if half_w % EDGE:
+        both = [gg.reshape(ranks, half_w, dim), gd.reshape(ranks, half_w, dim)]
+        both = jnp.concatenate(both, axis=1)
+    early = lax.all_to_all(both, ("dp", "seq"), split_axis=0, concat_axis=0, tiled=True)
     pairs = exchange([after(part, *d_gates) for part in pairs])
 
     top = of_micro(None, EDGE, width)
@@ -952,7 +975,8 @@
         edge_kernel,
         (micros,),
         [of_four(0), of_four(1)]
-        + [of_micro(None, 8, 128)] * 4
+        + [whole(lanes)]
+        + [held] * 3
         + [of_five(4, EDGE), top, of_micro(None, 8, 128), of_four(3)]
         + gate_specs[:2]
         + [sq_spec, sq_spec, *conv_specs],
@@ -967,11 +991,10 @@
     *d_inners, late = call(
         front_back_kernel,
         (1,),
-        [whole(lanes)] * 6
-        + [
-            whole((micros, width, width)), whole((micros, EDGE, width)), whole((8, width)),
-            whole((micros, EDGE, width)),
-        ]
+        [whole(lanes)]
+        + [held] * 3
+        + [whole(lanes)] * 2
+        + [held, whole((micros, EDGE, width)), whole((8, width)), held]
         + gate_specs
         + [sq_spec] * 3
         + conv_specs
@@ -1076,7 +1099,7 @@
     g_gate, g_wq, g_wk, g_wv, g_cw, g_cb, g_gn, g_sk, g_ln, g_ib, g_fb = call(
         table_kernel,
         (1,),
-        [whole(small.shape)] * 4,
+        [whole(small.shape)] + [held] * 3,
         [whole(shape) for shape, _ in flat],
         flat,
         [pltpu.VMEM((hd, SMALL, width), F32)],

time: 249 us -> 239 us (0.960)
  waiting for transfers between devices: 45.4 us -> 56.4 us
  Pallas kernels: 125 us -> 115 us
  local copies, waits for them, and re-layouts: 13.1 us -> 8.82 us
  starting transfers between devices: 53.7 us -> 49.7 us
  other arithmetic: 9.46 us -> 6.5 us
    ppermute x25 -> x23, waiting for transfers between devices: 26 us -> 39.6 us  [across(): return lax.ppermute(value, 'head', [(at, at ^ rel) for at in range(hd)])]
    pallas_call x9 -> x8, Pallas kernels: 125 us -> 115 us  [call(): pl.pallas_call(body, grid_spec=pltpu.PrefetchScalarGridSpec(num_scalar_pr...]
    unnamed x86 -> x48, local copies, waits for them, and re-layouts: 6.11 us -> 2.59 us
    ppermute x25 -> x23, starting transfers between devices: 32.1 us -> 29.8 us  [across(): return lax.ppermute(value, 'head', [(at, at ^ rel) for at in range(hd)])]
  transfers between devices with their start and end apart: 39 -> 36, of which waited for: 21 -> 21; matrix products, arithmetic and copies ran while one was open for 6% -> 5% of each run, Pallas kernels for 31% -> 28%
where the time goes in v2:
time: 239 us; the launch traced here: 238 us
  Pallas kernels  115 us (48%)
  waiting for transfers between devices  56.4 us (24%)
  starting transfers between devices  49.7 us (21%)
  local copies, waits for them, and re-layouts  8.82 us (4%)
  other arithmetic  6.5 us (3%)
    pallas_call x8, Pallas kernels, call(): pl.pallas_call(body, grid_spec=pltpu.PrefetchScalarGridSpec(num_scalar_pr...  115 us
    ppermute x23, waiting for transfers between devices, across(): return lax.ppermute(value, 'head', [(at, at ^ rel) for at in range(hd)])  39.6 us
    ppermute x23, starting transfers between devices, across(): return lax.ppermute(value, 'head', [(at, at ^ rel) for at in range(hd)])  29.8 us
    ppermute x1, waiting for transfers between devices, per_device(): lax.ppermute(g_gate, 'seq', [(1, 0)])  9.19 us
    all_to_all x1, starting transfers between devices, per_device(): lax.all_to_all(both, ('dp', 'seq'), split_axis=0, concat_axis=0, tiled=True)  5.71 us
  transfers between devices with their start and end apart: 36, of which 21 were waited for; matrix products, arithmetic and copies ran while one was open for 5% of the time, Pallas kernels for 28%

profile of v2, /device:TPU:0, one launch (start us, length us, event | category | flops | bytes accessed | tf_op | source)
XLA Modules:
  0.0 237.8 jit_solution(9185370182557838738)
XLA Ops:
  0.7 3.0 %collective-permute-start = (bf16[2,256,768]{2,1,0:T(8,128)(2,1)}, bf16[2,256,768]{2,1,0:T(8,128)(2,1)}, u32[]{:S(2)}, u32[]{:S(2)}) collective-permute-start(bf16[2,256,768]{2,1,0:T(8,128)(2,1)} %rest_0_.1), channel_id=1, source_target_pairs={{0,1},{1,0},{2,3},{3,2},{4,5},{5,4},{6,7},{7,6},{8,9},{9,8},{10,11... | collective-permute-start | bytes 2359304 | tf_op jit(solution)/shard_map/ppermute | solution.py:796
  11.1 10.4 %collective-permute-done.x1 = bf16[2,256,768]{2,1,0:T(8,128)(2,1)} collective-permute-done((bf16[2,256,768]{2,1,0:T(8,128)(2,1)}, bf16[2,256,768]{2,1,0:T(8,128)(2,1)}, u32[]{:S(2)}, u32[]{:S(2)}) %collective-permute-start) | collective-permute-done | bytes 786464 | tf_op jit(solution)/shard_map/ppermute | solution.py:796
  25.6 1.8 slice_bitcast_fusion.2
  27.9 5.8 %collective-permute-done.2.x3a = bf16[256,768]{1,0:T(8,128)(2,1)S(1)} collective-permute-done((bf16[256,768]{1,0:T(8,128)(2,1)S(1)}, bf16[256,768]{1,0:T(8,128)(2,1)S(1)}, u32[]{:S(2)}, u32[]{:S(2)}) %collective-permute-start.2) | collective-permute-done | bytes 393248 | tf_op jit(solution)/shard_map/ppermute | solution.py:796
  33.7 3.2 %collective-permute-done.3.x3b = bf16[256,768]{1,0:T(8,128)(2,1)S(1)} collective-permute-done((bf16[256,768]{1,0:T(8,128)(2,1)}, bf16[256,768]{1,0:T(8,128)(2,1)S(1)}, u32[]{:S(2)}, u32[]{:S(2)}) %collective-permute-start.3) | collective-permute-done | bytes 393248 | tf_op jit(solution)/shard_map/ppermute | solution.py:796
  41.2 17.1 %shard_map.271 = (bf16[2,1024,768]{2,1,0:T(8,128)(2,1)}, f32[2,1024,384]{2,1,0:T(8,128)}, bf16[2,5,1024,384]{3,2,1,0:T(8,128)(2,1)}, bf16[2,16,384]{2,1,0:T(8,128)(2,1)S(1)}, f32[2,8,1024]{2,1,0:T(8,128)S(1)}) custom-call(s32[10]{0:T(128)S(1)} %pad_add_fusion.sc, bf16[2,256,768]{2,1,0:T(8,128)(2,1)} %rest_0_.1, ...), custom_call_target="tpu_custom_call" | custom-call | flops 1150000000 | bytes 1000000 | tf_op jit(solution)/shard_map/pallas_call | solution.py:750
  64.0 2.4 %collective-permute-done.9.g3 = f32[2,8,1024]{2,1,0:T(8,128)S(1)} collective-permute-done((f32[2,8,1024]{2,1,0:T(8,128)S(1)}, f32[2,8,1024]{2,1,0:T(8,128)S(1)}, u32[]{:S(2)}, u32[]{:S(2)}) %collective-permute-start.9) | collective-permute-done | bytes 65568 | tf_op jit(solution)/shard_map/ppermute | solution.py:796
  67.6 6.0 %shard_map.272 = (f32[2,8,1024]{2,1,0:T(8,128)S(1)}, f32[2,384,384]{2,1,0:T(8,128)S(1)}) custom-call(s32[10]{0:T(128)S(1)} %pad_add_fusion.sc, f32[4]{0:T(128)S(1)} %copy-done.6, f32[4]{0:T(128)S(1)} %copy-done.7, f32[2,8,1024]{2,1,0:T(8,128)S(1)} %get-tuple-element.138.g0, f32[2,8,1024]{2,1,0:T(8,128)S(1)} %collective-permute-done.7.g1, ...), custom_call_target="tpu_custom_call" | custom-call | flops 402500000 | bytes 1000000 | tf_op jit(solution)/shard_map/pallas_call | solution.py:750
  73.6 2.5 %collective-permute-done.10.c3a = bf16[256,768]{1,0:T(8,128)(2,1)S(1)} collective-permute-done((bf16[256,768]{1,0:T(8,128)(2,1)S(1)}, bf16[256,768]{1,0:T(8,128)(2,1)S(1)}, u32[]{:S(2)}, u32[]{:S(2)}) %collective-permute-start.10) | collective-permute-done | bytes 393248 | tf_op jit(solution)/shard_map/ppermute | solution.py:796
  77.9 2.2 collective-permute-done.12.s_in
  81.2 47.6 %shard_map.273 = (bf16[4,256,384]{2,1,0:T(8,128)(2,1)}, bf16[4,256,384]{2,1,0:T(8,128)(2,1)}, bf16[4,256,384]{2,1,0:T(8,128)(2,1)}, bf16[4,256,384]{2,1,0:T(8,12...) custom-call(s32[10]{0:T(128)S(1)} %pad_add_fusion.sc, ...), custom_call_target="tpu_custom_call" | custom-call | flops 2587500032 | bytes 1000000 | tf_op jit(solution)/shard_map/pallas_call | solution.py:750
  130.1 5.7 %all-to-all-start = ((bf16[8,96,768]{2,1,0:T(8,128)(2,1)}), bf16[8,96,768]{2,1,0:T(8,128)(2,1)}, u32[]{:S(2)}, u32[]{:S(2)}) async-start(bf16[8,96,768]{2,1,0:T(8,128)(2,1)} %get-tuple-element.188), calls=%async_computation | async-start | bytes 2359296 | tf_op jit(solution)/shard_map/all_to_all | solution.py:966
  135.8 5.9 %shard_map.274.d0 = f32[2,8,1024]{2,1,0:T(8,128)S(1)} custom-call(s32[10]{0:T(128)S(1)} %pad_add_fusion.sc, bf16[2,5,1024,384]{3,2,1,0:T(8,128)(2,1)} %get-tuple-element.134.k.v.five.inner, bf16[2,5,1024,384]{3,2,1,0:T(8,128)(2,1)} %get-tuple-element.134.k.v.five.inner, f32[2,8,1024]{2,1,0:T(8,128)S(1)} %get-tuple-element.147.rows.rows_t, ...), custom_call_target="tpu_custom_call" | custom-call | flops 460000000 | bytes 1000000 | tf_op jit(solution)/shard_map/pallas_call | solution.py:750
  146.8 2.1 collective-permute-done.16.d3
  152.4 2.6 %shard_map.275 = f32[2,16,384]{2,1,0:T(8,128)S(1)} custom-call(s32[10]{0:T(128)S(1)} %pad_add_fusion.sc, f32[2,4,1024,384]{3,2,1,0:T(8,128)} %get-tuple-element.162.dq.dk.skip_d.four, f32[2,4,1024,384]{3,2,1,0:T(8,128)} %get-tuple-element.162.dq.dk.skip_d.four, f32[2,8,1024]{2,1,0:T(8,128)S(1)} %shard_map.274.d0, ...), custom_call_target="tpu_custom_call" | custom-call | flops 230000000 | bytes 1000000 | tf_op jit(solution)/shard_map/pallas_call | solution.py:750
  158.1 24.4 %shard_map.276 = (bf16[2,256,384]{2,1,0:T(8,128)(2,1)}, bf16[2,256,384]{2,1,0:T(8,128)(2,1)}, bf16[2,256,384]{2,1,0:T(8,128)(2,1)}, bf16[2,256,384]{2,1,0:T(8,128)(2,1)}, f32[408,768]{1,0:T(8,128)}) custom-call(s32[10]{0:T(128)S(1)} %pad_add_fusion.sc, f32[2,8,1024]{2,1,0:T(8,128)S(1)} %shard_map.274.d0, f32[2,8,1024]{2,1,0:T(8,128)S(1)} %collective-permute-done.14.d1, ...), custom_call_target="tpu_custom_call" | custom-call | flops 1610000000 | bytes 1000000 | tf_op jit(solution)/shard_map/pallas_call | solution.py:750
  182.5 2.6 %collective-permute-done.19.rest_4_ = bf16[4,256,384]{2,1,0:T(8,128)(2,1)S(1)} collective-permute-done((bf16[4,256,384]{2,1,0:T(8,128)(2,1)S(1)}, bf16[4,256,384]{2,1,0:T(8,128)(2,1)S(1)}, u32[]{:S(2)}, u32[]{:S(2)}) %collective-permute-start.19) | collective-permute-done | bytes 786464 | tf_op jit(solution)/shard_map/ppermute | solution.py:796
  197.0 9.2 %collective-permute-done.29 = f32[48,768]{1,0:T(8,128)S(1)} collective-permute-done((f32[48,768]{1,0:T(8,128)S(1)}, f32[48,768]{1,0:T(8,128)S(1)}, u32[]{:S(2)}, u32[]{:S(2)}) %collective-permute-start.29) | collective-permute-done | bytes 147488 | tf_op jit(solution)/shard_map/ppermute | solution.py:1061
  206.2 2.9 %collective-permute-done.28 = f32[24,768]{1,0:T(8,128)S(1)} collective-permute-done((f32[24,768]{1,0:T(8,128)S(1)}, f32[24,768]{1,0:T(8,128)S(1)}, u32[]{:S(2)}, u32[]{:S(2)}) %collective-permute-start.28) | collective-permute-done | bytes 73760 | tf_op jit(solution)/shard_map/ppermute | solution.py:1054
  209.1 3.4 %collective-permute-start.33 = (f32[96,768]{1,0:T(8,128)S(1)}, f32[96,768]{1,0:T(8,128)S(1)}, u32[]{:S(2)}, u32[]{:S(2)}) collective-permute-start(f32[96,768]{1,0:T(8,128)S(1)} %slice_select_fusion), channel_id=1, source_target_pairs={{0,16},{1,20},{2,24},{3,28},{4,0},{5,4},{6,8},{7,12},{8,17},{9,21}... | collective-permute-start | bytes 884744 | tf_op jit(solution)/shard_map/ppermute | solution.py:1071
  213.2 10.2 %shard_map.277 = (bf16[2,256,768]{2,1,0:T(8,128)(2,1)}, bf16[2,256,768]{2,1,0:T(8,128)(2,1)}) custom-call(s32[10]{0:T(128)S(1)} %pad_add_fusion.sc, f32[1,768]{1,0:T(1,128)S(1)} %reshape.223.gain, bf16[2,256,768]{2,1,0:T(8,128)(2,1)} %rest_0_.1, bf16[2,256,768]{2,1,0:T(8,128)(2,1)} %rest_1_.1, bf16[4,256,384]{2,1,0:T(8,128)(2,1)} %get-tuple-element.179.rest_2_, ...), custom_call_target="tpu_custom_call" | custom-call | flops 575000000 | bytes 1000000 | tf_op jit(solution)/shard_map/pallas_call | solution.py:750
  223.4 3.4 %collective-permute-start.30 = (f32[24,768]{1,0:T(8,128)S(1)}, f32[24,768]{1,0:T(8,128)S(1)}, u32[]{:S(2)}, u32[]{:S(2)}) collective-permute-start(f32[24,768]{1,0:T(8,128)S(1)} %broadcast_select_fusion.t0), channel_id=1, source_target_pairs={{0,1},{1,0},{2,3},{3,2},{4,5},{5,4},{6,7},{7,6},{8,9},{9,8},{10,11... | collective-permute-start | bytes 221192 | tf_op jit(solution)/shard_map/ppermute | solution.py:796
  226.8 3.1 %collective-permute-start.31 = (f32[24,768]{1,0:T(8,128)S(1)}, f32[24,768]{1,0:T(8,128)S(1)}, u32[]{:S(2)}, u32[]{:S(2)}) collective-permute-start(f32[24,768]{1,0:T(8,128)S(1)} %broadcast_select_fusion.t0), channel_id=1, source_target_pairs={{0,2},{1,3},{2,0},{3,1},{4,6},{5,7},{6,4},{7,5},{8,10},{9,11},{10,... | collective-permute-start | bytes 221192 | tf_op jit(solution)/shard_map/ppermute | solution.py:796
  233.0 2.1 collective-permute-done.32.t3
  (159 shorter events, 56.9 us)
Async XLA Ops:
  0.7 20.9 %collective-permute-start = (bf16[2,256,768]{2,1,0:T(8,128)(2,1)}, bf16[2,256,768]{2,1,0:T(8,128)(2,1)}, u32[]{:S(2)}, u32[]{:S(2)}) collective-permute-start(bf16[2,256,768]{2,1,0:T(8,128)(2,1)} %rest_0_.1), channel_id=1, source_target_pairs={{0,1},{1,0},{2,3},{3,2},{4,5},{5,4},{6,7},{7,6},{8,9},{9,8},{10,11... | collective-permute-start | bytes 2359304 | tf_op jit(solution)/shard_map/ppermute | solution.py:796
  3.7 19.3 %collective-permute-start.1 = (bf16[2,256,768]{2,1,0:T(8,128)(2,1)}, bf16[2,256,768]{2,1,0:T(8,128)(2,1)}, u32[]{:S(2)}, u32[]{:S(2)}) collective-permute-start(bf16[2,256,768]{2,1,0:T(8,128)(2,1)} %rest_0_.1), channel_id=1, source_target_pairs={{0,2},{1,3},{2,0},{3,1},{4,6},{5,7},{6,4},{7,5},{8,10},{9,11},{10,... | collective-permute-start | bytes 2359304 | tf_op jit(solution)/shard_map/ppermute | solution.py:796
  24.0 9.7 %collective-permute-start.2 = (bf16[256,768]{1,0:T(8,128)(2,1)S(1)}, bf16[256,768]{1,0:T(8,128)(2,1)S(1)}, u32[]{:S(2)}, u32[]{:S(2)}) collective-permute-start(bf16[256,768]{1,0:T(8,128)(2,1)S(1)} %slice_bitcast_fusion.3), channel_id=1, source_target_pairs={{0,2},{1,3},{2,0},{3,1},{4,6},{5,7},{6,4},{7,5},{8,10},{9,11},{10,... | collective-permute-start | bytes 1179656 | tf_op jit(solution)/shard_map/ppermute | solution.py:796
  27.4 9.6 %collective-permute-start.3 = (bf16[256,768]{1,0:T(8,128)(2,1)}, bf16[256,768]{1,0:T(8,128)(2,1)S(1)}, u32[]{:S(2)}, u32[]{:S(2)}) collective-permute-start(bf16[256,768]{1,0:T(8,128)(2,1)} %slice_bitcast_fusion.2), channel_id=1, source_target_pairs={{0,1},{1,0},{2,3},{3,2},{4,5},{5,4},{6,7},{7,6},{8,9},{9,8},{10,11... | collective-permute-start | bytes 1179656 | tf_op jit(solution)/shard_map/ppermute | solution.py:796
  37.0 21.3 %collective-permute-start.5 = (bf16[2,256,768]{2,1,0:T(8,128)(2,1)S(1)}, bf16[2,256,768]{2,1,0:T(8,128)(2,1)S(1)}, u32[]{:S(2)}, u32[]{:S(2)}) collective-permute-start(bf16[2,256,768]{2,1,0:T(8,128)(2,1)S(1)} %copy-done.8), channel_id=1, source_target_pairs={{0,1},{1,0},{2,3},{3,2},{4,5},{5,4},{6,7},{7,6},{8,9},{9,8},{10,11... | collective-permute-start | bytes 2359304 | tf_op jit(solution)/shard_map/ppermute | solution.py:796
  37.6 20.8 %collective-permute-start.6 = (bf16[2,256,768]{2,1,0:T(8,128)(2,1)S(1)}, bf16[2,256,768]{2,1,0:T(8,128)(2,1)S(1)}, u32[]{:S(2)}, u32[]{:S(2)}) collective-permute-start(bf16[2,256,768]{2,1,0:T(8,128)(2,1)S(1)} %copy-done.8), channel_id=1, source_target_pairs={{0,2},{1,3},{2,0},{3,1},{4,6},{5,7},{6,4},{7,5},{8,10},{9,11},{10,... | collective-permute-start | bytes 2359304 | tf_op jit(solution)/shard_map/ppermute | solution.py:796
  61.3 5.2 %collective-permute-start.9 = (f32[2,8,1024]{2,1,0:T(8,128)S(1)}, f32[2,8,1024]{2,1,0:T(8,128)S(1)}, u32[]{:S(2)}, u32[]{:S(2)}) collective-permute-start(f32[2,8,1024]{2,1,0:T(8,128)S(1)} %get-tuple-element.138.g0), channel_id=1, source_target_pairs={{0,3},{1,2},{2,1},{3,0},{4,7},{5,6},{6,5},{7,4},{8,11},{9,10},{10,... | collective-permute-start | bytes 196616 | tf_op jit(solution)/shard_map/ppermute | solution.py:796
  66.4 9.7 %collective-permute-start.10 = (bf16[256,768]{1,0:T(8,128)(2,1)S(1)}, bf16[256,768]{1,0:T(8,128)(2,1)S(1)}, u32[]{:S(2)}, u32[]{:S(2)}) collective-permute-start(bf16[256,768]{1,0:T(8,128)(2,1)S(1)} %slice_bitcast_fusion.1), channel_id=1, source_target_pairs={{0,2},{1,3},{2,0},{3,1},{4,6},{5,7},{6,4},{7,5},{8,10},{9,11},{10,... | collective-permute-start | bytes 1179656 | tf_op jit(solution)/shard_map/ppermute | solution.py:796
  66.9 9.5 %collective-permute-start.11 = (bf16[256,768]{1,0:T(8,128)(2,1)S(1)}, bf16[256,768]{1,0:T(8,128)(2,1)S(1)}, u32[]{:S(2)}, u32[]{:S(2)}) collective-permute-start(bf16[256,768]{1,0:T(8,128)(2,1)S(1)} %slice_bitcast_fusion), channel_id=1, source_target_pairs={{0,1},{1,0},{2,3},{3,2},{4,5},{5,4},{6,7},{7,6},{8,9},{9,8},{10,11... | collective-permute-start | bytes 1179656 | tf_op jit(solution)/shard_map/ppermute | solution.py:796
  128.8 7.0 %collective-permute-start.13 = (f32[2,384,384]{2,1,0:T(8,128)}, f32[2,384,384]{2,1,0:T(8,128)S(1)}, u32[]{:S(2)}, u32[]{:S(2)}) collective-permute-start(f32[2,384,384]{2,1,0:T(8,128)} %get-tuple-element.159), channel_id=1, source_target_pairs={{4,0},{5,1},{6,2},{7,3},{12,8},{13,9},{14,10},{15,11},{20,16},{21,... | collective-permute-start | bytes 3538952 | tf_op jit(solution)/shard_map/ppermute | solution.py:950
  130.1 57.3 %all-to-all-start = ((bf16[8,96,768]{2,1,0:T(8,128)(2,1)}), bf16[8,96,768]{2,1,0:T(8,128)(2,1)}, u32[]{:S(2)}, u32[]{:S(2)}) async-start(bf16[8,96,768]{2,1,0:T(8,128)(2,1)} %get-tuple-element.188), calls=%async_computation | async-start | bytes 2359296 | tf_op jit(solution)/shard_map/all_to_all | solution.py:966
  148.9 33.6 %collective-permute-start.20 = (bf16[4,256,384]{2,1,0:T(8,128)(2,1)S(1)}, bf16[4,256,384]{2,1,0:T(8,128)(2,1)S(1)}, u32[]{:S(2)}, u32[]{:S(2)}) collective-permute-start(bf16[4,256,384]{2,1,0:T(8,128)(2,1)S(1)} %copy-done.21), channel_id=1, source_target_pairs={{0,3},{1,2},{2,1},{3,0},{4,7},{5,6},{6,5},{7,4},{8,11},{9,10},{10,... | collective-permute-start | bytes 2359304 | tf_op jit(solution)/shard_map/ppermute | solution.py:796
  150.6 34.5 %collective-permute-start.19 = (bf16[4,256,384]{2,1,0:T(8,128)(2,1)S(1)}, bf16[4,256,384]{2,1,0:T(8,128)(2,1)S(1)}, u32[]{:S(2)}, u32[]{:S(2)}) collective-permute-start(bf16[4,256,384]{2,1,0:T(8,128)(2,1)S(1)} %copy-done.20), channel_id=1, source_target_pairs={{0,2},{1,3},{2,0},{3,1},{4,6},{5,7},{6,4},{7,5},{8,10},{9,11},{10,... | collective-permute-start | bytes 2359304 | tf_op jit(solution)/shard_map/ppermute | solution.py:796
  152.1 33.0 %collective-permute-start.18 = (bf16[4,256,384]{2,1,0:T(8,128)(2,1)S(1)}, bf16[4,256,384]{2,1,0:T(8,128)(2,1)}, u32[]{:S(2)}, u32[]{:S(2)}) collective-permute-start(bf16[4,256,384]{2,1,0:T(8,128)(2,1)S(1)} %copy-done.19), channel_id=1, source_target_pairs={{0,1},{1,0},{2,3},{3,2},{4,5},{5,4},{6,7},{7,6},{8,9},{9,8},{10,11... | collective-permute-start | bytes 2359304 | tf_op jit(solution)/shard_map/ppermute | solution.py:796
  185.2 23.9 %collective-permute-start.21 = (bf16[2,256,384]{2,1,0:T(8,128)(2,1)}, bf16[2,256,384]{2,1,0:T(8,128)(2,1)S(1)}, u32[]{:S(2)}, u32[]{:S(2)}) collective-permute-start(bf16[2,256,384]{2,1,0:T(8,128)(2,1)} %get-tuple-element.184), channel_id=1, source_target_pairs={{0,1},{1,0},{2,3},{3,2},{4,5},{5,4},{6,7},{7,6},{8,9},{9,8},{10,11... | collective-permute-start | bytes 1179656 | tf_op jit(solution)/shard_map/ppermute | solution.py:796
  186.2 22.9 %collective-permute-start.22 = (bf16[2,256,384]{2,1,0:T(8,128)(2,1)}, bf16[2,256,384]{2,1,0:T(8,128)(2,1)S(1)}, u32[]{:S(2)}, u32[]{:S(2)}) collective-permute-start(bf16[2,256,384]{2,1,0:T(8,128)(2,1)} %get-tuple-element.185), channel_id=1, source_target_pairs={{0,2},{1,3},{2,0},{3,1},{4,6},{5,7},{6,4},{7,5},{8,10},{9,11},{10,... | collective-permute-start | bytes 1179656 | tf_op jit(solution)/shard_map/ppermute | solution.py:796
  192.8 16.3 %collective-permute-start.23 = (bf16[2,256,384]{2,1,0:T(8,128)(2,1)S(1)}, bf16[2,256,384]{2,1,0:T(8,128)(2,1)S(1)}, u32[]{:S(2)}, u32[]{:S(2)}) collective-permute-start(bf16[2,256,384]{2,1,0:T(8,128)(2,1)S(1)} %copy-done.22), channel_id=1, source_target_pairs={{0,3},{1,2},{2,1},{3,0},{4,7},{5,6},{6,5},{7,4},{8,11},{9,10},{10,... | collective-permute-start | bytes 1179656 | tf_op jit(solution)/shard_map/ppermute | solution.py:796
  194.2 11.9 %collective-permute-start.29 = (f32[48,768]{1,0:T(8,128)S(1)}, f32[48,768]{1,0:T(8,128)S(1)}, u32[]{:S(2)}, u32[]{:S(2)}) collective-permute-start(f32[48,768]{1,0:T(8,128)S(1)} %get-tuple-element.220), channel_id=1, source_target_pairs={{4,0},{5,1},{6,2},{7,3},{12,8},{13,9},{14,10},{15,11},{20,16},{21,... | collective-permute-start | bytes 442376 | tf_op jit(solution)/shard_map/ppermute | solution.py:1061
  195.7 13.4 %collective-permute-start.28 = (f32[24,768]{1,0:T(8,128)S(1)}, f32[24,768]{1,0:T(8,128)S(1)}, u32[]{:S(2)}, u32[]{:S(2)}) collective-permute-start(f32[24,768]{1,0:T(8,128)S(1)} %slice_add_fusion), channel_id=1, source_target_pairs={{4,0},{5,1},{6,2},{7,3},{12,8},{13,9},{14,10},{15,11},{20,16},{21,... | collective-permute-start | bytes 221192 | tf_op jit(solution)/shard_map/ppermute | solution.py:1054
  209.1 27.3 %collective-permute-start.33 = (f32[96,768]{1,0:T(8,128)S(1)}, f32[96,768]{1,0:T(8,128)S(1)}, u32[]{:S(2)}, u32[]{:S(2)}) collective-permute-start(f32[96,768]{1,0:T(8,128)S(1)} %slice_select_fusion), channel_id=1, source_target_pairs={{0,16},{1,20},{2,24},{3,28},{4,0},{5,4},{6,8},{7,12},{8,17},{9,21}... | collective-permute-start | bytes 884744 | tf_op jit(solution)/shard_map/ppermute | solution.py:1071
  212.5 17.4 %collective-permute-start.34 = (f32[48,768]{1,0:T(8,128)S(1)}, f32[48,768]{1,0:T(8,128)S(1)}, u32[]{:S(2)}, u32[]{:S(2)}) collective-permute-start(f32[48,768]{1,0:T(8,128)S(1)} %get-tuple-element.219), channel_id=1, source_target_pairs={{0,0},{1,8},{2,16},{3,24},{4,1},{5,9},{6,17},{7,25},{8,2},{9,10},{... | collective-permute-start | bytes 442376 | tf_op jit(solution)/shard_map/ppermute | solution.py:1068
  223.4 8.2 %collective-permute-start.30 = (f32[24,768]{1,0:T(8,128)S(1)}, f32[24,768]{1,0:T(8,128)S(1)}, u32[]{:S(2)}, u32[]{:S(2)}) collective-permute-start(f32[24,768]{1,0:T(8,128)S(1)} %broadcast_select_fusion.t0), channel_id=1, source_target_pairs={{0,1},{1,0},{2,3},{3,2},{4,5},{5,4},{6,7},{7,6},{8,9},{9,8},{10,11... | collective-permute-start | bytes 221192 | tf_op jit(solution)/shard_map/ppermute | solution.py:796
  226.8 6.3 %collective-permute-start.31 = (f32[24,768]{1,0:T(8,128)S(1)}, f32[24,768]{1,0:T(8,128)S(1)}, u32[]{:S(2)}, u32[]{:S(2)}) collective-permute-start(f32[24,768]{1,0:T(8,128)S(1)} %broadcast_select_fusion.t0), channel_id=1, source_target_pairs={{0,2},{1,3},{2,0},{3,1},{4,6},{5,7},{6,4},{7,5},{8,10},{9,11},{10,... | collective-permute-start | bytes 221192 | tf_op jit(solution)/shard_map/ppermute | solution.py:796
  229.9 5.3 %collective-permute-start.32 = (f32[24,768]{1,0:T(8,128)S(1)}, f32[24,768]{1,0:T(8,128)S(1)}, u32[]{:S(2)}, u32[]{:S(2)}) collective-permute-start(f32[24,768]{1,0:T(8,128)S(1)} %broadcast_select_fusion.t0), channel_id=1, source_target_pairs={{0,3},{1,2},{2,1},{3,0},{4,7},{5,6},{6,5},{7,4},{8,11},{9,10},{10,... | collective-permute-start | bytes 221192 | tf_op jit(solution)/shard_map/ppermute | solution.py:796
  (35 other events, 299.9 us)

commit v3 on v2

--- a/solution.py
+++ b/solution.py
@@ -187,7 +187,7 @@
 ):
     p0, p1, p2, p3, gd_o, gg_o, both_o, four_o, ds_o, small_o, sums_o = rest[:11]
     fb, zb, nb, cb, wb, pb, four, gd, gg, go, acc, a_high, decays = rest[11:24]
-    q2, v2, dh2, dbr, brs, dgs, in_sems, out_sems, pack_sems = rest[24:]
+    q2, v2, dh2, dbr, in_sems, out_sems, pack_sems = rest[24:]
     h = sc[0]
     micros, _, span, width = fb.shape
     chunk = acc.shape[0]
@@ -295,14 +295,14 @@
         cols = jnp.transpose(rows[m, :, own])
         cum, seg, carried, valid = cols[:, 0:1], cols[:, 2:3], cols[:, 4:5], cols[:, 6:7]
 
-        def attend(j):
-            at = slice(j * two, (j + 1) * two)
+        def attend(j, wide=two):
+            at = slice(j * two, j * two + wide)
             scores = nt(fb[m, 0, own, :], fb[m, 1, at, :]) * factor
-            allowed = (seg == rows[m, 2:3, at]) & (j * two + iota((1, two), 1) <= here)
+            allowed = (seg == rows[m, 2:3, at]) & (j * two + iota((1, wide), 1) <= here)
             decay = jnp.exp(jnp.where(allowed, cum + rows[m, 1:2, at], NEVER))
-            decays[j] = decay
+            decays[j, :, 0:wide] = decay
             high, low = split(scores * decay)
-            a_high[j] = high
+            a_high[j, :, 0:wide] = high
             return mm(high, fb[m, 2, at, :]) + mm(low, fb[m, 2, at, :])
 
         q2[:, 0:width] = fb[m, 0, own, :]
@@ -313,7 +313,11 @@
         cb[m, i] = (cb[m, i].astype(F32) * valid).astype(BF)
         dbr[...] = nt(cb[m, i], wb[...])
 
-        @pl.when(i >= 2)
+        @pl.when(i == 2)
+        def _():
+            acc[...] += attend(1, chunk)
+
+        @pl.when(i == 3)
         def _():
             acc[...] += attend(1)
 
@@ -331,10 +335,10 @@
             gate_act = gate * sig
             act_f = fb[m, 3, at, :].astype(F32)
             mid = normed_h * gn[...] + sk[...] * act_f
-            brs[part, :] = (mid * gate_act).astype(BF)
+            pb[i, 2 * m, part, :] = (mid * gate_act).astype(BF)
             d_branch = dbr[part, :]
             d_mid = d_branch * gate_act
-            dgs[part, :] = (d_branch * mid * (sig + gate_act * (1.0 - sig))).astype(BF)
+            pb[i, 2 * m + 1, part, :] = (d_branch * mid * (sig + gate_act * (1.0 - sig))).astype(BF)
             sum_gn, sum_sk = sum_gn + folded(d_mid * normed_h), sum_sk + folded(d_mid * act_f)
             four[m, 3, at, :] = d_mid * sk[...]
             d_norm = (d_mid * gn[...]).astype(BF).astype(F32)
@@ -346,17 +350,15 @@
             q2[part, width:] = (d_hid * carried[part]).astype(BF)
         small_o[0:1, :] += jnp.sum(sum_gn, axis=0, keepdims=True)
         small_o[1:2, :] += jnp.sum(sum_sk, axis=0, keepdims=True)
-        pb[i, 2 * m] = brs[...]
-        pb[i, 2 * m + 1] = dgs[...]
-        gd[...] += tn(brs[...], cb[m, i])
-        gg[...] += tn(dgs[...], nb[m, own, :])
+        gd[...] += tn(pb[i, 2 * m], cb[m, i])
+        gg[...] += tn(pb[i, 2 * m + 1], nb[m, own, :])
         ds_o[m] += tn(fb[m, 0, own, :], q2[:, width:])
         acc[...] = carried * nt(dh2[:, 0:width], s_in[m].astype(BF))
-        def attend_back(j):
-            at = slice(j * two, (j + 1) * two)
+        def attend_back(j, wide=two):
+            at = slice(j * two, j * two + wide)
             d_att = nt(dh2[...], v2[at, :])
-            four[m, 2, at, :] += tn(a_high[j], dh2[:, 0:width])
-            w_high, w_low = split(decays[j] * d_att * factor)
+            four[m, 2, at, :] += tn(a_high[j, :, 0:wide], dh2[:, 0:width])
+            w_high, w_low = split(decays[j, :, 0:wide] * d_att * factor)
             four[m, 1, at, :] += tn(w_high, fb[m, 0, own, :]) + tn(w_low, fb[m, 0, own, :])
             return mm(w_high, fb[m, 1, at, :]) + mm(w_low, fb[m, 1, at, :])
 
@@ -378,7 +380,11 @@
         def _():
             key_out(m, 0).start()
 
-        @pl.when(i >= 2)
+        @pl.when(i == 2)
+        def _():
+            acc[...] += attend_back(1, chunk)
+
+        @pl.when(i == 3)
         def _():
             acc[...] += attend_back(1)
 
@@ -389,19 +395,18 @@
         four[m, 0, own, :] = acc[...]
         for copy in rows_out(m, i):
             copy.start()
-        sums_o[m, :, own] = lane_sums(acc[...] * fb[m, 0, own, :].astype(F32))
         return none
 
     lax.fori_loop(0, 4 * micros, one, 0)
 
     def finish(at_step, none):
-        m, at = at_step // 4, rows_of(at_step % 4)
+        m, at = at_step // 2, rows_of(at_step % 2, two)
+        row_sum = lane_sums(four[m, 0, at, :] * fb[m, 0, at, :].astype(F32))
         col_sum = lane_sums(four[m, 1, at, :] * fb[m, 1, at, :].astype(F32))
-        held = sums_o[m, :, at]
-        sums_o[m, :, at] = jnp.where(iota((8, chunk), 0) == 0, col_sum, held - col_sum)
+        sums_o[m, :, at] = jnp.where(iota((8, two), 0) == 0, col_sum, row_sum - col_sum)
         return none
 
-    lax.fori_loop(0, 4 * micros, finish, 0)
+    lax.fori_loop(0, 2 * micros, finish, 0)
     for m in range(micros):
         for rel in range(4):
             pair_out(m, rel, rel ^ h).wait()
@@ -938,8 +943,6 @@
             pltpu.VMEM((span, 2 * width), BF),
             pltpu.VMEM((rows, 2 * width), BF),
             pltpu.VMEM((rows, width), F32),
-            pltpu.VMEM((rows, width), BF),
-            pltpu.VMEM((rows, width), BF),
             dma((micros, 6, 4)),
             dma((micros, 5, 4)),
             dma((2, ranks)),
@@ -1035,23 +1038,20 @@
     small = late[width:]
     blocks = late[:width].reshape(dp, 2 * half_w, dim)
     d = lax.axis_index("dp")
-    if dp == 4:
+    if dp == 4 and SMALL <= 2 * half_w:
         high = lax.reduce_precision(small, 8, 7)
         table = jnp.concatenate([high.astype(BF), (small - high).astype(BF)], axis=0)
+        table = jnp.pad(table, ((0, 2 * half_w - SMALL), (0, 0)))
 
         def to_plane(rel):
             block = lax.dynamic_index_in_dim(blocks, d ^ rel, 0, keepdims=False).astype(BF)
-            block = jnp.concatenate([block, table], axis=0)
-            if rel == 0:
-                return block
-            pairs_of = [(a * sq + 1, (a ^ rel) * sq + 1) for a in range(dp)]
-            return lax.ppermute(block, ("dp", "seq"), pairs_of)
+            block = jnp.where(s == 1, block, table)
+            return lax.ppermute(block, "dp", [(a, a ^ rel) for a in range(dp)]) if rel else block
 
         terms = [to_plane(rel).astype(F32) for rel in range(dp)]
-        terms = (terms[0] + terms[1]) + (terms[2] + terms[3])
-        g_inner, small = terms[: 2 * half_w], terms[2 * half_w :]
-        small = small[: SMALL // 2] + small[SMALL // 2 :]
-        small = jnp.where(s == 1, small, lax.ppermute(small, "seq", [(1, 0)]))
+        g_inner = (terms[0] + terms[1]) + (terms[2] + terms[3])
+        small = g_inner[: SMALL // 2] + g_inner[SMALL // 2 : SMALL]
+        small = jnp.where(s == 0, small, lax.ppermute(small, "seq", [(0, 1)]))
     else:
         small = lax.psum(small, "dp")
         terms = lax.all_to_all(blocks.astype(BF), "dp", split_axis=0, concat_axis=0, tiled=True)
@@ -1088,7 +1088,7 @@
             pltpu.VMEM((micros * rows, inner), BF),
             dma((10, hd)),
         ],
-        10,
+        100,
         [sc, gain, tokens, cotangent, *pairs, *d_inners, w_up, w_down],
     )
 

time: 239 us -> 236 us (0.987)
    ppermute x1, waiting for transfers between devices: 9.19 us -> 0.01 us  [per_device(): lax.ppermute(g_gate, 'seq', [(1, 0)])]
    ppermute x4, waiting for transfers between devices: 2.91 us -> 8.07 us  [the longest x3 7.86 us: to_plane(): lax.ppermute(block, 'dp', [(a, a ^ rel) for a in range(dp)])]
    ppermute x23, waiting for transfers between devices: 39.6 us -> 44.6 us  [across(): return lax.ppermute(value, 'head', [(at, at ^ rel) for at in range(hd)])]
    ppermute x4, starting transfers between devices: 3.32 us -> 5.98 us  [the longest x3 4.61 us: to_plane(): lax.ppermute(block, 'dp', [(a, a ^ rel) for a in range(dp)])]
  transfers between devices with their start and end apart: 36 -> 36, of which waited for: 21 -> 24; matrix products, arithmetic and copies ran while one was open for 5% -> 4% of each run, Pallas kernels for 28% -> 29%
where the time goes in v3:
time: 236 us; the launch traced here: 235 us
  Pallas kernels  113 us (48%)
  waiting for transfers between devices  57.7 us (24%)
  starting transfers between devices  48.8 us (21%)
  local copies, waits for them, and re-layouts  8.9 us (4%)
  other arithmetic  5.09 us (2%)
    pallas_call x8, Pallas kernels, call(): pl.pallas_call(body, grid_spec=pltpu.PrefetchScalarGridSpec(num_scalar_pr...  113 us
    ppermute x23, waiting for transfers between devices, across(): return lax.ppermute(value, 'head', [(at, at ^ rel) for at in range(hd)])  44.6 us
    ppermute x23, starting transfers between devices, across(): return lax.ppermute(value, 'head', [(at, at ^ rel) for at in range(hd)])  28 us
    ppermute x3, waiting for transfers between devices, to_plane(): lax.ppermute(block, 'dp', [(a, a ^ rel) for a in range(dp)])  7.86 us
    all_to_all x1, starting transfers between devices, per_device(): lax.all_to_all(both, ('dp', 'seq'), split_axis=0, concat_axis=0, tiled=True)  5.69 us
  transfers between devices with their start and end apart: 36, of which 24 were waited for; matrix products, arithmetic and copies ran while one was open for 4% of the time, Pallas kernels for 29%

profile of v3, /device:TPU:0, one launch (start us, length us, event | category | flops | bytes accessed | tf_op | source)
XLA Modules:
  0.0 235.1 jit_solution(4518977965533091682)
XLA Ops:
  0.7 3.0 %collective-permute-start = (bf16[2,256,768]{2,1,0:T(8,128)(2,1)}, bf16[2,256,768]{2,1,0:T(8,128)(2,1)S(1)}, u32[]{:S(2)}, u32[]{:S(2)}) collective-permute-start(bf16[2,256,768]{2,1,0:T(8,128)(2,1)} %rest_0_.1), channel_id=1, source_target_pairs={{0,1},{1,0},{2,3},{3,2},{4,5},{5,4},{6,7},{7,6},{8,9},{9,8},{10,11... | collective-permute-start | bytes 2359304 | tf_op jit(solution)/shard_map/ppermute | solution.py:801
  11.1 10.3 %collective-permute-done.x1 = bf16[2,256,768]{2,1,0:T(8,128)(2,1)S(1)} collective-permute-done((bf16[2,256,768]{2,1,0:T(8,128)(2,1)}, bf16[2,256,768]{2,1,0:T(8,128)(2,1)S(1)}, u32[]{:S(2)}, u32[]{:S(2)}) %collective-permute-start) | collective-permute-done | bytes 786464 | tf_op jit(solution)/shard_map/ppermute | solution.py:801
  26.9 5.8 %collective-permute-done.2.x3a = bf16[256,768]{1,0:T(8,128)(2,1)S(1)} collective-permute-done((bf16[256,768]{1,0:T(8,128)(2,1)S(1)}, bf16[256,768]{1,0:T(8,128)(2,1)S(1)}, u32[]{:S(2)}, u32[]{:S(2)}) %collective-permute-start.2) | collective-permute-done | bytes 393248 | tf_op jit(solution)/shard_map/ppermute | solution.py:801
  32.7 3.2 %collective-permute-done.3.x3b = bf16[256,768]{1,0:T(8,128)(2,1)S(1)} collective-permute-done((bf16[256,768]{1,0:T(8,128)(2,1)}, bf16[256,768]{1,0:T(8,128)(2,1)S(1)}, u32[]{:S(2)}, u32[]{:S(2)}) %collective-permute-start.3) | collective-permute-done | bytes 393248 | tf_op jit(solution)/shard_map/ppermute | solution.py:801
  40.2 17.0 %shard_map.271 = (bf16[2,1024,768]{2,1,0:T(8,128)(2,1)}, f32[2,1024,384]{2,1,0:T(8,128)}, bf16[2,5,1024,384]{3,2,1,0:T(8,128)(2,1)}, bf16[2,16,384]{2,1,0:T(8,128)(2,1)S(1)}, f32[2,8,1024]{2,1,0:T(8,128)S(1)}) custom-call(s32[10]{0:T(128)S(1)} %pad_add_fusion.sc, bf16[2,256,768]{2,1,0:T(8,128)(2,1)} %rest_0_.1, bf16[2,256,768]{2,1,0:T(8,128)(2,1)} %copy-done.8, ...), custom_call_target="tpu_custom_call" | custom-call | flops 1150000000 | bytes 1000000 | tf_op jit(solution)/shard_map/pallas_call | solution.py:755
  62.9 2.4 %collective-permute-done.9.g3 = f32[2,8,1024]{2,1,0:T(8,128)S(1)} collective-permute-done((f32[2,8,1024]{2,1,0:T(8,128)S(1)}, f32[2,8,1024]{2,1,0:T(8,128)S(1)}, u32[]{:S(2)}, u32[]{:S(2)}) %collective-permute-start.9) | collective-permute-done | bytes 65568 | tf_op jit(solution)/shard_map/ppermute | solution.py:801
  66.6 6.0 %shard_map.272 = (f32[2,8,1024]{2,1,0:T(8,128)S(1)}, f32[2,384,384]{2,1,0:T(8,128)S(1)}) custom-call(s32[10]{0:T(128)S(1)} %pad_add_fusion.sc, f32[4]{0:T(128)S(1)} %copy-done.5, f32[4]{0:T(128)S(1)} %copy-done.6, f32[2,8,1024]{2,1,0:T(8,128)S(1)} %get-tuple-element.138.g0, f32[2,8,1024]{2,1,0:T(8,128)S(1)} %collective-permute-done.7.g1, ...), custom_call_target="tpu_custom_call" | custom-call | flops 402500000 | bytes 1000000 | tf_op jit(solution)/shard_map/pallas_call | solution.py:755
  72.6 2.4 %collective-permute-done.10.c3a = bf16[256,768]{1,0:T(8,128)(2,1)S(1)} collective-permute-done((bf16[256,768]{1,0:T(8,128)(2,1)S(1)}, bf16[256,768]{1,0:T(8,128)(2,1)S(1)}, u32[]{:S(2)}, u32[]{:S(2)}) %collective-permute-start.10) | collective-permute-done | bytes 393248 | tf_op jit(solution)/shard_map/ppermute | solution.py:801
  76.9 2.2 collective-permute-done.12.s_in
  80.1 45.8 %shard_map.273 = (bf16[4,256,384]{2,1,0:T(8,128)(2,1)}, bf16[4,256,384]{2,1,0:T(8,128)(2,1)}, bf16[4,256,384]{2,1,0:T(8,128)(2,1)}, bf16[4,256,384]{2,1,0:T(8,12...) custom-call(s32[10]{0:T(128)S(1)} %pad_add_fusion.sc, ...), custom_call_target="tpu_custom_call" | custom-call | flops 2587500032 | bytes 1000000 | tf_op jit(solution)/shard_map/pallas_call | solution.py:755
  127.2 5.7 %all-to-all-start = ((bf16[8,96,768]{2,1,0:T(8,128)(2,1)}), bf16[8,96,768]{2,1,0:T(8,128)(2,1)}, u32[]{:S(2)}, u32[]{:S(2)}) async-start(bf16[8,96,768]{2,1,0:T(8,128)(2,1)} %get-tuple-element.188), calls=%async_computation | async-start | bytes 2359296 | tf_op jit(solution)/shard_map/all_to_all | solution.py:969
  132.9 5.9 %shard_map.274.d0 = f32[2,8,1024]{2,1,0:T(8,128)S(1)} custom-call(s32[10]{0:T(128)S(1)} %pad_add_fusion.sc, bf16[2,5,1024,384]{3,2,1,0:T(8,128)(2,1)} %get-tuple-element.134.k.v.five.inner, bf16[2,5,1024,384]{3,2,1,0:T(8,128)(2,1)} %get-tuple-element.134.k.v.five.inner, f32[2,8,1024]{2,1,0:T(8,128)S(1)} %get-tuple-element.147.rows.rows_t, ...), custom_call_target="tpu_custom_call" | custom-call | flops 460000000 | bytes 1000000 | tf_op jit(solution)/shard_map/pallas_call | solution.py:755
  143.9 2.1 collective-permute-done.16.d3
  149.5 2.6 %shard_map.275 = f32[2,16,384]{2,1,0:T(8,128)S(1)} custom-call(s32[10]{0:T(128)S(1)} %pad_add_fusion.sc, f32[2,4,1024,384]{3,2,1,0:T(8,128)} %get-tuple-element.162.dq.dk.skip_d.four, f32[2,4,1024,384]{3,2,1,0:T(8,128)} %get-tuple-element.162.dq.dk.skip_d.four, f32[2,8,1024]{2,1,0:T(8,128)S(1)} %shard_map.274.d0, ...), custom_call_target="tpu_custom_call" | custom-call | flops 230000000 | bytes 1000000 | tf_op jit(solution)/shard_map/pallas_call | solution.py:755
  155.2 24.5 %shard_map.276 = (bf16[2,256,384]{2,1,0:T(8,128)(2,1)}, bf16[2,256,384]{2,1,0:T(8,128)(2,1)}, bf16[2,256,384]{2,1,0:T(8,128)(2,1)}, bf16[2,256,384]{2,1,0:T(8,128)(2,1)}, f32[408,768]{1,0:T(8,128)}) custom-call(s32[10]{0:T(128)S(1)} %pad_add_fusion.sc, f32[2,8,1024]{2,1,0:T(8,128)S(1)} %shard_map.274.d0, f32[2,8,1024]{2,1,0:T(8,128)S(1)} %collective-permute-done.14.d1, ...), custom_call_target="tpu_custom_call" | custom-call | flops 1610000000 | bytes 1000000 | tf_op jit(solution)/shard_map/pallas_call | solution.py:755
  179.8 2.4 %collective-permute-done.19.rest_4_ = bf16[4,256,384]{2,1,0:T(8,128)(2,1)S(1)} collective-permute-done((bf16[4,256,384]{2,1,0:T(8,128)(2,1)S(1)}, bf16[4,256,384]{2,1,0:T(8,128)(2,1)S(1)}, u32[]{:S(2)}, u32[]{:S(2)}) %collective-permute-start.19) | collective-permute-done | bytes 786464 | tf_op jit(solution)/shard_map/ppermute | solution.py:801
  186.9 1.8 collective-permute-start.25
  188.8 2.8 %collective-permute-start.26 = (bf16[96,768]{1,0:T(8,128)(2,1)S(1)}, bf16[96,768]{1,0:T(8,128)(2,1)S(1)}, u32[]{:S(2)}, u32[]{:S(2)}) collective-permute-start(bf16[96,768]{1,0:T(8,128)(2,1)S(1)} %get-tuple-element.219), channel_id=1, source_target_pairs={{0,16},{8,24},{16,0},{24,8},{1,17},{9,25},{17,1},{25,9},{2,18},{10... | collective-permute-start | bytes 442376 | tf_op jit(solution)/shard_map/ppermute | solution.py:1049
  193.4 3.0 %collective-permute-done.25 = bf16[96,768]{1,0:T(8,128)(2,1)S(1)} collective-permute-done((bf16[96,768]{1,0:T(8,128)(2,1)S(1)}, bf16[96,768]{1,0:T(8,128)(2,1)S(1)}, u32[]{:S(2)}, u32[]{:S(2)}) %collective-permute-start.25) | collective-permute-done | bytes 147488 | tf_op jit(solution)/shard_map/ppermute | solution.py:1049
  197.9 4.8 %collective-permute-done.26 = bf16[96,768]{1,0:T(8,128)(2,1)S(1)} collective-permute-done((bf16[96,768]{1,0:T(8,128)(2,1)S(1)}, bf16[96,768]{1,0:T(8,128)(2,1)S(1)}, u32[]{:S(2)}, u32[]{:S(2)}) %collective-permute-start.26) | collective-permute-done | bytes 147488 | tf_op jit(solution)/shard_map/ppermute | solution.py:1049
  205.2 6.6 %collective-permute-done.22.rest_8_ = bf16[2,256,384]{2,1,0:T(8,128)(2,1)S(1)} collective-permute-done((bf16[2,256,384]{2,1,0:T(8,128)(2,1)S(1)}, bf16[2,256,384]{2,1,0:T(8,128)(2,1)S(1)}, u32[]{:S(2)}, u32[]{:S(2)}) %collective-permute-start.22) | collective-permute-done | bytes 393248 | tf_op jit(solution)/shard_map/ppermute | solution.py:801
  213.3 10.2 %shard_map.277 = (bf16[2,256,768]{2,1,0:T(8,128)(2,1)}, bf16[2,256,768]{2,1,0:T(8,128)(2,1)}) custom-call(s32[10]{0:T(128)S(1)} %pad_add_fusion.sc, f32[1,768]{1,0:T(1,128)S(1)} %reshape.223.gain, bf16[2,256,768]{2,1,0:T(8,128)(2,1)} %rest_0_.1, bf16[2,256,768]{2,1,0:T(8,128)(2,1)} %rest_1_.1, bf16[4,256,384]{2,1,0:T(8,128)(2,1)} %get-tuple-element.179.rest_2_, ...), custom_call_target="tpu_custom_call" | custom-call | flops 5750000128 | bytes 1000000 | tf_op jit(solution)/shard_map/pallas_call | solution.py:755
  223.6 3.5 %collective-permute-start.31 = (f32[24,768]{1,0:T(8,128)S(1)}, f32[24,768]{1,0:T(8,128)S(1)}, u32[]{:S(2)}, u32[]{:S(2)}) collective-permute-start(f32[24,768]{1,0:T(8,128)S(1)} %broadcast_select_fusion.t0), channel_id=1, source_target_pairs={{0,2},{1,3},{2,0},{3,1},{4,6},{5,7},{6,4},{7,5},{8,10},{9,11},{10,... | collective-permute-start | bytes 221192 | tf_op jit(solution)/shard_map/ppermute | solution.py:801
  229.4 2.9 %collective-permute-done.32.t3 = f32[24,768]{1,0:T(8,128)S(1)} collective-permute-done((f32[24,768]{1,0:T(8,128)S(1)}, f32[24,768]{1,0:T(8,128)S(1)}, u32[]{:S(2)}, u32[]{:S(2)}) %collective-permute-start.32) | collective-permute-done | bytes 73760 | tf_op jit(solution)/shard_map/ppermute | solution.py:801
  (161 shorter events, 56.8 us)
Async XLA Ops:
  0.7 20.8 %collective-permute-start = (bf16[2,256,768]{2,1,0:T(8,128)(2,1)}, bf16[2,256,768]{2,1,0:T(8,128)(2,1)S(1)}, u32[]{:S(2)}, u32[]{:S(2)}) collective-permute-start(bf16[2,256,768]{2,1,0:T(8,128)(2,1)} %rest_0_.1), channel_id=1, source_target_pairs={{0,1},{1,0},{2,3},{3,2},{4,5},{5,4},{6,7},{7,6},{8,9},{9,8},{10,11... | collective-permute-start | bytes 2359304 | tf_op jit(solution)/shard_map/ppermute | solution.py:801
  3.7 19.3 %collective-permute-start.1 = (bf16[2,256,768]{2,1,0:T(8,128)(2,1)}, bf16[2,256,768]{2,1,0:T(8,128)(2,1)}, u32[]{:S(2)}, u32[]{:S(2)}) collective-permute-start(bf16[2,256,768]{2,1,0:T(8,128)(2,1)} %rest_0_.1), channel_id=1, source_target_pairs={{0,2},{1,3},{2,0},{3,1},{4,6},{5,7},{6,4},{7,5},{8,10},{9,11},{10,... | collective-permute-start | bytes 2359304 | tf_op jit(solution)/shard_map/ppermute | solution.py:801
  23.0 9.7 %collective-permute-start.2 = (bf16[256,768]{1,0:T(8,128)(2,1)S(1)}, bf16[256,768]{1,0:T(8,128)(2,1)S(1)}, u32[]{:S(2)}, u32[]{:S(2)}) collective-permute-start(bf16[256,768]{1,0:T(8,128)(2,1)S(1)} %slice_bitcast_fusion.3), channel_id=1, source_target_pairs={{0,2},{1,3},{2,0},{3,1},{4,6},{5,7},{6,4},{7,5},{8,10},{9,11},{10,... | collective-permute-start | bytes 1179656 | tf_op jit(solution)/shard_map/ppermute | solution.py:801
  26.4 9.6 %collective-permute-start.3 = (bf16[256,768]{1,0:T(8,128)(2,1)}, bf16[256,768]{1,0:T(8,128)(2,1)S(1)}, u32[]{:S(2)}, u32[]{:S(2)}) collective-permute-start(bf16[256,768]{1,0:T(8,128)(2,1)} %slice_bitcast_fusion.2), channel_id=1, source_target_pairs={{0,1},{1,0},{2,3},{3,2},{4,5},{5,4},{6,7},{7,6},{8,9},{9,8},{10,11... | collective-permute-start | bytes 1179656 | tf_op jit(solution)/shard_map/ppermute | solution.py:801
  36.0 21.3 %collective-permute-start.5 = (bf16[2,256,768]{2,1,0:T(8,128)(2,1)}, bf16[2,256,768]{2,1,0:T(8,128)(2,1)S(1)}, u32[]{:S(2)}, u32[]{:S(2)}) collective-permute-start(bf16[2,256,768]{2,1,0:T(8,128)(2,1)} %rest_1_.1), channel_id=1, source_target_pairs={{0,1},{1,0},{2,3},{3,2},{4,5},{5,4},{6,7},{7,6},{8,9},{9,8},{10,11... | collective-permute-start | bytes 2359304 | tf_op jit(solution)/shard_map/ppermute | solution.py:801
  36.6 20.7 %collective-permute-start.6 = (bf16[2,256,768]{2,1,0:T(8,128)(2,1)}, bf16[2,256,768]{2,1,0:T(8,128)(2,1)S(1)}, u32[]{:S(2)}, u32[]{:S(2)}) collective-permute-start(bf16[2,256,768]{2,1,0:T(8,128)(2,1)} %rest_1_.1), channel_id=1, source_target_pairs={{0,2},{1,3},{2,0},{3,1},{4,6},{5,7},{6,4},{7,5},{8,10},{9,11},{10,... | collective-permute-start | bytes 2359304 | tf_op jit(solution)/shard_map/ppermute | solution.py:801
  65.3 9.7 %collective-permute-start.10 = (bf16[256,768]{1,0:T(8,128)(2,1)S(1)}, bf16[256,768]{1,0:T(8,128)(2,1)S(1)}, u32[]{:S(2)}, u32[]{:S(2)}) collective-permute-start(bf16[256,768]{1,0:T(8,128)(2,1)S(1)} %slice_bitcast_fusion.1), channel_id=1, source_target_pairs={{0,2},{1,3},{2,0},{3,1},{4,6},{5,7},{6,4},{7,5},{8,10},{9,11},{10,... | collective-permute-start | bytes 1179656 | tf_op jit(solution)/shard_map/ppermute | solution.py:801
  65.9 9.5 %collective-permute-start.11 = (bf16[256,768]{1,0:T(8,128)(2,1)S(1)}, bf16[256,768]{1,0:T(8,128)(2,1)S(1)}, u32[]{:S(2)}, u32[]{:S(2)}) collective-permute-start(bf16[256,768]{1,0:T(8,128)(2,1)S(1)} %slice_bitcast_fusion), channel_id=1, source_target_pairs={{0,1},{1,0},{2,3},{3,2},{4,5},{5,4},{6,7},{7,6},{8,9},{9,8},{10,11... | collective-permute-start | bytes 1179656 | tf_op jit(solution)/shard_map/ppermute | solution.py:801
  125.9 7.0 %collective-permute-start.13 = (f32[2,384,384]{2,1,0:T(8,128)}, f32[2,384,384]{2,1,0:T(8,128)S(1)}, u32[]{:S(2)}, u32[]{:S(2)}) collective-permute-start(f32[2,384,384]{2,1,0:T(8,128)} %get-tuple-element.159), channel_id=1, source_target_pairs={{4,0},{5,1},{6,2},{7,3},{12,8},{13,9},{14,10},{15,11},{20,16},{21,... | collective-permute-start | bytes 3538952 | tf_op jit(solution)/shard_map/ppermute | solution.py:953
  127.2 56.2 %all-to-all-start = ((bf16[8,96,768]{2,1,0:T(8,128)(2,1)}), bf16[8,96,768]{2,1,0:T(8,128)(2,1)}, u32[]{:S(2)}, u32[]{:S(2)}) async-start(bf16[8,96,768]{2,1,0:T(8,128)(2,1)} %get-tuple-element.188), calls=%async_computation | async-start | bytes 2359296 | tf_op jit(solution)/shard_map/all_to_all | solution.py:969
  146.0 33.8 %collective-permute-start.20 = (bf16[4,256,384]{2,1,0:T(8,128)(2,1)S(1)}, bf16[4,256,384]{2,1,0:T(8,128)(2,1)S(1)}, u32[]{:S(2)}, u32[]{:S(2)}) collective-permute-start(bf16[4,256,384]{2,1,0:T(8,128)(2,1)S(1)} %copy-done.22), channel_id=1, source_target_pairs={{0,3},{1,2},{2,1},{3,0},{4,7},{5,6},{6,5},{7,4},{8,11},{9,10},{10,... | collective-permute-start | bytes 2359304 | tf_op jit(solution)/shard_map/ppermute | solution.py:801
  147.6 34.5 %collective-permute-start.19 = (bf16[4,256,384]{2,1,0:T(8,128)(2,1)S(1)}, bf16[4,256,384]{2,1,0:T(8,128)(2,1)S(1)}, u32[]{:S(2)}, u32[]{:S(2)}) collective-permute-start(bf16[4,256,384]{2,1,0:T(8,128)(2,1)S(1)} %copy-done.21), channel_id=1, source_target_pairs={{0,2},{1,3},{2,0},{3,1},{4,6},{5,7},{6,4},{7,5},{8,10},{9,11},{10,... | collective-permute-start | bytes 2359304 | tf_op jit(solution)/shard_map/ppermute | solution.py:801
  149.2 33.0 %collective-permute-start.18 = (bf16[4,256,384]{2,1,0:T(8,128)(2,1)S(1)}, bf16[4,256,384]{2,1,0:T(8,128)(2,1)S(1)}, u32[]{:S(2)}, u32[]{:S(2)}) collective-permute-start(bf16[4,256,384]{2,1,0:T(8,128)(2,1)S(1)} %copy-done.20), channel_id=1, source_target_pairs={{0,1},{1,0},{2,3},{3,2},{4,5},{5,4},{6,7},{7,6},{8,9},{9,8},{10,11... | collective-permute-start | bytes 2359304 | tf_op jit(solution)/shard_map/ppermute | solution.py:801
  184.9 7.5 %collective-permute-start.29 = (f32[48,768]{1,0:T(8,128)S(1)}, f32[48,768]{1,0:T(8,128)S(1)}, u32[]{:S(2)}, u32[]{:S(2)}) collective-permute-start(f32[48,768]{1,0:T(8,128)S(1)} %get-tuple-element.221), channel_id=1, source_target_pairs={{4,0},{5,1},{6,2},{7,3},{12,8},{13,9},{14,10},{15,11},{20,16},{21,... | collective-permute-start | bytes 442376 | tf_op jit(solution)/shard_map/ppermute | solution.py:1061
  186.9 9.5 %collective-permute-start.25 = (bf16[96,768]{1,0:T(8,128)(2,1)S(1)}, bf16[96,768]{1,0:T(8,128)(2,1)S(1)}, u32[]{:S(2)}, u32[]{:S(2)}) collective-permute-start(bf16[96,768]{1,0:T(8,128)(2,1)S(1)} %get-tuple-element.217), channel_id=1, source_target_pairs={{0,8},{8,0},{16,24},{24,16},{1,9},{9,1},{17,25},{25,17},{2,10},{10... | collective-permute-start | bytes 442376 | tf_op jit(solution)/shard_map/ppermute | solution.py:1049
  188.8 14.0 %collective-permute-start.26 = (bf16[96,768]{1,0:T(8,128)(2,1)S(1)}, bf16[96,768]{1,0:T(8,128)(2,1)S(1)}, u32[]{:S(2)}, u32[]{:S(2)}) collective-permute-start(bf16[96,768]{1,0:T(8,128)(2,1)S(1)} %get-tuple-element.219), channel_id=1, source_target_pairs={{0,16},{8,24},{16,0},{24,8},{1,17},{9,25},{17,1},{25,9},{2,18},{10... | collective-permute-start | bytes 442376 | tf_op jit(solution)/shard_map/ppermute | solution.py:1049
  191.5 11.2 %collective-permute-start.27 = (bf16[96,768]{1,0:T(8,128)(2,1)S(1)}, bf16[96,768]{1,0:T(8,128)(2,1)S(1)}, u32[]{:S(2)}, u32[]{:S(2)}) collective-permute-start(bf16[96,768]{1,0:T(8,128)(2,1)S(1)} %get-tuple-element.218), channel_id=1, source_target_pairs={{0,24},{8,16},{16,8},{24,0},{1,25},{9,17},{17,9},{25,1},{2,26},{10... | collective-permute-start | bytes 442376 | tf_op jit(solution)/shard_map/ppermute | solution.py:1049
  191.5 13.6 %collective-permute-start.21 = (bf16[2,256,384]{2,1,0:T(8,128)(2,1)}, bf16[2,256,384]{2,1,0:T(8,128)(2,1)S(1)}, u32[]{:S(2)}, u32[]{:S(2)}) collective-permute-start(bf16[2,256,384]{2,1,0:T(8,128)(2,1)} %get-tuple-element.184), channel_id=1, source_target_pairs={{0,1},{1,0},{2,3},{3,2},{4,5},{5,4},{6,7},{7,6},{8,9},{9,8},{10,11... | collective-permute-start | bytes 1179656 | tf_op jit(solution)/shard_map/ppermute | solution.py:801
  192.4 19.4 %collective-permute-start.22 = (bf16[2,256,384]{2,1,0:T(8,128)(2,1)S(1)}, bf16[2,256,384]{2,1,0:T(8,128)(2,1)S(1)}, u32[]{:S(2)}, u32[]{:S(2)}) collective-permute-start(bf16[2,256,384]{2,1,0:T(8,128)(2,1)S(1)} %copy-done.24), channel_id=1, source_target_pairs={{0,2},{1,3},{2,0},{3,1},{4,6},{5,7},{6,4},{7,5},{8,10},{9,11},{10,... | collective-permute-start | bytes 1179656 | tf_op jit(solution)/shard_map/ppermute | solution.py:801
  196.5 15.3 %collective-permute-start.23 = (bf16[2,256,384]{2,1,0:T(8,128)(2,1)S(1)}, bf16[2,256,384]{2,1,0:T(8,128)(2,1)S(1)}, u32[]{:S(2)}, u32[]{:S(2)}) collective-permute-start(bf16[2,256,384]{2,1,0:T(8,128)(2,1)S(1)} %copy-done.23), channel_id=1, source_target_pairs={{0,3},{1,2},{2,1},{3,0},{4,7},{5,6},{6,5},{7,4},{8,11},{9,10},{10,... | collective-permute-start | bytes 1179656 | tf_op jit(solution)/shard_map/ppermute | solution.py:801
  204.3 24.2 %collective-permute-start.34 = (f32[48,768]{1,0:T(8,128)S(1)}, f32[48,768]{1,0:T(8,128)S(1)}, u32[]{:S(2)}, u32[]{:S(2)}) collective-permute-start(f32[48,768]{1,0:T(8,128)S(1)} %get-tuple-element.220), channel_id=1, source_target_pairs={{0,0},{1,8},{2,16},{3,24},{4,1},{5,9},{6,17},{7,25},{8,2},{9,10},{... | collective-permute-start | bytes 442376 | tf_op jit(solution)/shard_map/ppermute | solution.py:1068
  211.8 21.9 %collective-permute-start.33 = (f32[96,768]{1,0:T(8,128)S(1)}, f32[96,768]{1,0:T(8,128)S(1)}, u32[]{:S(2)}, u32[]{:S(2)}) collective-permute-start(f32[96,768]{1,0:T(8,128)S(1)} %get-tuple-element.200), channel_id=1, source_target_pairs={{0,16},{1,20},{2,24},{3,28},{4,0},{5,4},{6,8},{7,12},{8,17},{9,21}... | collective-permute-start | bytes 884744 | tf_op jit(solution)/shard_map/ppermute | solution.py:1071
  223.5 5.3 %collective-permute-start.30 = (f32[24,768]{1,0:T(8,128)S(1)}, f32[24,768]{1,0:T(8,128)S(1)}, u32[]{:S(2)}, u32[]{:S(2)}) collective-permute-start(f32[24,768]{1,0:T(8,128)S(1)} %broadcast_select_fusion.t0), channel_id=1, source_target_pairs={{0,1},{1,0},{2,3},{3,2},{4,5},{5,4},{6,7},{7,6},{8,9},{9,8},{10,11... | collective-permute-start | bytes 221192 | tf_op jit(solution)/shard_map/ppermute | solution.py:801
  223.6 5.9 %collective-permute-start.31 = (f32[24,768]{1,0:T(8,128)S(1)}, f32[24,768]{1,0:T(8,128)S(1)}, u32[]{:S(2)}, u32[]{:S(2)}) collective-permute-start(f32[24,768]{1,0:T(8,128)S(1)} %broadcast_select_fusion.t0), channel_id=1, source_target_pairs={{0,2},{1,3},{2,0},{3,1},{4,6},{5,7},{6,4},{7,5},{8,10},{9,11},{10,... | collective-permute-start | bytes 221192 | tf_op jit(solution)/shard_map/ppermute | solution.py:801
  (37 other events, 309.7 us)
